TPU v7x, 256 devices: a whole 4x4x8 slice. The times are simulated.
256 devices in a mesh: group: 16 (over x, z_hi, core), tp: 16 (over y, z_lo).
Axes of the slice: x: 4, y: 4, z: 8 (z_hi: 2, z_lo: 4; z = z_hi * 4 + z_lo), core: 2. Of those that a mesh axis runs over, the one named last changes fastest.
Arguments:
- states: bfloat16 [4, 1024, 5120], P(None, 'group'), may hold values from -6 to 6
- query_weight: bfloat16 [5120, 4096], P(None, 'tp'), may hold values from -0.078125 to 0.078125
- key_value_weight: bfloat16 [5120, 1024], P(None, 'tp'), may hold values from -0.078125 to 0.078125
- output_weight: bfloat16 [4096, 5120], P('tp'), may hold values from -0.09375 to 0.09375
- query_adapter_lower: bfloat16 [5120, 64], P(('group', 'tp')), may hold values from -0.078125 to 0.078125
- query_adapter_upper: bfloat16 [64, 4096], P('group', 'tp'), may hold values from -0.75 to 0.75
- output_adapter_lower: bfloat16 [64, 4096], P('group', 'tp'), may hold values from -0.09375 to 0.09375
- output_adapter_upper: bfloat16 [5120, 64], P(('group', 'tp')), may hold values from -0.75 to 0.75
- cached_key_rows: bfloat16 [1024, 4, 64, 128], P('group'), may hold values from -160 to 160
- cached_value_rows: bfloat16 [1024, 4, 64, 128], P('group'), may hold values from -6 to 6
- cached_length: int32 [1024], P('group'), may hold values from 1 to 64, as said below
Outputs:
- attn_out: bfloat16 [4, 1024, 5120], P(None, 'group', 'tp')
Inputs may be any that keep to these rules, and one draw needn't show every extreme that they name: `cached_length`: some rollout has exactly 64 cached positions.
All inputs are finite; a program needn't handle non-finite values.
Results may differ from a plain program's by a relative error of at most 0.024.
The roundings to bfloat16 on the way count: a program that leaves them out, or rounds other values in their place, can miss the bound.
Values may be sent and summed in bfloat16 or wider, within the bound.
No kernel may reach another device: no remote copies, remote signals or barrier semaphores. Data moves between devices by JAX's collectives and lax.ppermute only.
A program may use at most 128 MiB of HBM per device.

v0:
```python
import jax
import jax.numpy as jnp
from jax import lax
from jax.sharding import PartitionSpec as P

QH = 32
KVH = 4
HD = 128


adapter_scale = 2.0


def local(
    states,
    query_weight,
    key_value_weight,
    output_weight,
    query_adapter_lower,
    query_adapter_upper,
    output_adapter_lower,
    output_adapter_upper,
    cached_key_rows,
    cached_value_rows,
    cached_length,
):
    query_lower_factor, o_up = (
        lax.all_gather(query_adapter_lower, ("group", "tp"), axis=0, tiled=True),
        lax.all_gather(output_adapter_upper, ("group", "tp"), axis=0, tiled=True),
    )
    query_upper_factor, o_down = (
        lax.all_gather(query_adapter_upper, "group", axis=0, tiled=True),
        lax.all_gather(output_adapter_lower, "group", axis=0, tiled=True),
    )
    combined_query_weight = (
        query_weight.astype(jnp.float32)
        + adapter_scale
        * jnp.dot(query_lower_factor, query_upper_factor, preferred_element_type=jnp.float32)
    ).astype(jnp.bfloat16)
    steps, rows, width = states.shape
    flat = states.reshape(steps * rows, width).astype(jnp.float32)
    normed = (flat * lax.rsqrt(jnp.mean(flat * flat, axis=1, keepdims=True) + 1e-06)).astype(
        jnp.bfloat16
    )
    kv_part = (
        jnp.dot(normed, key_value_weight, preferred_element_type=jnp.float32)
        .astype(jnp.bfloat16)
        .reshape(steps, rows, -1)
    )
    kv_full = lax.all_gather(kv_part, "tp", axis=2, tiled=True)
    heads_dev = combined_query_weight.shape[1] // HD
    queries = (
        jnp.dot(normed, combined_query_weight, preferred_element_type=jnp.float32)
        .astype(jnp.bfloat16)
        .reshape(steps, rows, heads_dev, HD)
    )
    kv_head = lax.axis_index("tp") * heads_dev // (QH // KVH)
    keys_here = lax.dynamic_slice_in_dim(cached_key_rows, kv_head, 1, 1)[:, 0]
    vals_here = lax.dynamic_slice_in_dim(cached_value_rows, kv_head, 1, 1)[:, 0]
    new_keys = lax.dynamic_slice_in_dim(kv_full, kv_head * HD, HD, 2)
    new_vals = lax.dynamic_slice_in_dim(kv_full, KVH * HD + kv_head * HD, HD, 2)
    cached = keys_here.shape[1]
    positions = jnp.arange(cached, dtype=jnp.int32)
    mask_cache = (positions[None, :] < cached_length[:, None])[:, None, :]
    factor = 1.0 / HD**0.5
    contexts = []
    for step in range(steps):
        query_now = queries[step]
        score_cache = (
            jnp.einsum("rhd,rpd->rhp", query_now, keys_here, preferred_element_type=jnp.float32)
            * factor
        )
        score_cache = jnp.where(mask_cache, score_cache, -1e30)
        score_new = (
            jnp.einsum(
                "rhd,jrd->rhj", query_now, new_keys[: step + 1], preferred_element_type=jnp.float32
            )
            * factor
        )
        scores = jnp.concatenate([score_cache, score_new], axis=-1)
        top = jnp.max(scores, axis=-1, keepdims=True)
        expo = jnp.exp(scores - top)
        probs = (expo / jnp.sum(expo, axis=-1, keepdims=True)).astype(jnp.bfloat16)
        context = jnp.einsum(
            "rhp,rpd->rhd", probs[..., :cached], vals_here, preferred_element_type=jnp.float32
        )
        context = context + jnp.einsum(
            "rhj,jrd->rhd",
            probs[..., cached:],
            new_vals[: step + 1],
            preferred_element_type=jnp.float32,
        )
        contexts.append(context.astype(jnp.bfloat16).reshape(rows, heads_dev * HD))
    output_update = lax.dot_general(
        o_down, o_up, (((0,), (1,)), ((), ())), preferred_element_type=jnp.float32
    )
    combined_output_weight = (
        output_weight.astype(jnp.float32) + adapter_scale * output_update
    ).astype(jnp.bfloat16)
    terms = [
        jnp.dot(ctx, combined_output_weight, preferred_element_type=jnp.float32) for ctx in contexts
    ]
    outputs = []
    for step in range(steps):
        outputs.append(
            lax.psum_scatter(
                terms[step].astype(jnp.bfloat16), "tp", scatter_dimension=1, tiled=True
            )
        )
    return jnp.stack(outputs, axis=0)


def solution(mesh):
    in_specs = (
        P(None, "group", None),
        P(None, "tp"),
        P(None, "tp"),
        P("tp", None),
        P(("group", "tp"), None),
        P("group", "tp"),
        P("group", "tp"),
        P(("group", "tp"), None),
        P("group", None, None, None),
        P("group", None, None, None),
        P("group"),
    )
    out_specs = P(None, "group", "tp")
    return jax.shard_map(local, mesh=mesh, in_specs=in_specs, out_specs=out_specs, check_vma=False)
```

profile of v0, /device:TPU:32, one launch (start us, length us, event | category | flops | bytes accessed | tf_op | source)
XLA Modules:
  0.0 1798.1 jit_solution(9969747720216330690)
XLA Ops:
  6.5 2.5 multiply_reduce_fusion
  9.1 2.2 fusion.4
  11.4 671.9 %all-gather = bf16[256,20,64]{2,1,0:T(8,128)(2,1)} all-gather(bf16[1,20,64]{2,1,0:T(8,128)(2,1)S(1)} %bitcast.116), channel_id=1, replica_groups=mesh['group'=16,'tp'=16] {'group','tp'}, dimensions={0}, use_global_device_ids=true | all-gather | bytes 657920 | tf_op jit(solution)/shard_map/all_gather | solution.py:28
  683.3 3.5 reshape.113
  686.8 23.9 %all-gather.1 = bf16[16,4,256]{2,1,0:T(4,128)(2,1)S(1)} all-gather(bf16[1,4,256]{2,1,0:T(4,128)(2,1)S(1)} %bitcast.118), channel_id=1, replica_groups=mesh['group'=16,'tp'=16] {'group'}, dimensions={0}, use_global_device_ids=true | all-gather | bytes 34816 | tf_op jit(solution)/shard_map/all_gather | solution.py:32
  710.7 3.8 fusion.6
  714.6 1.9 fusion.24
  717.2 1.9 fusion.22
  719.8 1.9 fusion.20
  722.5 1.9 fusion.18
  725.1 1.8 fusion.71
  727.6 1.5 convolution_convert_fusion.4
  730.0 53.0 %all_gather.17 = bf16[4,64,1024]{1,0,2:T(4,128)(2,1)S(1)} all-gather(bf16[4,64,64]{1,0,2:T(4,128)(2,1)S(1)} %reshape.101), channel_id=1, replica_groups=mesh['group'=16,'tp'=16] {'tp'}, dimensions={2}, use_global_device_ids=true | all-gather | bytes 557056 | tf_op jit(solution)/shard_map/all_gather | solution.py:50
  787.5 628.3 %all-gather.3 = bf16[256,20,64]{2,1,0:T(8,128)(2,1)S(1)} all-gather(bf16[1,20,64]{2,1,0:T(8,128)(2,1)S(1)} %bitcast.117), channel_id=1, replica_groups=mesh['group'=16,'tp'=16] {'group','tp'}, dimensions={0}, use_global_device_ids=true | all-gather | bytes 657920 | tf_op jit(solution)/shard_map/all_gather | solution.py:29
  1417.2 23.9 %all-gather.2 = bf16[16,4,256]{2,1,0:T(4,128)(2,1)S(1)} all-gather(bf16[1,4,256]{2,1,0:T(4,128)(2,1)S(1)} %bitcast.119), channel_id=1, replica_groups=mesh['group'=16,'tp'=16] {'group'}, dimensions={0}, use_global_device_ids=true | all-gather | bytes 34816 | tf_op jit(solution)/shard_map/all_gather | solution.py:33
  1441.7 3.0 fusion.3
  1444.8 1.6 fusion.7
  1446.4 1.4 convolution_convert_fusion.3
  1447.9 2.3 copy.50
  1450.5 1.7 fusion.50
  1454.1 1.6 fusion.15
  1458.1 2.3 copy.52
  1460.5 1.7 fusion.39
  1464.2 1.6 fusion.13
  1468.2 2.3 copy.54
  1472.9 1.6 fusion.11
  1474.7 1.4 convolution_convert_fusion
  1476.1 2.3 copy.56
  1478.5 52.3 %reduce-scatter.13.cloned.1.call-done = bf16[320,64]{1,0:T(8,128)(2,1)} async-done(((bf16[5120,64]{1,0:T(8,128)(2,1)}), bf16[320,64]{1,0:T(8,128)(2,1)}) %reduce-scatter.13.cloned.1.call-update) | async-done | bytes 40976
  1531.8 85.5 %reduce-scatter.15.cloned.1.call-done = bf16[320,64]{1,0:T(8,128)(2,1)} async-done(((bf16[5120,64]{1,0:T(8,128)(2,1)}), bf16[320,64]{1,0:T(8,128)(2,1)}) %reduce-scatter.15.cloned.1.call-update) | async-done | bytes 40976
  1618.3 85.4 %reduce-scatter.17.cloned.1.call-done = bf16[320,64]{1,0:T(8,128)(2,1)} async-done(((bf16[5120,64]{1,0:T(8,128)(2,1)}), bf16[320,64]{1,0:T(8,128)(2,1)}) %reduce-scatter.17.cloned.1.call-update) | async-done | bytes 40976
  1704.7 85.2 %reduce-scatter.19.cloned.1.call-done = bf16[320,64]{1,0:T(8,128)(2,1)} async-done(((bf16[5120,64]{1,0:T(8,128)(2,1)}), bf16[320,64]{1,0:T(8,128)(2,1)}) %reduce-scatter.19.cloned.1.call-update) | async-done | bytes 40976
  (117 shorter events, 27.4 us)
Async XLA Ops:
  6.5 721.0 %copy-start = (bf16[5120,64]{0,1:T(8,128)(2,1)S(1)}, bf16[5120,64]{0,1:T(8,128)(2,1)}, u32[]{:S(2)}) copy-start(bf16[5120,64]{0,1:T(8,128)(2,1)} %param.13) | copy-start | bytes 1966084
  6.5 2.6 copy-start.1
  6.5 1524.3 %reduce-scatter.13.cloned.1.call-start = ((), (), s32[]{:S(2)}) async-start(), calls=%async_computation.4 | async-start | bytes 1392640
  9.1 2.2 copy-start.14
  11.3 675.4 %copy-start.17 = (bf16[4,256]{1,0:T(4,128)(2,1)S(1)}, bf16[4,256]{1,0:T(4,128)(2,1)}, u32[]{:S(2)}) copy-start(bf16[4,256]{1,0:T(4,128)(2,1)} %param.16) | copy-start | bytes 6148
  11.3 699.3 %copy-start.2 = (bf16[256,5120]{1,0:T(8,128)(2,1)S(1)}, bf16[256,5120]{1,0:T(8,128)(2,1)}, u32[]{:S(2)}) copy-start(bf16[256,5120]{1,0:T(8,128)(2,1)} %fusion.4) | copy-start | bytes 7864324
  714.5 2.6 copy-start.8
  714.5 10.5 copy-start.19
  717.2 2.6 copy-start.7
  719.8 2.6 copy-start.5
  722.5 2.6 copy-start.3
  727.6 60.0 %copy-start.15 = (bf16[20,64]{1,0:T(8,128)(2,1)S(1)}, bf16[20,64]{1,0:T(8,128)(2,1)}, u32[]{:S(2)}) copy-start(bf16[20,64]{1,0:T(8,128)(2,1)} %param.18) | copy-start | bytes 7684
  783.2 1.0 copy-start.12
  784.2 633.0 %copy-start.18 = (bf16[4,256]{1,0:T(4,128)(2,1)S(1)}, bf16[4,256]{1,0:T(4,128)(2,1)}, u32[]{:S(2)}) copy-start(bf16[4,256]{1,0:T(4,128)(2,1)} %param.17) | copy-start | bytes 6148
  1441.7 3.1 copy-start.9
  1441.7 3.1 copy-start.10
  1441.7 3.1 copy-start.11
  1447.9 5.2 copy-start.16
  1450.2 167.1 %reduce-scatter.15.cloned.1.call-start = ((), (), s32[]{:S(2)}) async-start(), calls=%async_computation.5 | async-start | bytes 1392640
  1456.7 3.8 copy-start.6
  1460.5 243.2 %reduce-scatter.17.cloned.1.call-start = ((), (), s32[]{:S(2)}) async-start(), calls=%async_computation.6 | async-start | bytes 1392640
  1466.8 3.8 copy-start.4
  1466.8 3.8 copy-start.13
  1470.6 319.3 %reduce-scatter.19.cloned.1.call-start = ((), (), s32[]{:S(2)}) async-start(), calls=%async_computation.7 | async-start | bytes 1392640
Sparse Core Ops, SparseCore 0:
  1450.3 80.4 reduce-scatter.12
  1533.3 83.9 reduce-scatter.14
  1619.8 83.7 reduce-scatter.16
  1706.1 83.7 reduce-scatter.18
where the time goes:
time: 1800 us
  blocking collectives  1400 us (78%)
  waiting for transfers between devices  308 us (17%)
  matrix products  35.4 us (2%)
  local copies, waits for them, and re-layouts  30.1 us (2%)
    all_gather x1, blocking collectives, local(): lax.all_gather(query_adapter_lower, ('group', 'tp'), axis=0, tiled=True)  672 us
    all_gather x1, blocking collectives, local(): lax.all_gather(output_adapter_upper, ('group', 'tp'), axis=0, tiled=True)  628 us
    unnamed x8, waiting for transfers between devices  308 us
    all_gather x1, blocking collectives, local(): kv_full = lax.all_gather(kv_part, 'tp', axis=2, tiled=True)  53 us
  transfers between devices with their start and end apart: 4, of which 4 were waited for; matrix products, arithmetic and copies ran while one was open for 2% of the time, Pallas kernels for 0%

commit v1 on v0

v1 whole, which is shorter than its diff:
```python
import jax
import jax.numpy as jnp
import numpy as np
from jax import lax
from jax.experimental import pallas as pl
from jax.experimental.pallas import tpu as pltpu
from jax.sharding import Mesh
from jax.sharding import PartitionSpec as P

HD = 128
STEPS = 4
ROWS = 256
WIDTH = 5120
NX, NZH, NC, NY, NZ = 4, 2, 2, 4, 4
GROUP = ("x", "zh", "c")
TP = ("y", "z")
BF = jnp.bfloat16
F32 = jnp.float32
VLIMIT = 56 * 1024 * 1024
MSG = 48
XROWS = 720

SMEM = pl.BlockSpec(memory_space=pltpu.SMEM)


def params():
    return pltpu.CompilerParams(vmem_limit_bytes=VLIMIT)


def mm(a, b):
    return jnp.dot(a, b, preferred_element_type=F32)


def mm_t(a, b):
    return lax.dot_general(a, b, (((1,), (1,)), ((), ())), preferred_element_type=F32)


def norm_kernel(states, wkv_t, blocks, kv_t, flat):
    def rows(i, carry):
        r = pl.multiple_of(i * 32, 32)
        x = states[pl.ds(r, 32), :].astype(F32)
        scale = lax.rsqrt(jnp.mean(x * x, axis=1, keepdims=True) + 1e-06)
        normed = (x * scale).astype(BF)
        flat[pl.ds(r, 32), :] = normed
        for xc in range(8):
            g = (xc // 2) * 4 + xc % 2
            blocks[xc, pl.ds(r, 32), :] = jnp.concatenate(
                [normed[:, g * 320 : g * 320 + 320], normed[:, g * 320 + 640 : g * 320 + 960]], axis=1
            )
        return carry

    lax.fori_loop(0, ROWS // 32, rows, 0)
    kv_t[...] = mm_t(flat[...], wkv_t[...]).T.astype(BF)


def sort_kernel(ids, got, out):
    i = lax.broadcasted_iota(jnp.int32, (80, 4 * MSG), 0)
    j = lax.broadcasted_iota(jnp.int32, (80, 4 * MSG), 1)
    hit = i < 0
    for p in range(4):
        hit = hit | ((j - MSG * p == i - 20 * p) & (i >= 20 * p) & (i < 20 * p + 20))
    pick = jnp.where(hit, 1.0, 0.0).astype(BF)
    for q in range(8):
        out[80 * q : 80 * q + 80, :] = mm(pick, got[4 * q : 4 * q + 4].reshape(4 * MSG, 128)).astype(BF)
    y, z = ids[3], ids[4]
    own = [got[zh * 16 + y * NZ + z, 32:48, :].astype(F32)[:8] for zh in range(2)]
    out[640:656, :] = jnp.concatenate(own, axis=0).astype(BF)
    for yy in range(NY):
        part = [got[zh * 16 + yy * NZ + z, 32:48, :].astype(F32)[8:] for zh in range(2)]
        out[656 + 16 * yy : 672 + 16 * yy, :] = jnp.concatenate(part, axis=0).astype(BF)


def rank_order(ids, half, first):
    r = lax.broadcasted_iota(jnp.int32, (128, 128), 0)
    j = lax.broadcasted_iota(jnp.int32, (128, 128), 1)
    x, c = ids[0], ids[2]
    k, o = (j >> 5) & 3, (j >> 4) & 1
    zh, h, i = (j >> 3) & 1, (j >> 2) & 1, j & 3
    xs = (x - k + 4) & 3
    rank = (xs * 4 + zh * 2 + (c + o - 2 * c * o)) * 4 + i
    return jnp.where((h == half) & (r == rank + first), 1.0, 0.0).astype(BF)


def attend_kernel(ids, head, *refs):
    blocks = refs[:8]
    wq, normed, kc, vc, kv0, kv1, kv2, kv3, lens, ctx, kv, qs, cs = refs[8:]
    x, c, z = ids[0], ids[2], ids[4]
    stack = jnp.concatenate([b[640:656, :] for b in blocks], axis=0)
    upper = jnp.concatenate(
        [2.0 * mm(rank_order(ids, h, 0), stack) for h in range(2)], axis=1
    ).astype(BF)
    total = jnp.zeros((ROWS, 256), F32)
    for k in range(4):
        for o in range(2):
            xs = (x - k + 4) & 3
            cs_ = c + o - 2 * c * o
            rank = mm(blocks[2 * k + o][0:640, :], upper)
            off = pl.multiple_of((xs * 4 + cs_) * 320, 320)
            base = jnp.concatenate([wq[pl.ds(off, 320), :], wq[pl.ds(off + 640, 320), :]], axis=0)
            merged = (base.astype(F32) + rank).astype(BF)
            total = total + mm(normed[xs * 2 + cs_], merged)
    qs[...] = total.astype(BF).astype(F32)
    for k, ref in enumerate((kv0, kv1, kv2, kv3)):
        kv[(z - k + 4) & 3] = ref[...]
    key_t = kv[0:2].reshape(128, 256)
    val = kv[2:4].reshape(128, 256).astype(F32).T.astype(BF)
    factor = 1.0 / HD**0.5
    c8 = lax.broadcasted_iota(jnp.int32, (8, 512), 1)
    r8 = lax.broadcasted_iota(jnp.int32, (8, 512), 0)
    own_cached = (c8 >> 6) == r8
    pos = c8 & 63
    cn = lax.broadcasted_iota(jnp.int32, (64, 256), 1)
    rn = lax.broadcasted_iota(jnp.int32, (64, 256), 0)
    seen = (cn >> 6) <= (rn >> 4)

    def batch(b, carry):
        r = pl.multiple_of(b * 8, 8)
        q = jnp.concatenate(
            [qs[pl.ds(s * 64 + r, 8), h * 128 : h * 128 + 128] for s in range(4) for h in range(2)], axis=0
        ).astype(BF)
        keys = kc[pl.ds(r, 8), 0].reshape(512, 128)
        vals = vc[pl.ds(r, 8), 0].reshape(512, 128)
        ok = own_cached & (pos < lens[pl.ds(r, 8), :])
        okc = jnp.concatenate([jnp.where(ok, 0.0, -1e30)] * 8, axis=0)
        okn = seen & ((cn & 63) == (rn & 7) + r)
        sc = jnp.where(okc == 0.0, mm_t(q, keys) * factor, -1e30)
        sn = jnp.where(okn, mm(q, key_t) * factor, -1e30)
        top = jnp.maximum(jnp.max(sc, axis=1, keepdims=True), jnp.max(sn, axis=1, keepdims=True))
        ec, en = jnp.exp(sc - top), jnp.exp(sn - top)
        total = jnp.sum(ec, axis=1, keepdims=True) + jnp.sum(en, axis=1, keepdims=True)
        pc, pn = (ec / total).astype(BF), (en / total).astype(BF)
        out = mm(pc, vals) + mm(pn, val)
        for s in range(4):
            for h in range(2):
                n = (s * 2 + h) * 8
                cs[pl.ds(s * 64 + r, 8), h * 128 : h * 128 + 128] = out[n : n + 8]
        return carry

    lax.fori_loop(0, 8, batch, 0)
    ctx[...] = cs[...].astype(BF)


def merge_o_kernel(ids, *refs):
    blocks = refs[:8]
    weights = refs[8:12]
    out, hold = refs[12:]
    x, c, y = ids[0], ids[2], ids[3]
    ks = (x - y + 4) & 3
    for k in range(4):
        for o in range(2):

            @pl.when(ks == k)
            def _():
                hold[o] = blocks[2 * k + o][0:640, :]

    order = [rank_order(ids, h, 64) for h in range(2)]
    for k in range(4):
        at = pl.multiple_of(656 + 16 * ((y - k + 4) & 3), 16)
        stack = jnp.concatenate([b[pl.ds(at, 16), :] for b in blocks], axis=0)
        lower = jnp.concatenate([2.0 * mm(order[h], stack) for h in range(2)], axis=1)
        lower_t = lower.T.astype(BF)
        for zz in range(4):
            zh, cc = zz // 2, zz % 2
            o = c + cc - 2 * c * cc
            u = hold[o, zh * 320 : zh * 320 + 320, :]
            w = weights[k][:, zz * 320 : zz * 320 + 320].astype(F32)
            out[k, zz] = (w + mm_t(lower_t, u)).astype(BF)


def project_kernel(c0, c1, c2, c3, merged, out):
    for zz in range(4):
        total = mm(c0[...], merged[0, zz])
        for k, ref in ((1, c1), (2, c2), (3, c3)):
            total = total + mm(ref[...], merged[k, zz])
        out[zz] = total.astype(BF)


def sum_kernel(parts, out):
    total = parts[0].astype(F32)
    for k in range(1, 4):
        total = total + parts[k].astype(F32)
    out[...] = total.astype(BF).reshape(out.shape)


def shift(axis, size, by):
    return [(i, (i + by) % size) for i in range(size)]


def kv_pairs(k):
    pairs = []
    for s in range(16):
        a, e, b = s // 4, (s % 4) // 2, s % 2
        pairs.append((s, (2 * (a % 2) + e) * 4 + ((a // 2) * 2 + b + k) % 4))
    return pairs


def local(states, wq, wkv, wo, qa_low, qa_up, oa_low, oa_up, kcache, vcache, lens):
    x, zh, c, y, z = (lax.axis_index(a) for a in ("x", "zh", "c", "y", "z"))
    ids = jnp.stack([x, zh, c, y, z]).astype(jnp.int32)

    def halves(a):
        return jnp.concatenate([a[:, :128], a[:, 128:]], axis=0)

    def block(target):
        return lax.dynamic_slice_in_dim(wo, target * 1280, 1280, 1)

    weights = [block(y)]
    for s in (1, 2, 3):
        weights.append(lax.ppermute(block((y + s) % 4), "y", shift("y", 4, s)))

    message = jnp.concatenate(
        [
            jnp.concatenate([qa_low, oa_up], axis=1),
            jnp.zeros((12, 128), BF),
            halves(qa_up),
            halves(oa_low),
        ],
        axis=0,
    )
    got = lax.all_to_all(
        jnp.broadcast_to(message[None], (32, MSG, 128)), ("zh", "y", "z"), 0, 0, tiled=True
    )
    mine = pl.pallas_call(
        sort_kernel,
        out_shape=jax.ShapeDtypeStruct((XROWS, 128), BF),
        in_specs=[SMEM, pl.BlockSpec(memory_space=pltpu.VMEM)],
        compiler_params=params(),
        name="sort_rows",
    )(ids, got)
    blocks = []
    for s in range(4):
        part = mine if s == 0 else lax.ppermute(mine, "x", shift("x", 4, s))
        blocks += [part, lax.ppermute(part, "c", [(0, 1), (1, 0)])]

    normed, kv_t = pl.pallas_call(
        norm_kernel,
        out_shape=(
            jax.ShapeDtypeStruct((8, ROWS, 640), BF),
            jax.ShapeDtypeStruct((64, ROWS), BF),
        ),
        scratch_shapes=[pltpu.VMEM((ROWS, WIDTH), BF)],
        compiler_params=params(),
        cost_estimate=pl.CostEstimate(flops=170_000_000, bytes_accessed=8_000_000, transcendentals=0),
        name="norm_kv",
    )(states.reshape(ROWS, WIDTH), wkv.T)
    new_kv = [lax.ppermute(kv_t, TP, kv_pairs(k)) for k in range(4)]

    vmem = pl.BlockSpec(memory_space=pltpu.VMEM)
    one = pl.BlockSpec((64, 1, 64, 128), lambda i, ids, head: (0, head[0], 0, 0))

    def whole(shape):
        return pl.BlockSpec(shape, lambda i, ids, head: (0,) * len(shape))

    ctx = pl.pallas_call(
        attend_kernel,
        out_shape=jax.ShapeDtypeStruct((ROWS, 256), BF),
        grid_spec=pltpu.PrefetchScalarGridSpec(
            num_scalar_prefetch=2,
            grid=(1,),
            in_specs=[whole((XROWS, 128))] * 8
            + [whole((WIDTH, 256)), whole((8, ROWS, 640)), one, one]
            + [whole((64, 256))] * 4
            + [whole((64, 1))],
            out_specs=whole((ROWS, 256)),
            scratch_shapes=[
                pltpu.VMEM((4, 64, 256), BF),
                pltpu.VMEM((ROWS, 256), F32),
                pltpu.VMEM((ROWS, 256), F32),
            ],
        ),
        compiler_params=params(),
        cost_estimate=pl.CostEstimate(flops=1_000_000_000, bytes_accessed=10_000_000, transcendentals=400_000),
        name="attend",
    )(ids, y.reshape(1).astype(jnp.int32), *blocks, wq, normed, kcache, vcache, *new_kv, lens.reshape(64, 1))

    others = [lax.ppermute(ctx, "y", shift("y", 4, s)) for s in (1, 2, 3)]
    merged = pl.pallas_call(
        merge_o_kernel,
        out_shape=jax.ShapeDtypeStruct((4, 4, 256, 320), BF),
        in_specs=[SMEM] + [vmem] * 12,
        scratch_shapes=[pltpu.VMEM((2, 640, 128), BF)],
        compiler_params=params(),
        cost_estimate=pl.CostEstimate(flops=340_000_000, bytes_accessed=8_000_000, transcendentals=0),
        name="merge_o",
    )(ids, *blocks, *weights)
    parts = pl.pallas_call(
        project_kernel,
        out_shape=jax.ShapeDtypeStruct((4, ROWS, 320), BF),
        compiler_params=params(),
        cost_estimate=pl.CostEstimate(flops=680_000_000, bytes_accessed=4_000_000, transcendentals=0),
        name="project",
    )(ctx, *others, merged)
    parts = lax.all_to_all(parts, "z", 0, 0, tiled=True)
    return pl.pallas_call(
        sum_kernel,
        out_shape=jax.ShapeDtypeStruct((4, 64, 320), BF),
        compiler_params=params(),
        name="sum_parts",
    )(parts)


def solution(mesh):
    fine = Mesh(np.asarray(mesh.devices).reshape(NX, NZH, NC, NY, NZ), GROUP + TP)
    every = GROUP + TP
    in_specs = (
        P(None, GROUP, None),
        P(None, TP),
        P(None, TP),
        P(TP, None),
        P(every, None),
        P(GROUP, TP),
        P(GROUP, TP),
        P(every, None),
        P(GROUP, None, None, None),
        P(GROUP, None, None, None),
        P(GROUP),
    )
    out_specs = P(None, GROUP, TP)
    return jax.shard_map(local, mesh=fine, in_specs=in_specs, out_specs=out_specs, check_vma=False)
```

time: 1800 us -> 129 us (0.07)
  blocking collectives: 1400 us -> 18.2 us
  waiting for transfers between devices: 308 us -> 24.9 us
  starting transfers between devices: 0.31 us -> 43.1 us
  matrix products: 35.4 us -> 0 us
  Pallas kernels: 0 us -> 31.7 us
  local copies, waits for them, and re-layouts: 30.1 us -> 9.88 us
    all_gather x5 -> x0, blocking collectives: 1400 us -> none  [the longest x1 672 us: local(): lax.all_gather(query_adapter_lower, ('group', 'tp'), axis=0, tiled=True)]
    unnamed x8 -> x0, waiting for transfers between devices: 308 us -> none
    dot_general x22 -> x0, matrix products: 35.4 us -> none  [the longest x4 7.48 us: local(): jnp.einsum('rhd,rpd->rhp', query_now, keys_here, preferred_element_type=j...]
    pallas_call x0 -> x6, Pallas kernels: none -> 31.7 us  [the longest x1 11.4 us: local(): pl.pallas_call(attend_kernel, out_shape=jax.ShapeDtypeStruct((ROWS, 256),...]
    ppermute x0 -> x17, starting transfers between devices: none -> 31.7 us  [the longest x3 22.2 us: local(): weights.append(lax.ppermute(block((y + s) % 4), 'y', shift('y', 4, s)))]
    all_to_all x0 -> x1, blocking collectives: none -> 18.2 us  [local(): parts = lax.all_to_all(parts, 'z', 0, 0, tiled=True)]
  transfers between devices with their start and end apart: 4 -> 18, of which waited for: 4 -> 8; matrix products, arithmetic and copies ran while one was open for 2% -> 2% of each run, Pallas kernels for 0% -> 20%
where the time goes in v1:
time: 129 us
  starting transfers between devices  43.1 us (33%)
  Pallas kernels  31.7 us (25%)
  waiting for transfers between devices  24.9 us (19%)
  blocking collectives  18.2 us (14%)
  local copies, waits for them, and re-layouts  9.88 us (8%)
    ppermute x3, starting transfers between devices, local(): weights.append(lax.ppermute(block((y + s) % 4), 'y', shift('y', 4, s)))  22.2 us
    all_to_all x1, blocking collectives, local(): parts = lax.all_to_all(parts, 'z', 0, 0, tiled=True)  18.2 us
    pallas_call x1, Pallas kernels, local(): pl.pallas_call(attend_kernel, out_shape=jax.ShapeDtypeStruct((ROWS, 256),...  11.4 us
    all_to_all x1, starting transfers between devices, local(): lax.all_to_all(jnp.broadcast_to(message[None], (32, MSG, 128)), ('zh', 'y...  11.4 us
    ppermute x3, waiting for transfers between devices, local(): weights.append(lax.ppermute(block((y + s) % 4), 'y', shift('y', 4, s)))  8.88 us
    all_to_all x1, waiting for transfers between devices, local(): lax.all_to_all(jnp.broadcast_to(message[None], (32, MSG, 128)), ('zh', 'y...  8.04 us
    pallas_call x1, Pallas kernels, local(): pl.pallas_call(merge_o_kernel, out_shape=jax.ShapeDtypeStruct((4, 4, 256,...  6.56 us
    ppermute x4, waiting for transfers between devices, local(): new_kv = [lax.ppermute(kv_t, TP, kv_pairs(k)) for k in range(4)]  6.46 us
  transfers between devices with their start and end apart: 18, of which 8 were waited for; matrix products, arithmetic and copies ran while one was open for 2% of the time, Pallas kernels for 20%

profile of v1, /device:TPU:32, one launch (start us, length us, event | category | flops | bytes accessed | tf_op | source)
XLA Modules:
  0.0 128.7 jit_solution(6416725768653088254)
XLA Ops:
  0.0 0.7 fusion
  0.7 0.8 pad_maximum_fusion
  1.7 0.8 broadcast_in_dim.10
  2.5 11.4 %all-to-all-start = ((bf16[32,48,128]{2,1,0:T(8,128)(2,1)}), bf16[32,48,128]{2,1,0:T(8,128)(2,1)S(1)}, u32[]{:S(2)}, u32[]{:S(2)}) async-start(bf16[32,48,128]{2,1,0:T(8,128)(2,1)} %broadcast_in_dim.10), calls=%async_computation | async-start | bytes 786432 | tf_op jit(solution)/shard_map/all_to_all | solution.py:220
  13.9 5.7 %norm_kv.1 = (bf16[8,256,640]{2,1,0:T(8,128)(2,1)}, bf16[64,256]{1,0:T(8,128)(2,1)}) custom-call(bf16[256,5120]{1,0:T(8,128)(2,1)} %bitcast.8, bf16[64,5120]{1,0:T(8,128)(2,1)} %bitcast.9), custom_call_target="tpu_custom_call" | custom-call | flops 170000000 | bytes 8000000 | tf_op jit(solution)/shard_map/norm_kv/pallas_call | solution.py:235
  20.4 8.0 %all-to-all-done.got = bf16[32,48,128]{2,1,0:T(8,128)(2,1)S(1)} async-done(((bf16[32,48,128]{2,1,0:T(8,128)(2,1)}), bf16[32,48,128]{2,1,0:T(8,128)(2,1)S(1)}, u32[]{:S(2)}, u32[]{:S(2)}) %all-to-all-start) | async-done | bytes 393248 | tf_op jit(solution)/shard_map/all_to_all | solution.py:220
  28.4 0.8 copy-done.2
  29.2 1.9 %sort_rows.1.refs_0_ = bf16[720,128]{1,0:T(8,128)(2,1)} custom-call(s32[5]{0:T(128)} %stack.23.ids, bf16[32,48,128]{2,1,0:T(8,128)(2,1)} %copy-done.2), custom_call_target="tpu_custom_call" | custom-call | tf_op jit(solution)/shard_map/sort_rows/pallas_call | solution.py:223
  31.1 2.8 %collective-permute-start.5 = (bf16[720,128]{1,0:T(8,128)(2,1)}, bf16[720,128]{1,0:T(8,128)(2,1)S(1)}, u32[]{:S(2)}, u32[]{:S(2)}) collective-permute-start(bf16[720,128]{1,0:T(8,128)(2,1)} %sort_rows.1.refs_0_), channel_id=1, source_target_pairs={{0,192},{64,0},{128,64},{192,128},{1,193},{65,1},{129,65},{193,129... | collective-permute-start | bytes 552968 | tf_op jit(solution)/shard_map/ppermute | solution.py:232
  33.9 1.6 %constant_dynamic-slice_fusion = (bf16[256,1280]{1,0:T(8,128)(2,1)}, bf16[256,1280]{1,0:T(8,128)(2,1)}, bf16[256,1280]{1,0:T(8,128)(2,1)}, bf16[256,1280]{1,0:T(8,128)(2,1)}) fusion(bf16[256,5120]{1,0:T(8,128)(2,1)S(1)} %copy-done, s32[]{:T(128)S(6)} %select_n.33, s32[]{:T(128)S(6)} %select_n.29, s32[]{:T(128)S(6)} %select_n.27, s32[]{:T(128)S(6)} %select_n.31), kind=kLoop, calls=%fused_computation.1 | loop fusion | bytes 5242896 | tf_op jit(solution)/shard_map/dynamic_slice | solution.py:205
  35.4 1.3 collective-permute-start.16
  36.7 0.8 collective-permute-start.9
  37.5 0.8 collective-permute-start.3
  38.3 0.9 collective-permute-start.1
  39.2 3.0 %collective-permute-done.9.refs_14_ = bf16[64,256]{1,0:T(8,128)(2,1)S(1)} collective-permute-done((bf16[64,256]{1,0:T(8,128)(2,1)S(1)}, bf16[64,256]{1,0:T(8,128)(2,1)S(1)}, u32[]{:S(2)}, u32[]{:S(2)}) %collective-permute-start.9) | collective-permute-done | bytes 32800 | tf_op jit(solution)/shard_map/ppermute | solution.py:246
  42.5 3.5 %collective-permute-done.8.refs_13_ = bf16[64,256]{1,0:T(8,128)(2,1)S(1)} collective-permute-done((bf16[64,256]{1,0:T(8,128)(2,1)S(1)}, bf16[64,256]{1,0:T(8,128)(2,1)S(1)}, u32[]{:S(2)}, u32[]{:S(2)}) %collective-permute-start.8) | collective-permute-done | bytes 32800 | tf_op jit(solution)/shard_map/ppermute | solution.py:246
  46.0 0.7 collective-permute-start.7
  46.7 16.5 %collective-permute-start.14 = (bf16[256,1280]{1,0:T(8,128)(2,1)}, bf16[256,1280]{1,0:T(8,128)(2,1)S(1)}, u32[]{:S(2)}, u32[]{:S(2)}) collective-permute-start(bf16[256,1280]{1,0:T(8,128)(2,1)} %get-tuple-element.10), channel_id=1, source_target_pairs={{0,4},{4,8},{8,12},{12,0},{1,5},{5,9},{9,13},{13,1},{2,6},{6,10},{... | collective-permute-start | bytes 1966088 | tf_op jit(solution)/shard_map/ppermute | solution.py:209
  63.3 4.4 %collective-permute-start.15 = (bf16[256,1280]{1,0:T(8,128)(2,1)}, bf16[256,1280]{1,0:T(8,128)(2,1)}, u32[]{:S(2)}, u32[]{:S(2)}) collective-permute-start(bf16[256,1280]{1,0:T(8,128)(2,1)} %get-tuple-element.12), channel_id=1, source_target_pairs={{0,8},{4,12},{8,0},{12,4},{1,9},{5,13},{9,1},{13,5},{2,10},{6,14},... | collective-permute-start | bytes 1966088 | tf_op jit(solution)/shard_map/ppermute | solution.py:209
  68.2 0.9 collective-permute-done.refs_1_
  69.6 0.7 copy.13.refs_16_
  71.5 11.4 %attend.1.c0 = bf16[256,256]{1,0:T(8,128)(2,1)} custom-call(s32[5]{0:T(128)} %stack.23.ids, s32[1]{0:T(128)} %bitcast.3.head, bf16[720,128]{1,0:T(8,128)(2,1)} %sort_rows.1.refs_0_, bf16[720,128]{1,0:T(8,128)(2,1)} %copy-done.6, bf16[720,128]{1,0:T(8,128)(2,1)} %copy-done.5, bf16[720,128]{1,0:T(8,128)(2,1)} %copy-done.9, bf16[720,128]{1,0:T(8,128)(2,1)} %copy-done.4, ...), custom_call_target="tpu_custom_call" | custom-call | flops 1000000000 | bytes 10000000 | tf_op jit(solution)/shard_map/attend/pallas_call | solution.py:254
  82.8 1.6 %collective-permute-start.12 = (bf16[256,256]{1,0:T(8,128)(2,1)}, bf16[256,256]{1,0:T(8,128)(2,1)S(1)}, u32[]{:S(2)}, u32[]{:S(2)}) collective-permute-start(bf16[256,256]{1,0:T(8,128)(2,1)} %attend.1.c0), channel_id=1, source_target_pairs={{0,8},{4,12},{8,0},{12,4},{1,9},{5,13},{9,1},{13,5},{2,10},{6,14},... | collective-permute-start | bytes 393224 | tf_op jit(solution)/shard_map/ppermute | solution.py:276
  85.0 8.9 %collective-permute-done.15.refs_10_ = bf16[256,1280]{1,0:T(8,128)(2,1)} collective-permute-done((bf16[256,1280]{1,0:T(8,128)(2,1)}, bf16[256,1280]{1,0:T(8,128)(2,1)}, u32[]{:S(2)}, u32[]{:S(2)}) %collective-permute-start.15) | collective-permute-done | bytes 655392 | tf_op jit(solution)/shard_map/ppermute | solution.py:209
  93.8 6.6 %merge_o.1.merged = bf16[4,4,256,320]{3,2,1,0:T(8,128)(2,1)} custom-call(s32[5]{0:T(128)} %stack.23.ids, bf16[720,128]{1,0:T(8,128)(2,1)} %sort_rows.1.refs_0_, bf16[720,128]{1,0:T(8,128)(2,1)} %copy-done.6, bf16[720,128]{1,0:T(8,128)(2,1)} %copy-done.5, bf16[720,128]{1,0:T(8,128)(2,1)} %copy-done.9, bf16[720,128]{1,0:T(8,128)(2,1)} %copy-done.4, ...), custom_call_target="tpu_custom_call" | custom-call | flops 340000000 | bytes 8000000 | tf_op jit(solution)/shard_map/merge_o/pallas_call | solution.py:277
  100.4 0.6 copy-done.12
  101.1 0.7 copy-done.14
  101.8 4.3 %project.1 = bf16[4,256,320]{2,1,0:T(8,128)(2,1)} custom-call(bf16[256,256]{1,0:T(8,128)(2,1)} %attend.1.c0, bf16[256,256]{1,0:T(8,128)(2,1)} %copy-done.14, bf16[256,256]{1,0:T(8,128)(2,1)} %copy-done.13, bf16[256,256]{1,0:T(8,128)(2,1)} %copy-done.12, bf16[4,4,256,320]{3,2,1,0:T(8,128)(2,1)} %merge_o.1.merged), custom_call_target="tpu_custom_call" | custom-call | flops 680000000 | bytes 4000000 | tf_op jit(solution)/shard_map/project/pallas_call | solution.py:286
  106.1 1.4 %copy.14 = bf16[4,256,320]{1,2,0:T(8,128)(2,1)S(1)} copy(bf16[4,256,320]{2,1,0:T(8,128)(2,1)} %project.1) | data formatting | bytes 1310720 | tf_op jit(solution)/shard_map/project/pallas_call | solution.py:286
  107.5 18.2 %all_to_all.10 = bf16[4,256,320]{1,2,0:T(8,128)(2,1)S(1)} all-to-all(bf16[4,256,320]{1,2,0:T(8,128)(2,1)S(1)} %copy.14), channel_id=1, replica_groups=mesh['x'=4,'zh'=2,'c'=2,'y'=4,'z'=4] {'z'}, dimensions={0} | all-to-all | bytes 1310720 | tf_op jit(solution)/shard_map/all_to_all | solution.py:293
  125.6 1.2 copy.15.parts
  126.8 1.9 %sum_parts.1 = bf16[4,64,320]{2,1,0:T(8,128)(2,1)} custom-call(bf16[4,256,320]{2,1,0:T(8,128)(2,1)} %copy.15.parts), custom_call_target="tpu_custom_call" | custom-call | tf_op jit(solution)/shard_map/sum_parts/pallas_call | solution.py:294
  (63 shorter events, 4.2 us)
Async XLA Ops:
  1.5 32.4 %copy-start = (bf16[256,5120]{1,0:T(8,128)(2,1)S(1)}, bf16[256,5120]{1,0:T(8,128)(2,1)}, u32[]{:S(2)}) copy-start(bf16[256,5120]{1,0:T(8,128)(2,1)} %param.14) | copy-start | bytes 7864324
  2.5 25.9 %all-to-all-start = ((bf16[32,48,128]{2,1,0:T(8,128)(2,1)}), bf16[32,48,128]{2,1,0:T(8,128)(2,1)S(1)}, u32[]{:S(2)}, u32[]{:S(2)}) async-start(bf16[32,48,128]{2,1,0:T(8,128)(2,1)} %broadcast_in_dim.10), calls=%async_computation | async-start | bytes 786432 | tf_op jit(solution)/shard_map/all_to_all | solution.py:220
  19.6 18.7 %collective-permute-start.10 = (bf16[64,256]{1,0:T(8,128)(2,1)}, bf16[64,256]{1,0:T(8,128)(2,1)S(1)}, u32[]{:S(2)}, u32[]{:S(2)}) collective-permute-start(bf16[64,256]{1,0:T(8,128)(2,1)} %get-tuple-element.8), channel_id=1, source_target_pairs={{0,3},{1,0},{2,7},{3,4},{4,11},{5,8},{6,15},{7,12},{8,1},{9,2},{10... | collective-permute-start | bytes 98312 | tf_op jit(solution)/shard_map/ppermute | solution.py:246
  31.1 5.6 %copy-start.20 = (bf16[64,256]{1,0:T(8,128)(2,1)S(1)}, bf16[64,256]{1,0:T(8,128)(2,1)}, u32[]{:S(2)}) copy-start(bf16[64,256]{1,0:T(8,128)(2,1)} %get-tuple-element.8) | copy-start | bytes 98308
  31.1 6.4 %copy-start.1 = (bf16[720,128]{1,0:T(8,128)(2,1)S(1)}, bf16[720,128]{1,0:T(8,128)(2,1)}, u32[]{:S(2)}) copy-start(bf16[720,128]{1,0:T(8,128)(2,1)} %sort_rows.1.refs_0_) | copy-start | bytes 552964
  31.1 38.5 %copy-start.19 = (s32[64]{0:T(128)S(1)}, s32[64]{0:T(128)}, u32[]{:S(2)}) copy-start(s32[64]{0:T(128)} %param.21) | copy-start | bytes 772
  31.1 32.1 %collective-permute-start.5 = (bf16[720,128]{1,0:T(8,128)(2,1)}, bf16[720,128]{1,0:T(8,128)(2,1)S(1)}, u32[]{:S(2)}, u32[]{:S(2)}) collective-permute-start(bf16[720,128]{1,0:T(8,128)(2,1)} %sort_rows.1.refs_0_), channel_id=1, source_target_pairs={{0,192},{64,0},{128,64},{192,128},{1,193},{65,1},{129,65},{193,129... | collective-permute-start | bytes 552968 | tf_op jit(solution)/shard_map/ppermute | solution.py:232
  35.4 49.0 %collective-permute-start.16 = (bf16[256,1280]{1,0:T(8,128)(2,1)}, bf16[256,1280]{1,0:T(8,128)(2,1)S(1)}, u32[]{:S(2)}, u32[]{:S(2)}) collective-permute-start(bf16[256,1280]{1,0:T(8,128)(2,1)} %get-tuple-element.9), channel_id=1, source_target_pairs={{0,12},{4,0},{8,4},{12,8},{1,13},{5,1},{9,5},{13,9},{2,14},{6,2},{... | collective-permute-start | bytes 1966088 | tf_op jit(solution)/shard_map/ppermute | solution.py:209
  36.7 5.4 %collective-permute-start.9 = (bf16[64,256]{1,0:T(8,128)(2,1)S(1)}, bf16[64,256]{1,0:T(8,128)(2,1)S(1)}, u32[]{:S(2)}, u32[]{:S(2)}) collective-permute-start(bf16[64,256]{1,0:T(8,128)(2,1)S(1)} %copy-done.20), channel_id=1, source_target_pairs={{0,2},{1,3},{2,6},{3,7},{4,10},{5,11},{6,14},{7,15},{8,0},{9,1},{1... | collective-permute-start | bytes 98312 | tf_op jit(solution)/shard_map/ppermute | solution.py:246
  37.5 30.2 %collective-permute-start.3 = (bf16[720,128]{1,0:T(8,128)(2,1)S(1)}, bf16[720,128]{1,0:T(8,128)(2,1)S(1)}, u32[]{:S(2)}, u32[]{:S(2)}) collective-permute-start(bf16[720,128]{1,0:T(8,128)(2,1)S(1)} %copy-done.1), channel_id=1, source_target_pairs={{0,128},{64,192},{128,0},{192,64},{1,129},{65,193},{129,1},{193,65... | collective-permute-start | bytes 552968 | tf_op jit(solution)/shard_map/ppermute | solution.py:232
  38.3 32.5 %copy-start.15 = (bf16[64,256]{1,0:T(8,128)(2,1)}, bf16[64,256]{1,0:T(8,128)(2,1)S(1)}, u32[]{:S(2)}) copy-start(bf16[64,256]{1,0:T(8,128)(2,1)S(1)} %collective-permute-done.10.refs_15_) | copy-start | bytes 98308
  38.3 29.4 %collective-permute-start.1 = (bf16[720,128]{1,0:T(8,128)(2,1)S(1)}, bf16[720,128]{1,0:T(8,128)(2,1)S(1)}, u32[]{:S(2)}, u32[]{:S(2)}) collective-permute-start(bf16[720,128]{1,0:T(8,128)(2,1)S(1)} %copy-done.1), channel_id=1, source_target_pairs={{0,64},{64,128},{128,192},{192,0},{1,65},{65,129},{129,193},{193,1... | collective-permute-start | bytes 552968 | tf_op jit(solution)/shard_map/ppermute | solution.py:232
  42.1 28.7 %copy-start.16 = (bf16[64,256]{1,0:T(8,128)(2,1)}, bf16[64,256]{1,0:T(8,128)(2,1)S(1)}, u32[]{:S(2)}) copy-start(bf16[64,256]{1,0:T(8,128)(2,1)S(1)} %collective-permute-done.9.refs_14_) | copy-start | bytes 98308
  42.1 3.9 %collective-permute-start.8 = (bf16[64,256]{1,0:T(8,128)(2,1)S(1)}, bf16[64,256]{1,0:T(8,128)(2,1)S(1)}, u32[]{:S(2)}, u32[]{:S(2)}) collective-permute-start(bf16[64,256]{1,0:T(8,128)(2,1)S(1)} %copy-done.20), channel_id=1, source_target_pairs={{0,1},{1,2},{2,5},{3,6},{4,9},{5,10},{6,13},{7,14},{8,3},{9,0},{10... | collective-permute-start | bytes 98312 | tf_op jit(solution)/shard_map/ppermute | solution.py:246
  46.0 24.8 %copy-start.17 = (bf16[64,256]{1,0:T(8,128)(2,1)}, bf16[64,256]{1,0:T(8,128)(2,1)S(1)}, u32[]{:S(2)}) copy-start(bf16[64,256]{1,0:T(8,128)(2,1)S(1)} %collective-permute-done.8.refs_13_) | copy-start | bytes 98308
  46.0 0.7 collective-permute-start.7
  46.7 24.1 %copy-start.18 = (bf16[64,256]{1,0:T(8,128)(2,1)}, bf16[64,256]{1,0:T(8,128)(2,1)S(1)}, u32[]{:S(2)}) copy-start(bf16[64,256]{1,0:T(8,128)(2,1)S(1)} %collective-permute-done.7.refs_12_) | copy-start | bytes 98308
  46.7 38.2 %collective-permute-start.14 = (bf16[256,1280]{1,0:T(8,128)(2,1)}, bf16[256,1280]{1,0:T(8,128)(2,1)S(1)}, u32[]{:S(2)}, u32[]{:S(2)}) collective-permute-start(bf16[256,1280]{1,0:T(8,128)(2,1)} %get-tuple-element.10), channel_id=1, source_target_pairs={{0,4},{4,8},{8,12},{12,0},{1,5},{5,9},{9,13},{13,1},{2,6},{6,10},{... | collective-permute-start | bytes 1966088 | tf_op jit(solution)/shard_map/ppermute | solution.py:209
  63.3 7.6 %copy-start.3 = (bf16[720,128]{1,0:T(8,128)(2,1)}, bf16[720,128]{1,0:T(8,128)(2,1)S(1)}, u32[]{:S(2)}) copy-start(bf16[720,128]{1,0:T(8,128)(2,1)S(1)} %collective-permute-done.5.refs_6_) | copy-start | bytes 552964
  63.3 30.6 %collective-permute-start.15 = (bf16[256,1280]{1,0:T(8,128)(2,1)}, bf16[256,1280]{1,0:T(8,128)(2,1)}, u32[]{:S(2)}, u32[]{:S(2)}) collective-permute-start(bf16[256,1280]{1,0:T(8,128)(2,1)} %get-tuple-element.12), channel_id=1, source_target_pairs={{0,8},{4,12},{8,0},{12,4},{1,9},{5,13},{9,1},{13,5},{2,10},{6,14},... | collective-permute-start | bytes 1966088 | tf_op jit(solution)/shard_map/ppermute | solution.py:209
  67.7 3.2 %copy-start.4 = (bf16[720,128]{1,0:T(8,128)(2,1)}, bf16[720,128]{1,0:T(8,128)(2,1)S(1)}, u32[]{:S(2)}) copy-start(bf16[720,128]{1,0:T(8,128)(2,1)S(1)} %collective-permute-done.3.refs_4_) | copy-start | bytes 552964
  67.7 1.4 %collective-permute-start = (bf16[720,128]{1,0:T(8,128)(2,1)S(1)}, bf16[720,128]{1,0:T(8,128)(2,1)S(1)}, u32[]{:S(2)}, u32[]{:S(2)}) collective-permute-start(bf16[720,128]{1,0:T(8,128)(2,1)S(1)} %copy-done.1), channel_id=1, source_target_pairs={{0,16},{16,0},{1,17},{17,1},{2,18},{18,2},{3,19},{19,3},{4,20},{20... | collective-permute-start | bytes 552968 | tf_op jit(solution)/shard_map/ppermute | solution.py:233
  67.7 3.2 %copy-start.5 = (bf16[720,128]{1,0:T(8,128)(2,1)}, bf16[720,128]{1,0:T(8,128)(2,1)S(1)}, u32[]{:S(2)}) copy-start(bf16[720,128]{1,0:T(8,128)(2,1)S(1)} %collective-permute-done.1.refs_2_) | copy-start | bytes 552964
  67.7 1.7 %collective-permute-start.6 = (bf16[720,128]{1,0:T(8,128)(2,1)S(1)}, bf16[720,128]{1,0:T(8,128)(2,1)S(1)}, u32[]{:S(2)}, u32[]{:S(2)}) collective-permute-start(bf16[720,128]{1,0:T(8,128)(2,1)S(1)} %collective-permute-done.5.refs_6_), channel_id=1, source_target_pairs={{0,16},{16,0},{1,17},{17,1},{2,18},{18,2},{3,19},{19,3},{4,20},{20... | collective-permute-start | bytes 552968 | tf_op jit(solution)/shard_map/ppermute | solution.py:233
  69.1 1.8 %copy-start.6 = (bf16[720,128]{1,0:T(8,128)(2,1)}, bf16[720,128]{1,0:T(8,128)(2,1)S(1)}, u32[]{:S(2)}) copy-start(bf16[720,128]{1,0:T(8,128)(2,1)S(1)} %collective-permute-done.refs_1_) | copy-start | bytes 552964
  69.1 1.4 %collective-permute-start.4 = (bf16[720,128]{1,0:T(8,128)(2,1)S(1)}, bf16[720,128]{1,0:T(8,128)(2,1)S(1)}, u32[]{:S(2)}, u32[]{:S(2)}) collective-permute-start(bf16[720,128]{1,0:T(8,128)(2,1)S(1)} %collective-permute-done.3.refs_4_), channel_id=1, source_target_pairs={{0,16},{16,0},{1,17},{17,1},{2,18},{18,2},{3,19},{19,3},{4,20},{20... | collective-permute-start | bytes 552968 | tf_op jit(solution)/shard_map/ppermute | solution.py:233
  69.3 1.4 %collective-permute-start.2 = (bf16[720,128]{1,0:T(8,128)(2,1)S(1)}, bf16[720,128]{1,0:T(8,128)(2,1)S(1)}, u32[]{:S(2)}, u32[]{:S(2)}) collective-permute-start(bf16[720,128]{1,0:T(8,128)(2,1)S(1)} %collective-permute-done.1.refs_2_), channel_id=1, source_target_pairs={{0,16},{16,0},{1,17},{17,1},{2,18},{18,2},{3,19},{19,3},{4,20},{20... | collective-permute-start | bytes 552968 | tf_op jit(solution)/shard_map/ppermute | solution.py:233
  82.8 17.6 %collective-permute-start.13 = (bf16[256,256]{1,0:T(8,128)(2,1)}, bf16[256,256]{1,0:T(8,128)(2,1)S(1)}, u32[]{:S(2)}, u32[]{:S(2)}) collective-permute-start(bf16[256,256]{1,0:T(8,128)(2,1)} %attend.1.c0), channel_id=1, source_target_pairs={{0,12},{4,0},{8,4},{12,8},{1,13},{5,1},{9,5},{13,9},{2,14},{6,2},{... | collective-permute-start | bytes 393224 | tf_op jit(solution)/shard_map/ppermute | solution.py:276
  82.8 17.6 %collective-permute-start.12 = (bf16[256,256]{1,0:T(8,128)(2,1)}, bf16[256,256]{1,0:T(8,128)(2,1)S(1)}, u32[]{:S(2)}, u32[]{:S(2)}) collective-permute-start(bf16[256,256]{1,0:T(8,128)(2,1)} %attend.1.c0), channel_id=1, source_target_pairs={{0,8},{4,12},{8,0},{12,4},{1,9},{5,13},{9,1},{13,5},{2,10},{6,14},... | collective-permute-start | bytes 393224 | tf_op jit(solution)/shard_map/ppermute | solution.py:276
  84.4 9.4 %copy-start.10 = (bf16[256,1280]{1,0:T(8,128)(2,1)}, bf16[256,1280]{1,0:T(8,128)(2,1)S(1)}, u32[]{:S(2)}) copy-start(bf16[256,1280]{1,0:T(8,128)(2,1)S(1)} %collective-permute-done.16.refs_11_) | copy-start | bytes 1966084
  84.4 16.0 %collective-permute-start.11 = (bf16[256,256]{1,0:T(8,128)(2,1)}, bf16[256,256]{1,0:T(8,128)(2,1)S(1)}, u32[]{:S(2)}, u32[]{:S(2)}) collective-permute-start(bf16[256,256]{1,0:T(8,128)(2,1)} %attend.1.c0), channel_id=1, source_target_pairs={{0,4},{4,8},{8,12},{12,0},{1,5},{5,9},{9,13},{13,1},{2,6},{6,10},{... | collective-permute-start | bytes 393224 | tf_op jit(solution)/shard_map/ppermute | solution.py:276
  85.0 8.9 %copy-start.11 = (bf16[256,1280]{1,0:T(8,128)(2,1)}, bf16[256,1280]{1,0:T(8,128)(2,1)S(1)}, u32[]{:S(2)}) copy-start(bf16[256,1280]{1,0:T(8,128)(2,1)S(1)} %collective-permute-done.14.refs_9_) | copy-start | bytes 1966084
  (7 other events, 5.6 us)

commit v2 on v1

v2 whole, which is shorter than its diff:
```python
import jax
import jax.numpy as jnp
import numpy as np
from jax import lax
from jax.experimental import pallas as pl
from jax.experimental.pallas import tpu as pltpu
from jax.sharding import Mesh
from jax.sharding import PartitionSpec as P

HD = 128
STEPS = 4
ROWS = 256
WIDTH = 5120
NX, NZH, NC, NY, NZ = 4, 2, 2, 4, 4
GROUP = ("x", "zh", "c")
TP = ("y", "z")
BF = jnp.bfloat16
F32 = jnp.float32
MSG = 40
XROWS = 720

SMEM = pl.BlockSpec(memory_space=pltpu.SMEM)


def params(mib):
    return pltpu.CompilerParams(vmem_limit_bytes=mib * 1024 * 1024)


def mm(a, b):
    return jnp.dot(a, b, preferred_element_type=F32)


def mm_t(a, b):
    return lax.dot_general(a, b, (((1,), (1,)), ((), ())), preferred_element_type=F32)


def pack_kernel(ids, low, up, q_up, o_low, wo, out, own, *rest):
    sent, (low_v, up_v, qu_v, ol_v, sems) = rest[:3], rest[3:]
    c, y = ids[2], ids[3]
    half = pl.ds(pl.multiple_of(c * 128, 128), 128)
    small = [
        pltpu.make_async_copy(a, b, sems.at[4 + n])
        for n, (a, b) in enumerate(((low, low_v), (up, up_v), (q_up, qu_v), (o_low, ol_v)))
    ]
    large = [pltpu.make_async_copy(wo.at[:, pl.ds(pl.multiple_of(y * 1280, 1280), 1280)], own, sems.at[0])]
    for n, ref in enumerate(sent):
        at = pl.multiple_of(((y + n + 1) & 3) * 1280, 1280)
        large.append(pltpu.make_async_copy(wo.at[half, pl.ds(at, 1280)], ref, sems.at[n + 1]))
    for copy in small + large:
        copy.start()
    for copy in small:
        copy.wait()

    def halves(ref):
        a = ref[...].astype(F32)
        return [a[:, :128], a[:, 128:]]

    first = jnp.concatenate([low_v[...].astype(F32), up_v[...].astype(F32)], axis=1)
    rows = [first, jnp.zeros((4, 128), F32)] + halves(qu_v) + halves(ol_v)
    message = jnp.concatenate(rows, axis=0).astype(BF)

    def write(i, carry):
        out[i] = message
        return carry

    lax.fori_loop(0, out.shape[0], write, 0)
    for copy in large:
        copy.wait()


def norm_kernel(states, wkv_t, blocks, kv_t, x_v, w_v, flat, out_v, sems):
    loads = [pltpu.make_async_copy(states.at[n], x_v.at[n], sems.at[n]) for n in range(STEPS)]
    loads.append(pltpu.make_async_copy(wkv_t, w_v, sems.at[STEPS]))
    for copy in loads:
        copy.start()
    for n in range(STEPS):
        loads[n].wait()

        def rows(i, carry):
            r = pl.multiple_of(i * 32, 32)
            x = x_v[n, pl.ds(r, 32), :].astype(F32)
            scale = lax.rsqrt(jnp.mean(x * x, axis=1, keepdims=True) + 1e-06)
            normed = (x * scale).astype(BF)
            to = pl.ds(pl.multiple_of(n * 64 + r, 32), 32)
            flat[to, :] = normed
            for xc in range(8):
                g = (xc // 2) * 4 + xc % 2
                out_v[xc, to, :] = jnp.concatenate(
                    [normed[:, g * 320 : g * 320 + 320], normed[:, g * 320 + 640 : g * 320 + 960]], axis=1
                )
            return carry

        lax.fori_loop(0, 2, rows, 0)
    store = pltpu.make_async_copy(out_v, blocks, sems.at[0])
    store.start()
    loads[STEPS].wait()
    kv_t[...] = mm_t(flat[...], w_v[...]).T.astype(BF)
    store.wait()


def sort_kernel(ids, got, out):
    i = lax.broadcasted_iota(jnp.int32, (80, MSG), 0)
    j = lax.broadcasted_iota(jnp.int32, (80, MSG), 1)
    picks = [jnp.where((j == i - 20 * p) & (j < 20), 1.0, 0.0).astype(BF) for p in range(4)]
    for q in range(8):
        rows = mm(picks[0], got[4 * q])
        for p in range(1, 4):
            rows = rows + mm(picks[p], got[4 * q + p])
        out[80 * q : 80 * q + 80, :] = rows.astype(BF)
    y, z = ids[3], ids[4]
    own = [got[zh * 16 + y * NZ + z].astype(F32)[24:32] for zh in range(2)]
    out[640:656, :] = jnp.concatenate(own, axis=0).astype(BF)
    for yy in range(NY):
        part = [got[zh * 16 + yy * NZ + z].astype(F32)[32:40] for zh in range(2)]
        out[656 + 16 * yy : 672 + 16 * yy, :] = jnp.concatenate(part, axis=0).astype(BF)


def rank_order(ids, half, first):
    r = lax.broadcasted_iota(jnp.int32, (128, 128), 0)
    j = lax.broadcasted_iota(jnp.int32, (128, 128), 1)
    x, c = ids[0], ids[2]
    k, o = (j >> 5) & 3, (j >> 4) & 1
    zh, h, i = (j >> 3) & 1, (j >> 2) & 1, j & 3
    xs = (x - k + 4) & 3
    rank = (xs * 4 + zh * 2 + (c + o - 2 * c * o)) * 4 + i
    return jnp.where((h == half) & (r == rank + first), 1.0, 0.0).astype(BF)


def attend_kernel(ids, *refs):
    blocks = refs[:8]
    wq_h, normed_h, kc_h, vc_h, kv0, kv1, kv2, kv3, lens, ctx = refs[8:18]
    kv, qs, cs, wq, normed, kc, vc, sems = refs[18:]
    x, c, y, z = ids[0], ids[2], ids[3], ids[4]
    steps, loads = [], []
    for n in range(8):
        k, o = n // 2, n % 2
        at = ((x - k + 4) & 3) * 2 + c + o - 2 * c * o
        row = (at >> 1) * 1280 + (at & 1) * 320
        parts = [pl.ds(pl.multiple_of(row + 640 * zh, 320), 320) for zh in range(2)]
        copies = [
            pltpu.make_async_copy(wq_h.at[parts[0]], wq.at[n, 0:320], sems.at[n, 0]),
            pltpu.make_async_copy(wq_h.at[parts[1]], wq.at[n, 320:640], sems.at[n, 1]),
            pltpu.make_async_copy(normed_h.at[at], normed.at[n], sems.at[n, 2]),
        ]
        steps.append(copies)
    loads = [
        pltpu.make_async_copy(kc_h.at[:, y], kc, sems.at[8, 0]),
        pltpu.make_async_copy(vc_h.at[:, y], vc, sems.at[8, 1]),
    ]
    for copies in steps + [loads]:
        for copy in copies:
            copy.start()
    stack = jnp.concatenate([b[640:656, :] for b in blocks], axis=0)
    upper = jnp.concatenate(
        [2.0 * mm(rank_order(ids, h, 0), stack) for h in range(2)], axis=1
    ).astype(BF)
    total = jnp.zeros((ROWS, 256), F32)
    for n in range(8):
        rank = mm(blocks[n][0:640, :], upper)
        for copy in steps[n]:
            copy.wait()
        merged = (wq[n].astype(F32) + rank).astype(BF)
        total = total + mm(normed[n], merged)
    qs[...] = total.astype(BF).astype(F32)
    for k, ref in enumerate((kv0, kv1, kv2, kv3)):
        kv[(z - k + 4) & 3] = ref[...]
    key_t = kv[0:2].reshape(128, 256)
    val = kv[2:4].reshape(128, 256).astype(F32).T.astype(BF)
    for copy in loads:
        copy.wait()
    factor = 1.0 / HD**0.5
    c8 = lax.broadcasted_iota(jnp.int32, (8, 512), 1)
    r8 = lax.broadcasted_iota(jnp.int32, (8, 512), 0)
    own_cached = (c8 >> 6) == r8
    pos = c8 & 63
    cn = lax.broadcasted_iota(jnp.int32, (64, 256), 1)
    rn = lax.broadcasted_iota(jnp.int32, (64, 256), 0)
    seen = (cn >> 6) <= (rn >> 4)

    def batch(b, carry):
        r = pl.multiple_of(b * 8, 8)
        q = jnp.concatenate(
            [qs[pl.ds(s * 64 + r, 8), h * 128 : h * 128 + 128] for s in range(4) for h in range(2)], axis=0
        ).astype(BF)
        keys = kc[pl.ds(r, 8)].reshape(512, 128)
        vals = vc[pl.ds(r, 8)].reshape(512, 128)
        length = jnp.zeros((8, 512), jnp.int32)
        for i in range(8):
            length = jnp.where(r8 == i, lens[r + i], length)
        ok = jnp.where(own_cached & (pos < length), 1.0, 0.0)
        okc = jnp.concatenate([ok] * 8, axis=0) > 0.5
        okn = seen & ((cn & 63) == (rn & 7) + r)
        sc = jnp.where(okc, mm_t(q, keys) * factor, -1e30)
        sn = jnp.where(okn, mm(q, key_t) * factor, -1e30)
        top = jnp.maximum(jnp.max(sc, axis=1, keepdims=True), jnp.max(sn, axis=1, keepdims=True))
        ec, en = jnp.exp(sc - top), jnp.exp(sn - top)
        total = jnp.sum(ec, axis=1, keepdims=True) + jnp.sum(en, axis=1, keepdims=True)
        pc, pn = (ec / total).astype(BF), (en / total).astype(BF)
        out = mm(pc, vals) + mm(pn, val)
        for s in range(4):
            for h in range(2):
                n = (s * 2 + h) * 8
                cs[pl.ds(s * 64 + r, 8), h * 128 : h * 128 + 128] = out[n : n + 8]
        return carry

    lax.fori_loop(0, 8, batch, 0, unroll=2)
    ctx[...] = cs[...].astype(BF)


def merge_o_kernel(ids, *refs):
    blocks = refs[:8]
    own = refs[8]
    same, other = refs[9:12], refs[12:15]
    out, hold, low = refs[15:]
    x, c, y = ids[0], ids[2], ids[3]
    ks = (x - y + 4) & 3
    for k in range(4):
        for o in range(2):

            @pl.when(ks == k)
            def _():
                hold[o] = blocks[2 * k + o][0:640, :]

    order = [rank_order(ids, h, 64) for h in range(2)]
    for k in range(4):
        yy = (y - k + 4) & 3
        at = pl.multiple_of(656 + 16 * yy, 16)
        stack = jnp.concatenate([b[pl.ds(at, 16), :] for b in blocks], axis=0)
        lower = jnp.concatenate([2.0 * mm(order[h], stack) for h in range(2)], axis=1)
        low[...] = lower.T.astype(BF)
        for zz in range(4):
            zh, cc = zz // 2, zz % 2
            o = c + cc - 2 * c * cc
            u = hold[o, zh * 320 : zh * 320 + 320, :]
            cols = slice(zz * 320, zz * 320 + 320)
            if k == 0:
                out[k, zz] = (own[:, cols].astype(F32) + mm_t(low[...], u)).astype(BF)
            else:
                for ref, core in ((same[k - 1], c), (other[k - 1], 1 - c)):
                    at = pl.ds(pl.multiple_of(core * 128, 128), 128)
                    out[k, zz, at] = (ref[:, cols].astype(F32) + mm_t(low[at, :], u)).astype(BF)


def project_kernel(c0, c1, c2, c3, merged, out):
    for zz in range(4):
        total = mm(c0[...], merged[0, zz])
        for k, ref in ((1, c1), (2, c2), (3, c3)):
            total = total + mm(ref[...], merged[k, zz])
        total = total.astype(BF)
        out[zz, 0:256] = total[:, 0:128]
        out[zz, 256:512] = total[:, 128:256]
        out[zz, 512:640] = jnp.concatenate([total[0:128, 256:320], total[128:256, 256:320]], axis=1)


def sum_kernel(parts, out):
    total = parts[0].astype(F32)
    for k in range(1, 4):
        total = total + parts[k].astype(F32)
    tail = jnp.concatenate([total[512:640, :64], total[512:640, 64:]], axis=0)
    full = jnp.concatenate([total[0:256], total[256:512], tail], axis=1).astype(BF)
    out[...] = full.reshape(out.shape)


def far(a):
    return pltpu.with_memory_space_constraint(a, pltpu.HBM)


def shift(axis, size, by):
    return [(i, (i + by) % size) for i in range(size)]


def kv_pairs(k):
    pairs = []
    for s in range(16):
        a, e, b = s // 4, (s % 4) // 2, s % 2
        pairs.append((s, (2 * (a % 2) + e) * 4 + ((a // 2) * 2 + b + k) % 4))
    return pairs


def local(states, wq, wkv, wo, qa_low, qa_up, oa_low, oa_up, kcache, vcache, lens):
    x, zh, c, y, z = (lax.axis_index(a) for a in ("x", "zh", "c", "y", "z"))
    ids = jnp.stack([x, zh, c, y, z]).astype(jnp.int32)

    vmem = pl.BlockSpec(memory_space=pltpu.VMEM)
    hbm = pl.BlockSpec(memory_space=pltpu.HBM)

    def array(*shape):
        return jax.ShapeDtypeStruct(shape, BF)

    messages, w_own, *w_sent = pl.pallas_call(
        pack_kernel,
        out_shape=(array(32, MSG, 128), array(256, 1280)) + (array(128, 1280),) * 3,
        in_specs=[SMEM] + [hbm] * 5,
        scratch_shapes=[
            pltpu.VMEM((20, 64), BF),
            pltpu.VMEM((20, 64), BF),
            pltpu.VMEM((4, 256), BF),
            pltpu.VMEM((4, 256), BF),
            pltpu.SemaphoreType.DMA((8,)),
        ],
        compiler_params=params(8),
        name="pack",
    )(ids, *(far(a) for a in (qa_low, oa_up, qa_up, oa_low, wo)))
    got = lax.all_to_all(messages, ("zh", "y", "z"), 0, 0, tiled=True)

    normed, kv_t = pl.pallas_call(
        norm_kernel,
        out_shape=(pltpu.HBM((8, ROWS, 640), BF), array(64, ROWS)),
        in_specs=[hbm, hbm],
        out_specs=(hbm, vmem),
        scratch_shapes=[
            pltpu.VMEM((STEPS, 64, WIDTH), BF),
            pltpu.VMEM((64, WIDTH), BF),
            pltpu.VMEM((ROWS, WIDTH), BF),
            pltpu.VMEM((8, ROWS, 640), BF),
            pltpu.SemaphoreType.DMA((5,)),
        ],
        compiler_params=params(24),
        cost_estimate=pl.CostEstimate(flops=170_000_000, bytes_accessed=8_000_000, transcendentals=0),
        name="norm_kv",
    )(far(states), far(wkv.T))
    new_kv = [lax.ppermute(kv_t, TP, kv_pairs(k)) for k in range(4)]

    swap = [(0, 1), (1, 0)]
    w_same = [lax.ppermute(w_sent[0], "y", shift("y", 4, 1))]
    got, normed, w_same[0] = lax.optimization_barrier((got, normed, w_same[0]))
    mine = pl.pallas_call(
        sort_kernel,
        out_shape=array(XROWS, 128),
        in_specs=[SMEM, vmem],
        compiler_params=params(6),
        name="sort_rows",
    )(ids, got)
    mine, w_second, *new_kv = lax.optimization_barrier((mine, w_sent[1], *new_kv))
    w_same.append(lax.ppermute(w_second, "y", shift("y", 4, 2)))
    parts = [mine] + [lax.ppermute(mine, "x", shift("x", 4, s)) for s in (1, 2, 3)]
    *parts, w_same[1], w_third = lax.optimization_barrier((*parts, w_same[1], w_sent[2]))
    w_same.append(lax.ppermute(w_third, "y", shift("y", 4, 3)))
    blocks = []
    for part in parts:
        blocks += [part, lax.ppermute(part, "c", swap)]

    ctx = pl.pallas_call(
        attend_kernel,
        out_shape=array(ROWS, 256),
        in_specs=[SMEM] + [vmem] * 8 + [hbm] * 4 + [vmem] * 4 + [SMEM],
        scratch_shapes=[
            pltpu.VMEM((4, 64, 256), BF),
            pltpu.VMEM((ROWS, 256), F32),
            pltpu.VMEM((ROWS, 256), F32),
            pltpu.VMEM((8, 640, 256), BF),
            pltpu.VMEM((8, ROWS, 640), BF),
            pltpu.VMEM((64, 64, 128), BF),
            pltpu.VMEM((64, 64, 128), BF),
            pltpu.SemaphoreType.DMA((9, 3)),
        ],
        compiler_params=params(24),
        cost_estimate=pl.CostEstimate(flops=1_000_000_000, bytes_accessed=10_000_000, transcendentals=400_000),
        name="attend",
    )(ids, *blocks, far(wq), far(normed), far(kcache), far(vcache), *new_kv, lens)

    others = [lax.ppermute(ctx, "y", shift("y", 4, s)) for s in (1, 2, 3)]
    w_other = [lax.ppermute(w, "c", swap) for w in w_same]
    merged = pl.pallas_call(
        merge_o_kernel,
        out_shape=array(4, 4, 256, 320),
        in_specs=[SMEM] + [vmem] * 15,
        scratch_shapes=[pltpu.VMEM((2, 640, 128), BF), pltpu.VMEM((256, 128), BF)],
        compiler_params=params(20),
        cost_estimate=pl.CostEstimate(flops=340_000_000, bytes_accessed=8_000_000, transcendentals=0),
        name="merge_o",
    )(ids, *blocks, w_own, *w_same, *w_other)
    parts = pl.pallas_call(
        project_kernel,
        out_shape=array(4, 640, 128),
        compiler_params=params(16),
        cost_estimate=pl.CostEstimate(flops=680_000_000, bytes_accessed=4_000_000, transcendentals=0),
        name="project",
    )(ctx, *others, merged)
    parts = lax.all_to_all(parts, "z", 0, 0, tiled=True)
    return pl.pallas_call(
        sum_kernel,
        out_shape=array(4, 64, 320),
        compiler_params=params(6),
        name="sum_parts",
    )(parts)


def solution(mesh):
    fine = Mesh(np.asarray(mesh.devices).reshape(NX, NZH, NC, NY, NZ), GROUP + TP)
    every = GROUP + TP
    in_specs = (
        P(None, GROUP, None),
        P(None, TP),
        P(None, TP),
        P(TP, None),
        P(every, None),
        P(GROUP, TP),
        P(GROUP, TP),
        P(every, None),
        P(GROUP, None, None, None),
        P(GROUP, None, None, None),
        P(GROUP),
    )
    out_specs = P(None, GROUP, TP)
    return jax.shard_map(local, mesh=fine, in_specs=in_specs, out_specs=out_specs, check_vma=False)
```

time: 129 us -> 100 us (0.78)
  local copies, waits for them, and re-layouts: 9.88 us -> 0.09 us
  Pallas kernels: 31.7 us -> 22.6 us
  waiting for transfers between devices: 24.9 us -> 18.5 us
  starting transfers between devices: 43.1 us -> 38.7 us
    ppermute x10 -> x13, starting transfers between devices: 27.5 us -> 16.9 us  [the longest x1 4.98 us: local(): w_same.append(lax.ppermute(w_second, 'y', shift('y', 4, 2)))]
    pallas_call x6 -> x7, Pallas kernels: 31.7 us -> 22.6 us  [the longest x1 8.62 us: local(): pl.pallas_call(attend_kernel, out_shape=array(ROWS, 256), in_specs=[SMEM]...]
    all_to_all x1, waiting for transfers between devices: 8.04 us -> 0.01 us  [local(): got = lax.all_to_all(messages, ('zh', 'y', 'z'), 0, 0, tiled=True)]
    ppermute x4, waiting for transfers between devices: 6.46 us -> 0.01 us  [local(): new_kv = [lax.ppermute(kv_t, TP, kv_pairs(k)) for k in range(4)]]
    ppermute x3, waiting for transfers between devices: 0.01 us -> 5.57 us  [local(): others = [lax.ppermute(ctx, 'y', shift('y', 4, s)) for s in (1, 2, 3)]]
    ppermute x4, starting transfers between devices: 2.07 us -> 5.72 us  [local(): new_kv = [lax.ppermute(kv_t, TP, kv_pairs(k)) for k in range(4)]]
    unnamed x42 -> x2, local copies, waits for them, and re-layouts: 2.74 us -> 0.01 us
    ppermute x3, starting transfers between devices: 2.11 us -> 4.73 us  [local(): others = [lax.ppermute(ctx, 'y', shift('y', 4, s)) for s in (1, 2, 3)]]
  transfers between devices with their start and end apart: 18 -> 21, of which waited for: 8 -> 10; matrix products, arithmetic and copies ran while one was open for 2% -> 0% of each run, Pallas kernels for 20% -> 18%
where the time goes in v2:
time: 100 us; the launch traced here: 98.5 us
  starting transfers between devices  38.7 us (39%)
  Pallas kernels  22.6 us (23%)
  waiting for transfers between devices  18.5 us (18%)
  blocking collectives  18.5 us (18%)
    all_to_all x1, blocking collectives, local(): parts = lax.all_to_all(parts, 'z', 0, 0, tiled=True)  18.5 us
    all_to_all x1, starting transfers between devices, local(): got = lax.all_to_all(messages, ('zh', 'y', 'z'), 0, 0, tiled=True)  11.4 us
    pallas_call x1, Pallas kernels, local(): pl.pallas_call(attend_kernel, out_shape=array(ROWS, 256), in_specs=[SMEM]...  8.62 us
    ppermute x3, waiting for transfers between devices, local(): lax.ppermute(mine, 'x', shift('x', 4, s))  7.33 us
    ppermute x4, starting transfers between devices, local(): new_kv = [lax.ppermute(kv_t, TP, kv_pairs(k)) for k in range(4)]  5.72 us
    ppermute x3, waiting for transfers between devices, local(): others = [lax.ppermute(ctx, 'y', shift('y', 4, s)) for s in (1, 2, 3)]  5.57 us
    ppermute x1, starting transfers between devices, local(): w_same.append(lax.ppermute(w_second, 'y', shift('y', 4, 2)))  4.98 us
    pallas_call x1, Pallas kernels, local(): pl.pallas_call(norm_kernel, out_shape=(pltpu.HBM((8, ROWS, 640), BF), arr...  4.94 us
  transfers between devices with their start and end apart: 21, of which 10 were waited for; matrix products, arithmetic and copies ran while one was open for 0% of the time, Pallas kernels for 18%

profile of v2, /device:TPU:32, one launch (start us, length us, event | category | flops | bytes accessed | tf_op | source)
XLA Modules:
  0.0 98.5 jit_solution(1627448209231652113)
XLA Ops:
  0.1 2.8 %pack.1 = (bf16[32,40,128]{2,1,0:T(8,128)(2,1)}, bf16[256,1280]{1,0:T(8,128)(2,1)S(1)}, bf16[128,1280]{1,0:T(8,128)(2,1)S(1)}, bf16[128,1280]{1,0:T(8,128)(2,1)S(1)}, bf16[128,1280]{1,0:T(8,128)(2,1)S(1)}) custom-call(s32[5]{0:T(128)S(1)} %stack.23.ids, bf16[20,64]{1,0:T(8,128)(2,1)} %low.1, bf16[20,64]{1,0:T(8,128)(2,1)} %up.1, bf16[4,256]{1,0:T(4,128)(2,1)} %q_up.1, ...), custom_call_target="tpu_custom_call" | custom-call | tf_op jit(solution)/shard_map/pack/pallas_call | solution.py:290
  2.9 11.4 %all-to-all-start = ((bf16[32,40,128]{2,1,0:T(8,128)(2,1)}), bf16[32,40,128]{2,1,0:T(8,128)(2,1)S(1)}, u32[]{:S(2)}, u32[]{:S(2)}) async-start(bf16[32,40,128]{2,1,0:T(8,128)(2,1)} %get-tuple-element.27), calls=%async_computation | async-start | bytes 655360 | tf_op jit(solution)/shard_map/all_to_all | solution.py:304
  14.3 1.5 %collective-permute-start = (bf16[128,1280]{1,0:T(8,128)(2,1)S(1)}, bf16[128,1280]{1,0:T(8,128)(2,1)S(1)}, u32[]{:S(2)}, u32[]{:S(2)}) collective-permute-start(bf16[128,1280]{1,0:T(8,128)(2,1)S(1)} %get-tuple-element.29), channel_id=1, source_target_pairs={{0,4},{4,8},{8,12},{12,0},{1,5},{5,9},{9,13},{13,1},{2,6},{6,10},{... | collective-permute-start | bytes 983048 | tf_op jit(solution)/shard_map/ppermute | solution.py:325
  15.8 4.9 %norm_kv.1 = (bf16[8,256,640]{2,1,0:T(8,128)(2,1)}, bf16[64,256]{1,0:T(8,128)(2,1)S(1)}) custom-call(bf16[4,64,5120]{2,1,0:T(8,128)(2,1)} %states.1, bf16[64,5120]{1,0:T(8,128)(2,1)} %bitcast.6), custom_call_target="tpu_custom_call" | custom-call | flops 170000000 | bytes 8000000 | tf_op jit(solution)/shard_map/norm_kv/pallas_call | solution.py:306
  20.8 0.6 collective-permute-start.4
  21.4 3.3 %collective-permute-start.3 = (bf16[64,256]{1,0:T(8,128)(2,1)S(1)}, bf16[64,256]{1,0:T(8,128)(2,1)S(1)}, u32[]{:S(2)}, u32[]{:S(2)}) collective-permute-start(bf16[64,256]{1,0:T(8,128)(2,1)S(1)} %get-tuple-element.32), channel_id=1, source_target_pairs={{0,2},{1,3},{2,6},{3,7},{4,10},{5,11},{6,14},{7,15},{8,0},{9,1},{1... | collective-permute-start | bytes 98312 | tf_op jit(solution)/shard_map/ppermute | solution.py:322
  24.7 1.2 %collective-permute-start.2 = (bf16[64,256]{1,0:T(8,128)(2,1)S(1)}, bf16[64,256]{1,0:T(8,128)(2,1)S(1)}, u32[]{:S(2)}, u32[]{:S(2)}) collective-permute-start(bf16[64,256]{1,0:T(8,128)(2,1)S(1)} %get-tuple-element.32), channel_id=1, source_target_pairs={{0,1},{1,2},{2,5},{3,6},{4,9},{5,10},{6,13},{7,14},{8,3},{9,0},{10... | collective-permute-start | bytes 98312 | tf_op jit(solution)/shard_map/ppermute | solution.py:322
  25.8 0.7 collective-permute-start.1
  26.5 2.4 %collective-permute-done.refs_9_ = bf16[128,1280]{1,0:T(8,128)(2,1)S(1)} collective-permute-done((bf16[128,1280]{1,0:T(8,128)(2,1)S(1)}, bf16[128,1280]{1,0:T(8,128)(2,1)S(1)}, u32[]{:S(2)}, u32[]{:S(2)}) %collective-permute-start) | collective-permute-done | bytes 327712 | tf_op jit(solution)/shard_map/ppermute | solution.py:325
  28.9 1.0 %sort_rows.1.refs_0_ = bf16[720,128]{1,0:T(8,128)(2,1)S(1)} custom-call(s32[5]{0:T(128)S(1)} %stack.23.ids, bf16[32,40,128]{2,1,0:T(8,128)(2,1)S(1)} %all-to-all-done.got), custom_call_target="tpu_custom_call" | custom-call | tf_op jit(solution)/shard_map/sort_rows/pallas_call | solution.py:327
  30.0 5.0 %collective-permute-start.8 = (bf16[128,1280]{1,0:T(8,128)(2,1)S(1)}, bf16[128,1280]{1,0:T(8,128)(2,1)S(1)}, u32[]{:S(2)}, u32[]{:S(2)}) collective-permute-start(bf16[128,1280]{1,0:T(8,128)(2,1)S(1)} %get-tuple-element.34), channel_id=1, source_target_pairs={{0,8},{4,12},{8,0},{12,4},{1,9},{5,13},{9,1},{13,5},{2,10},{6,14},... | collective-permute-start | bytes 983048 | tf_op jit(solution)/shard_map/ppermute | solution.py:335
  35.0 2.8 %collective-permute-start.7 = (bf16[720,128]{1,0:T(8,128)(2,1)S(1)}, bf16[720,128]{1,0:T(8,128)(2,1)S(1)}, u32[]{:S(2)}, u32[]{:S(2)}) collective-permute-start(bf16[720,128]{1,0:T(8,128)(2,1)S(1)} %sort_rows.1.refs_0_), channel_id=1, source_target_pairs={{0,192},{64,0},{128,64},{192,128},{1,193},{65,1},{129,65},{193,129... | collective-permute-start | bytes 552968 | tf_op jit(solution)/shard_map/ppermute | solution.py:336
  37.7 0.8 collective-permute-start.6
  38.5 0.9 collective-permute-start.5
  39.4 3.4 %collective-permute-done.7.refs_6_ = bf16[720,128]{1,0:T(8,128)(2,1)S(1)} collective-permute-done((bf16[720,128]{1,0:T(8,128)(2,1)S(1)}, bf16[720,128]{1,0:T(8,128)(2,1)S(1)}, u32[]{:S(2)}, u32[]{:S(2)}) %collective-permute-start.7) | collective-permute-done | bytes 184352 | tf_op jit(solution)/shard_map/ppermute | solution.py:336
  42.8 2.1 %collective-permute-done.6.refs_4_ = bf16[720,128]{1,0:T(8,128)(2,1)S(1)} collective-permute-done((bf16[720,128]{1,0:T(8,128)(2,1)S(1)}, bf16[720,128]{1,0:T(8,128)(2,1)S(1)}, u32[]{:S(2)}, u32[]{:S(2)}) %collective-permute-start.6) | collective-permute-done | bytes 184352 | tf_op jit(solution)/shard_map/ppermute | solution.py:336
  44.9 1.9 %collective-permute-done.5.refs_2_ = bf16[720,128]{1,0:T(8,128)(2,1)S(1)} collective-permute-done((bf16[720,128]{1,0:T(8,128)(2,1)S(1)}, bf16[720,128]{1,0:T(8,128)(2,1)S(1)}, u32[]{:S(2)}, u32[]{:S(2)}) %collective-permute-start.5) | collective-permute-done | bytes 184352 | tf_op jit(solution)/shard_map/ppermute | solution.py:336
  46.7 4.5 %collective-permute-start.16 = (bf16[128,1280]{1,0:T(8,128)(2,1)S(1)}, bf16[128,1280]{1,0:T(8,128)(2,1)S(1)}, u32[]{:S(2)}, u32[]{:S(2)}) collective-permute-start(bf16[128,1280]{1,0:T(8,128)(2,1)S(1)} %get-tuple-element.48), channel_id=1, source_target_pairs={{0,12},{4,0},{8,4},{12,8},{1,13},{5,1},{9,5},{13,9},{2,14},{6,2},{... | collective-permute-start | bytes 983048 | tf_op jit(solution)/shard_map/ppermute | solution.py:338
  51.3 0.5 collective-permute-start.10
  51.8 0.5 collective-permute-start.11
  52.3 0.4 collective-permute-done.9.refs_1_
  53.2 2.7 %collective-permute-done.16.refs_11_ = bf16[128,1280]{1,0:T(8,128)(2,1)S(1)} collective-permute-done((bf16[128,1280]{1,0:T(8,128)(2,1)S(1)}, bf16[128,1280]{1,0:T(8,128)(2,1)S(1)}, u32[]{:S(2)}, u32[]{:S(2)}) %collective-permute-start.16) | collective-permute-done | bytes 327712 | tf_op jit(solution)/shard_map/ppermute | solution.py:338
  55.9 8.6 %attend.1.c0 = bf16[256,256]{1,0:T(8,128)(2,1)S(1)} custom-call(s32[5]{0:T(128)S(1)} %stack.23.ids, bf16[720,128]{1,0:T(8,128)(2,1)S(1)} %sort_rows.1.refs_0_, bf16[720,128]{1,0:T(8,128)(2,1)S(1)} %collective-permute-done.9.refs_1_, bf16[720,128]{1,0:T(8,128)(2,1)S(1)} %collective-permute-done.5.refs_2_, ...), custom_call_target="tpu_custom_call" | custom-call | flops 1000000000 | bytes 10000000 | tf_op jit(solution)/shard_map/attend/pallas_call | solution.py:343
  64.5 3.8 %collective-permute-start.15 = (bf16[256,256]{1,0:T(8,128)(2,1)S(1)}, bf16[256,256]{1,0:T(8,128)(2,1)S(1)}, u32[]{:S(2)}, u32[]{:S(2)}) collective-permute-start(bf16[256,256]{1,0:T(8,128)(2,1)S(1)} %attend.1.c0), channel_id=1, source_target_pairs={{0,12},{4,0},{8,4},{12,8},{1,13},{5,1},{9,5},{13,9},{2,14},{6,2},{... | collective-permute-start | bytes 393224 | tf_op jit(solution)/shard_map/ppermute | solution.py:362
  68.3 1.0 collective-permute-start.13
  69.2 3.1 %merge_o.1.merged = bf16[4,4,256,320]{3,2,1,0:T(8,128)(2,1)S(1)} custom-call(s32[5]{0:T(128)S(1)} %stack.23.ids, bf16[720,128]{1,0:T(8,128)(2,1)S(1)} %sort_rows.1.refs_0_, bf16[720,128]{1,0:T(8,128)(2,1)S(1)} %collective-permute-done.9.refs_1_, bf16[720,128]{1,0:T(8,128)(2,1)S(1)} %collective-permute-done.5.refs_2_, ...), custom_call_target="tpu_custom_call" | custom-call | flops 340000000 | bytes 8000000 | tf_op jit(solution)/shard_map/merge_o/pallas_call | solution.py:364
  72.3 2.2 %collective-permute-done.15.c3 = bf16[256,256]{1,0:T(8,128)(2,1)S(1)} collective-permute-done((bf16[256,256]{1,0:T(8,128)(2,1)S(1)}, bf16[256,256]{1,0:T(8,128)(2,1)S(1)}, u32[]{:S(2)}, u32[]{:S(2)}) %collective-permute-start.15) | collective-permute-done | bytes 131104 | tf_op jit(solution)/shard_map/ppermute | solution.py:362
  74.5 1.7 %collective-permute-done.14.c2 = bf16[256,256]{1,0:T(8,128)(2,1)S(1)} collective-permute-done((bf16[256,256]{1,0:T(8,128)(2,1)S(1)}, bf16[256,256]{1,0:T(8,128)(2,1)S(1)}, u32[]{:S(2)}, u32[]{:S(2)}) %collective-permute-start.14) | collective-permute-done | bytes 131104 | tf_op jit(solution)/shard_map/ppermute | solution.py:362
  76.2 1.8 %collective-permute-done.13.c1 = bf16[256,256]{1,0:T(8,128)(2,1)S(1)} collective-permute-done((bf16[256,256]{1,0:T(8,128)(2,1)S(1)}, bf16[256,256]{1,0:T(8,128)(2,1)S(1)}, u32[]{:S(2)}, u32[]{:S(2)}) %collective-permute-start.13) | collective-permute-done | bytes 131104 | tf_op jit(solution)/shard_map/ppermute | solution.py:362
  77.9 1.3 %project.1 = bf16[4,640,128]{2,1,0:T(8,128)(2,1)S(1)} custom-call(bf16[256,256]{1,0:T(8,128)(2,1)S(1)} %attend.1.c0, bf16[256,256]{1,0:T(8,128)(2,1)S(1)} %collective-permute-done.13.c1, bf16[256,256]{1,0:T(8,128)(2,1)S(1)} %collective-permute-done.14.c2, bf16[256,256]{1,0:T(8,128)(2,1)S(1)} %collective-permute-done.15.c3, ...), custom_call_target="tpu_custom_call" | custom-call | flops 680000000 | bytes 4000000 | tf_op jit(solution)/shard_map/project/pallas_call | solution.py:373
  79.2 18.5 %all_to_all.10.parts = bf16[4,640,128]{2,1,0:T(8,128)(2,1)S(1)} all-to-all(bf16[4,640,128]{2,1,0:T(8,128)(2,1)S(1)} %project.1), channel_id=1, replica_groups=mesh['x'=4,'zh'=2,'c'=2,'y'=4,'z'=4] {'z'}, dimensions={0} | all-to-all | bytes 1310720 | tf_op jit(solution)/shard_map/all_to_all | solution.py:380
  97.7 0.8 sum_parts.1
  (21 shorter events, 0.6 us)
Async XLA Ops:
  2.9 53.0 %copy-start = (s32[64]{0:T(128)S(1)}, s32[64]{0:T(128)}, u32[]{:S(2)}) copy-start(s32[64]{0:T(128)} %refs_16_.1) | copy-start | bytes 772
  2.9 26.0 %all-to-all-start = ((bf16[32,40,128]{2,1,0:T(8,128)(2,1)}), bf16[32,40,128]{2,1,0:T(8,128)(2,1)S(1)}, u32[]{:S(2)}, u32[]{:S(2)}) async-start(bf16[32,40,128]{2,1,0:T(8,128)(2,1)} %get-tuple-element.27), calls=%async_computation | async-start | bytes 655360 | tf_op jit(solution)/shard_map/all_to_all | solution.py:304
  14.3 14.6 %collective-permute-start = (bf16[128,1280]{1,0:T(8,128)(2,1)S(1)}, bf16[128,1280]{1,0:T(8,128)(2,1)S(1)}, u32[]{:S(2)}, u32[]{:S(2)}) collective-permute-start(bf16[128,1280]{1,0:T(8,128)(2,1)S(1)} %get-tuple-element.29), channel_id=1, source_target_pairs={{0,4},{4,8},{8,12},{12,0},{1,5},{5,9},{9,13},{13,1},{2,6},{6,10},{... | collective-permute-start | bytes 983048 | tf_op jit(solution)/shard_map/ppermute | solution.py:325
  20.8 9.2 %collective-permute-start.4 = (bf16[64,256]{1,0:T(8,128)(2,1)S(1)}, bf16[64,256]{1,0:T(8,128)(2,1)S(1)}, u32[]{:S(2)}, u32[]{:S(2)}) collective-permute-start(bf16[64,256]{1,0:T(8,128)(2,1)S(1)} %get-tuple-element.32), channel_id=1, source_target_pairs={{0,3},{1,0},{2,7},{3,4},{4,11},{5,8},{6,15},{7,12},{8,1},{9,2},{10... | collective-permute-start | bytes 98312 | tf_op jit(solution)/shard_map/ppermute | solution.py:322
  21.4 8.5 %collective-permute-start.3 = (bf16[64,256]{1,0:T(8,128)(2,1)S(1)}, bf16[64,256]{1,0:T(8,128)(2,1)S(1)}, u32[]{:S(2)}, u32[]{:S(2)}) collective-permute-start(bf16[64,256]{1,0:T(8,128)(2,1)S(1)} %get-tuple-element.32), channel_id=1, source_target_pairs={{0,2},{1,3},{2,6},{3,7},{4,10},{5,11},{6,14},{7,15},{8,0},{9,1},{1... | collective-permute-start | bytes 98312 | tf_op jit(solution)/shard_map/ppermute | solution.py:322
  24.7 5.3 %collective-permute-start.2 = (bf16[64,256]{1,0:T(8,128)(2,1)S(1)}, bf16[64,256]{1,0:T(8,128)(2,1)S(1)}, u32[]{:S(2)}, u32[]{:S(2)}) collective-permute-start(bf16[64,256]{1,0:T(8,128)(2,1)S(1)} %get-tuple-element.32), channel_id=1, source_target_pairs={{0,1},{1,2},{2,5},{3,6},{4,9},{5,10},{6,13},{7,14},{8,3},{9,0},{10... | collective-permute-start | bytes 98312 | tf_op jit(solution)/shard_map/ppermute | solution.py:322
  25.8 4.1 %collective-permute-start.1 = (bf16[64,256]{1,0:T(8,128)(2,1)S(1)}, bf16[64,256]{1,0:T(8,128)(2,1)S(1)}, u32[]{:S(2)}, u32[]{:S(2)}) collective-permute-start(bf16[64,256]{1,0:T(8,128)(2,1)S(1)} %get-tuple-element.32), channel_id=1, source_target_pairs={{0,0},{1,1},{2,4},{3,5},{4,8},{5,9},{6,12},{7,13},{8,2},{9,3},{10,... | collective-permute-start | bytes 98312 | tf_op jit(solution)/shard_map/ppermute | solution.py:322
  30.0 16.8 %collective-permute-start.8 = (bf16[128,1280]{1,0:T(8,128)(2,1)S(1)}, bf16[128,1280]{1,0:T(8,128)(2,1)S(1)}, u32[]{:S(2)}, u32[]{:S(2)}) collective-permute-start(bf16[128,1280]{1,0:T(8,128)(2,1)S(1)} %get-tuple-element.34), channel_id=1, source_target_pairs={{0,8},{4,12},{8,0},{12,4},{1,9},{5,13},{9,1},{13,5},{2,10},{6,14},... | collective-permute-start | bytes 983048 | tf_op jit(solution)/shard_map/ppermute | solution.py:335
  35.0 7.8 %collective-permute-start.7 = (bf16[720,128]{1,0:T(8,128)(2,1)S(1)}, bf16[720,128]{1,0:T(8,128)(2,1)S(1)}, u32[]{:S(2)}, u32[]{:S(2)}) collective-permute-start(bf16[720,128]{1,0:T(8,128)(2,1)S(1)} %sort_rows.1.refs_0_), channel_id=1, source_target_pairs={{0,192},{64,0},{128,64},{192,128},{1,193},{65,1},{129,65},{193,129... | collective-permute-start | bytes 552968 | tf_op jit(solution)/shard_map/ppermute | solution.py:336
  37.7 7.1 %collective-permute-start.6 = (bf16[720,128]{1,0:T(8,128)(2,1)S(1)}, bf16[720,128]{1,0:T(8,128)(2,1)S(1)}, u32[]{:S(2)}, u32[]{:S(2)}) collective-permute-start(bf16[720,128]{1,0:T(8,128)(2,1)S(1)} %sort_rows.1.refs_0_), channel_id=1, source_target_pairs={{0,128},{64,192},{128,0},{192,64},{1,129},{65,193},{129,1},{193,65... | collective-permute-start | bytes 552968 | tf_op jit(solution)/shard_map/ppermute | solution.py:336
  38.5 8.2 %collective-permute-start.5 = (bf16[720,128]{1,0:T(8,128)(2,1)S(1)}, bf16[720,128]{1,0:T(8,128)(2,1)S(1)}, u32[]{:S(2)}, u32[]{:S(2)}) collective-permute-start(bf16[720,128]{1,0:T(8,128)(2,1)S(1)} %sort_rows.1.refs_0_), channel_id=1, source_target_pairs={{0,64},{64,128},{128,192},{192,0},{1,65},{65,129},{129,193},{193,1... | collective-permute-start | bytes 552968 | tf_op jit(solution)/shard_map/ppermute | solution.py:336
  46.7 9.1 %collective-permute-start.16 = (bf16[128,1280]{1,0:T(8,128)(2,1)S(1)}, bf16[128,1280]{1,0:T(8,128)(2,1)S(1)}, u32[]{:S(2)}, u32[]{:S(2)}) collective-permute-start(bf16[128,1280]{1,0:T(8,128)(2,1)S(1)} %get-tuple-element.48), channel_id=1, source_target_pairs={{0,12},{4,0},{8,4},{12,8},{1,13},{5,1},{9,5},{13,9},{2,14},{6,2},{... | collective-permute-start | bytes 983048 | tf_op jit(solution)/shard_map/ppermute | solution.py:338
  51.3 1.4 %collective-permute-start.9 = (bf16[720,128]{1,0:T(8,128)(2,1)S(1)}, bf16[720,128]{1,0:T(8,128)(2,1)S(1)}, u32[]{:S(2)}, u32[]{:S(2)}) collective-permute-start(bf16[720,128]{1,0:T(8,128)(2,1)S(1)} %sort_rows.1.refs_0_), channel_id=1, source_target_pairs={{0,16},{16,0},{1,17},{17,1},{2,18},{18,2},{3,19},{19,3},{4,20},{20... | collective-permute-start | bytes 552968 | tf_op jit(solution)/shard_map/ppermute | solution.py:341
  51.3 1.7 %collective-permute-start.10 = (bf16[720,128]{1,0:T(8,128)(2,1)S(1)}, bf16[720,128]{1,0:T(8,128)(2,1)S(1)}, u32[]{:S(2)}, u32[]{:S(2)}) collective-permute-start(bf16[720,128]{1,0:T(8,128)(2,1)S(1)} %collective-permute-done.5.refs_2_), channel_id=1, source_target_pairs={{0,16},{16,0},{1,17},{17,1},{2,18},{18,2},{3,19},{19,3},{4,20},{20... | collective-permute-start | bytes 552968 | tf_op jit(solution)/shard_map/ppermute | solution.py:341
  51.8 16.5 %collective-permute-start.17 = (bf16[128,1280]{1,0:T(8,128)(2,1)S(1)}, bf16[128,1280]{1,0:T(8,128)(2,1)S(1)}, u32[]{:S(2)}, u32[]{:S(2)}) collective-permute-start(bf16[128,1280]{1,0:T(8,128)(2,1)S(1)} %collective-permute-done.refs_9_), channel_id=1, source_target_pairs={{0,16},{16,0},{1,17},{17,1},{2,18},{18,2},{3,19},{19,3},{4,20},{20... | collective-permute-start | bytes 983048 | tf_op jit(solution)/shard_map/ppermute | solution.py:363
  51.8 4.1 %collective-permute-start.11 = (bf16[720,128]{1,0:T(8,128)(2,1)S(1)}, bf16[720,128]{1,0:T(8,128)(2,1)S(1)}, u32[]{:S(2)}, u32[]{:S(2)}) collective-permute-start(bf16[720,128]{1,0:T(8,128)(2,1)S(1)} %collective-permute-done.6.refs_4_), channel_id=1, source_target_pairs={{0,16},{16,0},{1,17},{17,1},{2,18},{18,2},{3,19},{19,3},{4,20},{20... | collective-permute-start | bytes 552968 | tf_op jit(solution)/shard_map/ppermute | solution.py:341
  52.7 3.2 %collective-permute-start.12 = (bf16[720,128]{1,0:T(8,128)(2,1)S(1)}, bf16[720,128]{1,0:T(8,128)(2,1)S(1)}, u32[]{:S(2)}, u32[]{:S(2)}) collective-permute-start(bf16[720,128]{1,0:T(8,128)(2,1)S(1)} %collective-permute-done.7.refs_6_), channel_id=1, source_target_pairs={{0,16},{16,0},{1,17},{17,1},{2,18},{18,2},{3,19},{19,3},{4,20},{20... | collective-permute-start | bytes 552968 | tf_op jit(solution)/shard_map/ppermute | solution.py:341
  52.9 16.3 %collective-permute-start.18 = (bf16[128,1280]{1,0:T(8,128)(2,1)S(1)}, bf16[128,1280]{1,0:T(8,128)(2,1)S(1)}, u32[]{:S(2)}, u32[]{:S(2)}) collective-permute-start(bf16[128,1280]{1,0:T(8,128)(2,1)S(1)} %collective-permute-done.8.refs_10_), channel_id=1, source_target_pairs={{0,16},{16,0},{1,17},{17,1},{2,18},{18,2},{3,19},{19,3},{4,20},{20... | collective-permute-start | bytes 983048 | tf_op jit(solution)/shard_map/ppermute | solution.py:363
  55.8 13.4 %collective-permute-start.19 = (bf16[128,1280]{1,0:T(8,128)(2,1)S(1)}, bf16[128,1280]{1,0:T(8,128)(2,1)S(1)}, u32[]{:S(2)}, u32[]{:S(2)}) collective-permute-start(bf16[128,1280]{1,0:T(8,128)(2,1)S(1)} %collective-permute-done.16.refs_11_), channel_id=1, source_target_pairs={{0,16},{16,0},{1,17},{17,1},{2,18},{18,2},{3,19},{19,3},{4,20},{20... | collective-permute-start | bytes 983048 | tf_op jit(solution)/shard_map/ppermute | solution.py:363
  64.5 10.0 %collective-permute-start.15 = (bf16[256,256]{1,0:T(8,128)(2,1)S(1)}, bf16[256,256]{1,0:T(8,128)(2,1)S(1)}, u32[]{:S(2)}, u32[]{:S(2)}) collective-permute-start(bf16[256,256]{1,0:T(8,128)(2,1)S(1)} %attend.1.c0), channel_id=1, source_target_pairs={{0,12},{4,0},{8,4},{12,8},{1,13},{5,1},{9,5},{13,9},{2,14},{6,2},{... | collective-permute-start | bytes 393224 | tf_op jit(solution)/shard_map/ppermute | solution.py:362
  68.3 7.9 %collective-permute-start.14 = (bf16[256,256]{1,0:T(8,128)(2,1)S(1)}, bf16[256,256]{1,0:T(8,128)(2,1)S(1)}, u32[]{:S(2)}, u32[]{:S(2)}) collective-permute-start(bf16[256,256]{1,0:T(8,128)(2,1)S(1)} %attend.1.c0), channel_id=1, source_target_pairs={{0,8},{4,12},{8,0},{12,4},{1,9},{5,13},{9,1},{13,5},{2,10},{6,14},... | collective-permute-start | bytes 393224 | tf_op jit(solution)/shard_map/ppermute | solution.py:362
  68.3 9.6 %collective-permute-start.13 = (bf16[256,256]{1,0:T(8,128)(2,1)S(1)}, bf16[256,256]{1,0:T(8,128)(2,1)S(1)}, u32[]{:S(2)}, u32[]{:S(2)}) collective-permute-start(bf16[256,256]{1,0:T(8,128)(2,1)S(1)} %attend.1.c0), channel_id=1, source_target_pairs={{0,4},{4,8},{8,12},{12,0},{1,5},{5,9},{9,13},{13,1},{2,6},{6,10},{... | collective-permute-start | bytes 393224 | tf_op jit(solution)/shard_map/ppermute | solution.py:362

commit v3 on v2

v3 whole, which is shorter than its diff:
```python
import jax
import jax.numpy as jnp
import numpy as np
from jax import lax
from jax.experimental import pallas as pl
from jax.experimental.pallas import tpu as pltpu
from jax.sharding import Mesh
from jax.sharding import PartitionSpec as P

HD = 128
STEPS = 4
ROWS = 256
WIDTH = 5120
NX, NZH, NC, NY, NZ = 4, 2, 2, 4, 4
GROUP = ("x", "zh", "c")
TP = ("y", "z")
BF = jnp.bfloat16
F32 = jnp.float32
MSG = 40
XROWS = 720

SMEM = pl.BlockSpec(memory_space=pltpu.SMEM)


def params(mib):
    return pltpu.CompilerParams(vmem_limit_bytes=mib * 1024 * 1024)


def mm(a, b):
    return jnp.dot(a, b, preferred_element_type=F32)


def mm_t(a, b):
    return lax.dot_general(a, b, (((1,), (1,)), ((), ())), preferred_element_type=F32)


def pack_kernel(low, up, q_up, o_low, out, low_v, up_v, qu_v, ol_v, sems):
    copies = [
        pltpu.make_async_copy(a, b, sems.at[n])
        for n, (a, b) in enumerate(((low, low_v), (up, up_v), (q_up, qu_v), (o_low, ol_v)))
    ]
    for copy in copies:
        copy.start()
    for copy in copies:
        copy.wait()

    def halves(ref):
        a = ref[...].astype(F32)
        return [a[:, :128], a[:, 128:]]

    first = jnp.concatenate([low_v[...].astype(F32), up_v[...].astype(F32)], axis=1)
    rows = [first, jnp.zeros((4, 128), F32)] + halves(qu_v) + halves(ol_v)
    message = jnp.concatenate(rows, axis=0).astype(BF)

    def write(i, carry):
        out[i] = message
        return carry

    lax.fori_loop(0, out.shape[0], write, 0)


def norm_kernel(ids, states, wkv_t, wo, blocks, kv_t, w1, w2, w3, x_v, w_v, flat, out_v, cut, sems):
    c, y = ids[2], ids[3]
    half = pl.ds(pl.multiple_of(c * 128, 128), 128)
    loads = [pltpu.make_async_copy(states.at[n], x_v.at[n], sems.at[n]) for n in range(STEPS)]
    loads.append(pltpu.make_async_copy(wkv_t, w_v, sems.at[STEPS]))
    cuts, puts = [], []
    for n, ref in enumerate((w1, w2, w3)):
        at = pl.multiple_of(((y + n + 1) & 3) * 1280, 1280)
        cuts.append(pltpu.make_async_copy(wo.at[half, pl.ds(at, 1280)], cut.at[n], sems.at[5 + n]))
        puts.append(pltpu.make_async_copy(cut.at[n], ref, sems.at[8 + n]))
    for copy in loads + cuts:
        copy.start()
    for n in range(STEPS):
        loads[n].wait()

        def rows(i, carry):
            r = pl.multiple_of(i * 32, 32)
            x = x_v[n, pl.ds(r, 32), :].astype(F32)
            scale = lax.rsqrt(jnp.mean(x * x, axis=1, keepdims=True) + 1e-06)
            normed = (x * scale).astype(BF)
            to = pl.ds(pl.multiple_of(n * 64 + r, 32), 32)
            flat[to, :] = normed
            for xc in range(8):
                g = (xc // 2) * 4 + xc % 2
                out_v[xc, to, :] = jnp.concatenate(
                    [normed[:, g * 320 : g * 320 + 320], normed[:, g * 320 + 640 : g * 320 + 960]], axis=1
                )
            return carry

        lax.fori_loop(0, 2, rows, 0)
    for cut_copy, put in zip(cuts, puts):
        cut_copy.wait()
        put.start()
    store = pltpu.make_async_copy(out_v, blocks, sems.at[11])
    store.start()
    loads[STEPS].wait()
    kv_t[...] = mm_t(flat[...], w_v[...]).T.astype(BF)
    for copy in puts + [store]:
        copy.wait()


def sort_kernel(ids, got, out):
    i = lax.broadcasted_iota(jnp.int32, (80, MSG), 0)
    j = lax.broadcasted_iota(jnp.int32, (80, MSG), 1)
    picks = [jnp.where((j == i - 20 * p) & (j < 20), 1.0, 0.0).astype(BF) for p in range(4)]
    for q in range(8):
        rows = mm(picks[0], got[4 * q])
        for p in range(1, 4):
            rows = rows + mm(picks[p], got[4 * q + p])
        out[80 * q : 80 * q + 80, :] = rows.astype(BF)
    y, z = ids[3], ids[4]
    own = [got[zh * 16 + y * NZ + z].astype(F32)[24:32] for zh in range(2)]
    out[640:656, :] = jnp.concatenate(own, axis=0).astype(BF)
    for yy in range(NY):
        part = [got[zh * 16 + yy * NZ + z].astype(F32)[32:40] for zh in range(2)]
        out[656 + 16 * yy : 672 + 16 * yy, :] = jnp.concatenate(part, axis=0).astype(BF)


def rank_order(ids, half, first):
    r = lax.broadcasted_iota(jnp.int32, (128, 128), 0)
    j = lax.broadcasted_iota(jnp.int32, (128, 128), 1)
    x, c = ids[0], ids[2]
    k, o = (j >> 5) & 3, (j >> 4) & 1
    zh, h, i = (j >> 3) & 1, (j >> 2) & 1, j & 3
    xs = x ^ k
    rank = (xs * 4 + zh * 2 + (c + o - 2 * c * o)) * 4 + i
    return jnp.where((h == half) & (r == rank + first), 1.0, 0.0).astype(BF)


def attend_kernel(ids, *refs):
    blocks = refs[:8]
    wq, normed_h, kc_h, vc_h = refs[8:12]
    pieces, lens, ctx = refs[12:16], refs[16], refs[17]
    kv, qs, cs, normed, kc, vc, sems = refs[18:]
    x, c, y, z = ids[0], ids[2], ids[3], ids[4]
    loads = [
        pltpu.make_async_copy(kc_h.at[:, y], kc, sems.at[0]),
        pltpu.make_async_copy(vc_h.at[:, y], vc, sems.at[1]),
    ]
    ats = [(x ^ (n // 2)) * 2 + c + n % 2 - 2 * c * (n % 2) for n in range(8)]
    steps = [pltpu.make_async_copy(normed_h.at[at], normed.at[n], sems.at[2 + n]) for n, at in enumerate(ats)]
    for copy in steps + loads:
        copy.start()
    stack = jnp.concatenate([b[640:656, :] for b in blocks], axis=0)
    upper = jnp.concatenate(
        [2.0 * mm(rank_order(ids, h, 0), stack) for h in range(2)], axis=1
    ).astype(BF)
    total = jnp.zeros((ROWS, 256), F32)
    for n in range(8):
        rank = mm(blocks[n][0:640, :], upper)
        at = ats[n]
        row = pl.multiple_of((at >> 1) * 1280 + (at & 1) * 320, 320)
        base = jnp.concatenate([wq[pl.ds(row, 320), :], wq[pl.ds(row + 640, 320), :]], axis=0)
        merged = (base.astype(F32) + rank).astype(BF)
        steps[n].wait()
        total = total + mm(normed[n], merged)
    qs[...] = total.astype(BF).astype(F32)
    for k, ref in enumerate(pieces):
        kv[(z ^ k) & 3] = ref[...]
    key_t = kv[0:2].reshape(128, 256)
    val = kv[2:4].reshape(128, 256).astype(F32).T.astype(BF)
    for copy in loads:
        copy.wait()
    factor = 1.0 / HD**0.5
    c8 = lax.broadcasted_iota(jnp.int32, (8, 512), 1)
    r8 = lax.broadcasted_iota(jnp.int32, (8, 512), 0)
    own_cached = (c8 >> 6) == r8
    pos = c8 & 63
    cn = lax.broadcasted_iota(jnp.int32, (64, 256), 1)
    rn = lax.broadcasted_iota(jnp.int32, (64, 256), 0)
    seen = (cn >> 6) <= (rn >> 4)

    def batch(b, carry):
        r = pl.multiple_of(b * 8, 8)
        q = jnp.concatenate(
            [qs[pl.ds(s * 64 + r, 8), h * 128 : h * 128 + 128] for s in range(4) for h in range(2)], axis=0
        ).astype(BF)
        keys = kc[pl.ds(r, 8)].reshape(512, 128)
        vals = vc[pl.ds(r, 8)].reshape(512, 128)
        length = jnp.zeros((8, 512), jnp.int32)
        for i in range(8):
            length = jnp.where(r8 == i, lens[r + i], length)
        ok = jnp.where(own_cached & (pos < length), 1.0, 0.0)
        okc = jnp.concatenate([ok] * 8, axis=0) > 0.5
        okn = seen & ((cn & 63) == (rn & 7) + r)
        sc = jnp.where(okc, mm_t(q, keys) * factor, -1e30)
        sn = jnp.where(okn, mm(q, key_t) * factor, -1e30)
        top = jnp.maximum(jnp.max(sc, axis=1, keepdims=True), jnp.max(sn, axis=1, keepdims=True))
        ec, en = jnp.exp(sc - top), jnp.exp(sn - top)
        total = jnp.sum(ec, axis=1, keepdims=True) + jnp.sum(en, axis=1, keepdims=True)
        inverse = 1.0 / total
        pc, pn = (ec * inverse).astype(BF), (en * inverse).astype(BF)
        out = mm(pc, vals) + mm(pn, val)
        for s in range(4):
            for h in range(2):
                n = (s * 2 + h) * 8
                cs[pl.ds(s * 64 + r, 8), h * 128 : h * 128 + 128] = out[n : n + 8]
        return carry

    lax.fori_loop(0, 8, batch, 0, unroll=4)
    ctx[...] = cs[...].astype(BF)


def merge_o_kernel(ids, *refs):
    blocks = refs[:8]
    wo = refs[8]
    same, other = refs[9:12], refs[12:15]
    out, hold, low, own, sem = refs[15:]
    x, c, y = ids[0], ids[2], ids[3]
    load = pltpu.make_async_copy(wo.at[:, pl.ds(pl.multiple_of(y * 1280, 1280), 1280)], own, sem)
    load.start()
    ks = x ^ y
    for k in range(4):
        for o in range(2):

            @pl.when(ks == k)
            def _():
                hold[o] = blocks[2 * k + o][0:640, :]

    order = [rank_order(ids, h, 64) for h in range(2)]
    for k in (1, 2, 3, 0):
        if k == 0:
            load.wait()
        yy = (y - k + 4) & 3
        at = pl.multiple_of(656 + 16 * yy, 16)
        stack = jnp.concatenate([b[pl.ds(at, 16), :] for b in blocks], axis=0)
        lower = jnp.concatenate([2.0 * mm(order[h], stack) for h in range(2)], axis=1)
        low[...] = lower.T.astype(BF)
        for zz in range(4):
            zh, cc = zz // 2, zz % 2
            o = c + cc - 2 * c * cc
            u = hold[o, zh * 320 : zh * 320 + 320, :]
            cols = slice(zz * 320, zz * 320 + 320)
            if k == 0:
                out[k, zz] = (own[:, cols].astype(F32) + mm_t(low[...], u)).astype(BF)
            else:
                for ref, core in ((same[k - 1], c), (other[k - 1], 1 - c)):
                    at = pl.ds(pl.multiple_of(core * 128, 128), 128)
                    out[k, zz, at] = (ref[:, cols].astype(F32) + mm_t(low[at, :], u)).astype(BF)


def project_kernel(ids, c0, c1, c2, c3, merged, *out):
    for n in (3, 2, 1, 0):
        zz = ids[4] ^ n
        total = mm(c0[...], merged[0, zz])
        for k, ref in ((1, c1), (2, c2), (3, c3)):
            total = total + mm(ref[...], merged[k, zz])
        total = total.astype(BF)
        out[n][0:256] = total[:, 0:128]
        out[n][256:512] = total[:, 128:256]
        out[n][512:640] = jnp.concatenate([total[0:128, 256:320], total[128:256, 256:320]], axis=1)


def sum_kernel(p0, p1, p2, p3, out):
    total = p0[...].astype(F32) + p1[...].astype(F32) + p2[...].astype(F32) + p3[...].astype(F32)
    tail = jnp.concatenate([total[512:640, :64], total[512:640, 64:]], axis=0)
    full = jnp.concatenate([total[0:256], total[256:512], tail], axis=1).astype(BF)
    out[...] = full.reshape(out.shape)


def near(a):
    return pltpu.with_memory_space_constraint(a, pltpu.VMEM)


def far(a):
    return pltpu.with_memory_space_constraint(a, pltpu.HBM)


def ring(s):
    return [(i, (i + s) % 4) for i in range(4)]


def partner(s):
    return [(i, i ^ s) for i in range(4)]


def kv_pairs(k):
    pairs = []
    for s in range(16):
        a, e, b = s // 4, (s % 4) // 2, s % 2
        pairs.append((s, (2 * (a % 2) + e) * 4 + (((a // 2) * 2 + b) ^ k)))
    return pairs


def local(states, wq, wkv, wo, qa_low, qa_up, oa_low, oa_up, kcache, vcache, lens):
    x, zh, c, y, z = (lax.axis_index(a) for a in ("x", "zh", "c", "y", "z"))
    ids = jnp.stack([x, zh, c, y, z]).astype(jnp.int32)

    vmem = pl.BlockSpec(memory_space=pltpu.VMEM)
    hbm = pl.BlockSpec(memory_space=pltpu.HBM)

    def array(*shape):
        return jax.ShapeDtypeStruct(shape, BF)

    messages = pl.pallas_call(
        pack_kernel,
        out_shape=array(32, MSG, 128),
        in_specs=[hbm] * 4,
        scratch_shapes=[
            pltpu.VMEM((20, 64), BF),
            pltpu.VMEM((20, 64), BF),
            pltpu.VMEM((4, 256), BF),
            pltpu.VMEM((4, 256), BF),
            pltpu.SemaphoreType.DMA((4,)),
        ],
        compiler_params=params(4),
        name="pack",
    )(*(far(a) for a in (qa_low, oa_up, qa_up, oa_low)))
    got = lax.all_to_all(messages, ("zh", "y", "z"), 0, 0, tiled=True)

    normed, kv_t, *w_sent = pl.pallas_call(
        norm_kernel,
        out_shape=(pltpu.HBM((8, ROWS, 640), BF), array(64, ROWS)) + (pltpu.HBM((128, 1280), BF),) * 3,
        in_specs=[SMEM, hbm, hbm, hbm],
        out_specs=(hbm, vmem, hbm, hbm, hbm),
        scratch_shapes=[
            pltpu.VMEM((STEPS, 64, WIDTH), BF),
            pltpu.VMEM((64, WIDTH), BF),
            pltpu.VMEM((ROWS, WIDTH), BF),
            pltpu.VMEM((8, ROWS, 640), BF),
            pltpu.VMEM((3, 128, 1280), BF),
            pltpu.SemaphoreType.DMA((12,)),
        ],
        compiler_params=params(20),
        cost_estimate=pl.CostEstimate(flops=170_000_000, bytes_accessed=8_000_000, transcendentals=0),
        name="norm_kv",
    )(ids, far(states), far(wkv.T), far(wo))
    new_kv = [lax.ppermute(kv_t, TP, kv_pairs(k)) for k in range(4)]

    swap = [(0, 1), (1, 0)]
    got, normed, kv_t = lax.optimization_barrier((got, normed, kv_t))
    mine = pl.pallas_call(
        sort_kernel,
        out_shape=array(XROWS, 128),
        in_specs=[SMEM, vmem],
        compiler_params=params(6),
        name="sort_rows",
    )(ids, got)
    mine, w_sent, new_kv = lax.optimization_barrier((mine, w_sent, new_kv))
    w_first = lax.ppermute(w_sent[0], "y", ring(1))
    w_third = lax.ppermute(w_sent[2], "y", ring(3))
    parts = [mine] + [lax.ppermute(mine, "x", partner(s)) for s in (1, 2, 3)]
    w_first, w_third, w_second = lax.optimization_barrier((w_first, w_third, w_sent[1]))
    w_same = [w_first, lax.ppermute(w_second, "y", ring(2)), w_third]
    blocks = []
    for part in parts:
        blocks += [part, lax.ppermute(part, "c", swap)]

    ctx = pl.pallas_call(
        attend_kernel,
        out_shape=array(ROWS, 256),
        in_specs=[SMEM] + [vmem] * 9 + [hbm] * 3 + [vmem] * 4 + [SMEM],
        scratch_shapes=[
            pltpu.VMEM((4, 64, 256), BF),
            pltpu.VMEM((ROWS, 256), F32),
            pltpu.VMEM((ROWS, 256), F32),
            pltpu.VMEM((8, ROWS, 640), BF),
            pltpu.VMEM((64, 64, 128), BF),
            pltpu.VMEM((64, 64, 128), BF),
            pltpu.SemaphoreType.DMA((10,)),
        ],
        compiler_params=params(24),
        cost_estimate=pl.CostEstimate(flops=1_000_000_000, bytes_accessed=10_000_000, transcendentals=400_000),
        name="attend",
    )(ids, *blocks, near(wq), far(normed), far(kcache), far(vcache), *new_kv, lens)

    others = {s: lax.ppermute(ctx, "y", ring(s)) for s in (1, 3, 2)}
    _, w_same = lax.optimization_barrier((ctx, w_same))
    w_other = [lax.ppermute(w, "c", swap) for w in w_same]
    merged = pl.pallas_call(
        merge_o_kernel,
        out_shape=array(4, 4, 256, 320),
        in_specs=[SMEM] + [vmem] * 8 + [hbm] + [vmem] * 6,
        scratch_shapes=[
            pltpu.VMEM((2, 640, 128), BF),
            pltpu.VMEM((256, 128), BF),
            pltpu.VMEM((256, 1280), BF),
            pltpu.SemaphoreType.DMA(()),
        ],
        compiler_params=params(20),
        cost_estimate=pl.CostEstimate(flops=340_000_000, bytes_accessed=8_000_000, transcendentals=0),
        name="merge_o",
    )(ids, *blocks, far(wo), *w_same, *w_other)
    sums = pl.pallas_call(
        project_kernel,
        out_shape=(array(640, 128),) * 4,
        in_specs=[SMEM] + [vmem] * 5,
        compiler_params=params(16),
        cost_estimate=pl.CostEstimate(flops=680_000_000, bytes_accessed=4_000_000, transcendentals=0),
        name="project",
    )(ids, ctx, others[1], others[2], others[3], merged)
    came = [lax.ppermute(sums[n], "z", partner(n)) for n in (3, 2, 1)]
    return pl.pallas_call(
        sum_kernel,
        out_shape=array(4, 64, 320),
        compiler_params=params(6),
        name="sum_parts",
    )(sums[0], *came)


def solution(mesh):
    fine = Mesh(np.asarray(mesh.devices).reshape(NX, NZH, NC, NY, NZ), GROUP + TP)
    every = GROUP + TP
    in_specs = (
        P(None, GROUP, None),
        P(None, TP),
        P(None, TP),
        P(TP, None),
        P(every, None),
        P(GROUP, TP),
        P(GROUP, TP),
        P(every, None),
        P(GROUP, None, None, None),
        P(GROUP, None, None, None),
        P(GROUP),
    )
    out_specs = P(None, GROUP, TP)
    return jax.shard_map(local, mesh=fine, in_specs=in_specs, out_specs=out_specs, check_vma=False)
```

time: 100 us -> 87 us (0.87)
  the two profiles are of different devices: /device:TPU:32 before, /device:TPU:2 now
where the time goes in v3:
time: 87 us; the launch traced here: 86.7 us
  starting transfers between devices  40.8 us (47%)
  waiting for transfers between devices  23.1 us (27%)
  Pallas kernels  22.6 us (26%)
    ppermute x3, waiting for transfers between devices, local(): came = [lax.ppermute(sums[n], 'z', partner(n)) for n in (3, 2, 1)]  12.4 us
    ppermute x4, starting transfers between devices, local(): new_kv = [lax.ppermute(kv_t, TP, kv_pairs(k)) for k in range(4)]  11.8 us
    all_to_all x1, starting transfers between devices, local(): got = lax.all_to_all(messages, ('zh', 'y', 'z'), 0, 0, tiled=True)  11.5 us
    pallas_call x1, Pallas kernels, local(): pl.pallas_call(attend_kernel, out_shape=array(ROWS, 256), in_specs=[SMEM]...  7.58 us
    pallas_call x1, Pallas kernels, local(): pl.pallas_call(norm_kernel, out_shape=(pltpu.HBM((8, ROWS, 640), BF), arr...  6.09 us
    ppermute x3, starting transfers between devices, local(): others = {s: lax.ppermute(ctx, 'y', ring(s)) for s in (1, 3, 2)}  4.94 us
    ppermute x3, starting transfers between devices, local(): came = [lax.ppermute(sums[n], 'z', partner(n)) for n in (3, 2, 1)]  4.47 us
    pallas_call x1, Pallas kernels, local(): pl.pallas_call(merge_o_kernel, out_shape=array(4, 4, 256, 320), in_specs=...  3.5 us
  transfers between devices with their start and end apart: 24, of which 9 were waited for; matrix products, arithmetic and copies ran while one was open for 0% of the time, Pallas kernels for 21%

profile of v3, /device:TPU:2, one launch (start us, length us, event | category | flops | bytes accessed | tf_op | source)
XLA Modules:
  0.0 86.7 jit_solution(18327145695364826095)
XLA Ops:
  0.0 1.7 %pack.1 = bf16[32,40,128]{2,1,0:T(8,128)(2,1)} custom-call(bf16[20,64]{1,0:T(8,128)(2,1)} %low.1, bf16[20,64]{1,0:T(8,128)(2,1)} %up.1, bf16[4,256]{1,0:T(4,128)(2,1)} %q_up.1, bf16[4,256]{1,0:T(4,128)(2,1)} %o_low.1), custom_call_target="tpu_custom_call" | custom-call | tf_op jit(solution)/shard_map/pack/pallas_call | solution.py:296
  1.8 11.5 %all-to-all-start = ((bf16[32,40,128]{2,1,0:T(8,128)(2,1)}), bf16[32,40,128]{2,1,0:T(8,128)(2,1)S(1)}, u32[]{:S(2)}, u32[]{:S(2)}) async-start(bf16[32,40,128]{2,1,0:T(8,128)(2,1)} %pack.1), calls=%async_computation | async-start | bytes 655360 | tf_op jit(solution)/shard_map/all_to_all | solution.py:310
  13.4 6.1 %norm_kv.1 = (bf16[8,256,640]{2,1,0:T(8,128)(2,1)}, bf16[64,256]{1,0:T(8,128)(2,1)S(1)}, bf16[128,1280]{1,0:T(8,128)(2,1)}, bf16[128,1280]{1,0:T(8,128)(2,1)}, bf16[128,1280]{1,0:T(8,128)(2,1)}) custom-call(s32[5]{0:T(128)S(1)} %stack.23.ids, bf16[4,64,5120]{2,1,0:T(8,128)(2,1)} %states.1, bf16[64,5120]{1,0:T(8,128)(2,1)} %bitcast.6, bf16[256,5120]{1,0:T(8,128)(2,1)} %refs_8_.3), custom_call_target="tpu_custom_call" | custom-call | flops 170000000 | bytes 8000000 | tf_op jit(solution)/shard_map/norm_kv/pallas_call | solution.py:312
  19.5 0.7 collective-permute-start
  20.1 1.9 %collective-permute-start.1 = (bf16[64,256]{1,0:T(8,128)(2,1)S(1)}, bf16[64,256]{1,0:T(8,128)(2,1)S(1)}, u32[]{:S(2)}, u32[]{:S(2)}) collective-permute-start(bf16[64,256]{1,0:T(8,128)(2,1)S(1)} %get-tuple-element.31), channel_id=1, source_target_pairs={{0,1},{1,0},{2,5},{3,4},{4,9},{5,8},{6,13},{7,12},{8,3},{9,2},{10,... | collective-permute-start | bytes 98312 | tf_op jit(solution)/shard_map/ppermute | solution.py:329
  22.0 5.1 %collective-permute-start.2 = (bf16[64,256]{1,0:T(8,128)(2,1)S(1)}, bf16[64,256]{1,0:T(8,128)(2,1)S(1)}, u32[]{:S(2)}, u32[]{:S(2)}) collective-permute-start(bf16[64,256]{1,0:T(8,128)(2,1)S(1)} %get-tuple-element.31), channel_id=1, source_target_pairs={{0,2},{1,3},{2,6},{3,7},{4,10},{5,11},{6,14},{7,15},{8,0},{9,1},{1... | collective-permute-start | bytes 98312 | tf_op jit(solution)/shard_map/ppermute | solution.py:329
  27.1 4.2 %collective-permute-start.3 = (bf16[64,256]{1,0:T(8,128)(2,1)S(1)}, bf16[64,256]{1,0:T(8,128)(2,1)S(1)}, u32[]{:S(2)}, u32[]{:S(2)}) collective-permute-start(bf16[64,256]{1,0:T(8,128)(2,1)S(1)} %get-tuple-element.31), channel_id=1, source_target_pairs={{0,3},{1,2},{2,7},{3,6},{4,11},{5,10},{6,15},{7,14},{8,1},{9,0},{1... | collective-permute-start | bytes 98312 | tf_op jit(solution)/shard_map/ppermute | solution.py:329
  31.2 1.0 %sort_rows.1.refs_0_ = bf16[720,128]{1,0:T(8,128)(2,1)S(1)} custom-call(s32[5]{0:T(128)S(1)} %stack.23.ids, bf16[32,40,128]{2,1,0:T(8,128)(2,1)S(1)} %all-to-all-done.got), custom_call_target="tpu_custom_call" | custom-call | tf_op jit(solution)/shard_map/sort_rows/pallas_call | solution.py:333
  32.3 1.1 %collective-permute-done.3.refs_15_ = bf16[64,256]{1,0:T(8,128)(2,1)S(1)} collective-permute-done((bf16[64,256]{1,0:T(8,128)(2,1)S(1)}, bf16[64,256]{1,0:T(8,128)(2,1)S(1)}, u32[]{:S(2)}, u32[]{:S(2)}) %collective-permute-start.3) | collective-permute-done | bytes 32800 | tf_op jit(solution)/shard_map/ppermute | solution.py:329
  33.4 3.3 %collective-permute-start.14 = (bf16[128,1280]{1,0:T(8,128)(2,1)}, bf16[128,1280]{1,0:T(8,128)(2,1)S(1)}, u32[]{:S(2)}, u32[]{:S(2)}) collective-permute-start(bf16[128,1280]{1,0:T(8,128)(2,1)} %get-tuple-element.42), channel_id=1, source_target_pairs={{0,4},{4,8},{8,12},{12,0},{1,5},{5,9},{9,13},{13,1},{2,6},{6,10},{... | collective-permute-start | bytes 983048 | tf_op jit(solution)/shard_map/ppermute | solution.py:341
  36.7 1.5 %collective-permute-start.9 = (bf16[720,128]{1,0:T(8,128)(2,1)S(1)}, bf16[720,128]{1,0:T(8,128)(2,1)S(1)}, u32[]{:S(2)}, u32[]{:S(2)}) collective-permute-start(bf16[720,128]{1,0:T(8,128)(2,1)S(1)} %sort_rows.1.refs_0_), channel_id=1, source_target_pairs={{0,192},{64,128},{128,64},{192,0},{1,193},{65,129},{129,65},{193,1... | collective-permute-start | bytes 552968 | tf_op jit(solution)/shard_map/ppermute | solution.py:343
  38.2 1.8 %collective-permute-start.5 = (bf16[720,128]{1,0:T(8,128)(2,1)S(1)}, bf16[720,128]{1,0:T(8,128)(2,1)S(1)}, u32[]{:S(2)}, u32[]{:S(2)}) collective-permute-start(bf16[720,128]{1,0:T(8,128)(2,1)S(1)} %sort_rows.1.refs_0_), channel_id=1, source_target_pairs={{0,64},{64,0},{128,192},{192,128},{1,65},{65,1},{129,193},{193,129... | collective-permute-start | bytes 552968 | tf_op jit(solution)/shard_map/ppermute | solution.py:343
  40.1 1.7 %collective-permute-done.14.refs_9_ = bf16[128,1280]{1,0:T(8,128)(2,1)S(1)} collective-permute-done((bf16[128,1280]{1,0:T(8,128)(2,1)}, bf16[128,1280]{1,0:T(8,128)(2,1)S(1)}, u32[]{:S(2)}, u32[]{:S(2)}) %collective-permute-start.14) | collective-permute-done | bytes 327712 | tf_op jit(solution)/shard_map/ppermute | solution.py:341
  41.9 3.0 %collective-permute-done.15.refs_11_ = bf16[128,1280]{1,0:T(8,128)(2,1)S(1)} collective-permute-done((bf16[128,1280]{1,0:T(8,128)(2,1)}, bf16[128,1280]{1,0:T(8,128)(2,1)S(1)}, u32[]{:S(2)}, u32[]{:S(2)}) %collective-permute-start.15) | collective-permute-done | bytes 327712 | tf_op jit(solution)/shard_map/ppermute | solution.py:342
  44.9 0.5 collective-permute-start.10
  45.5 1.5 %collective-permute-done.7.refs_4_ = bf16[720,128]{1,0:T(8,128)(2,1)S(1)} collective-permute-done((bf16[720,128]{1,0:T(8,128)(2,1)S(1)}, bf16[720,128]{1,0:T(8,128)(2,1)S(1)}, u32[]{:S(2)}, u32[]{:S(2)}) %collective-permute-start.7) | collective-permute-done | bytes 184352 | tf_op jit(solution)/shard_map/ppermute | solution.py:343
  47.0 1.4 %collective-permute-done.8.refs_5_ = bf16[720,128]{1,0:T(8,128)(2,1)S(1)} collective-permute-done((bf16[720,128]{1,0:T(8,128)(2,1)S(1)}, bf16[720,128]{1,0:T(8,128)(2,1)S(1)}, u32[]{:S(2)}, u32[]{:S(2)}) %collective-permute-start.8) | collective-permute-done | bytes 184352 | tf_op jit(solution)/shard_map/ppermute | solution.py:348
  48.4 7.6 %attend.1.c0 = bf16[256,256]{1,0:T(8,128)(2,1)S(1)} custom-call(s32[5]{0:T(128)S(1)} %stack.23.ids, bf16[720,128]{1,0:T(8,128)(2,1)S(1)} %sort_rows.1.refs_0_, bf16[720,128]{1,0:T(8,128)(2,1)S(1)} %collective-permute-done.4.refs_1_, bf16[720,128]{1,0:T(8,128)(2,1)S(1)} %collective-permute-done.5.refs_2_, ...), custom_call_target="tpu_custom_call" | custom-call | flops 1000000000 | bytes 10000000 | tf_op jit(solution)/shard_map/attend/pallas_call | solution.py:350
  56.0 0.2 collective-permute-start.17
  56.3 0.4 collective-permute-start.18
  56.8 2.0 %collective-permute-start.11 = (bf16[256,256]{1,0:T(8,128)(2,1)S(1)}, bf16[256,256]{1,0:T(8,128)(2,1)S(1)}, u32[]{:S(2)}, u32[]{:S(2)}) collective-permute-start(bf16[256,256]{1,0:T(8,128)(2,1)S(1)} %attend.1.c0), channel_id=1, source_target_pairs={{0,4},{4,8},{8,12},{12,0},{1,5},{5,9},{9,13},{13,1},{2,6},{6,10},{... | collective-permute-start | bytes 393224 | tf_op jit(solution)/shard_map/ppermute | solution.py:368
  58.8 0.6 collective-permute-start.12
  59.4 2.3 %collective-permute-start.13 = (bf16[256,256]{1,0:T(8,128)(2,1)S(1)}, bf16[256,256]{1,0:T(8,128)(2,1)S(1)}, u32[]{:S(2)}, u32[]{:S(2)}) collective-permute-start(bf16[256,256]{1,0:T(8,128)(2,1)S(1)} %attend.1.c0), channel_id=1, source_target_pairs={{0,12},{4,0},{8,4},{12,8},{1,13},{5,1},{9,5},{13,9},{2,14},{6,2},{... | collective-permute-start | bytes 393224 | tf_op jit(solution)/shard_map/ppermute | solution.py:368
  61.7 3.5 %merge_o.1.merged = bf16[4,4,256,320]{3,2,1,0:T(8,128)(2,1)S(1)} custom-call(s32[5]{0:T(128)S(1)} %stack.23.ids, bf16[720,128]{1,0:T(8,128)(2,1)S(1)} %sort_rows.1.refs_0_, bf16[720,128]{1,0:T(8,128)(2,1)S(1)} %collective-permute-done.4.refs_1_, bf16[720,128]{1,0:T(8,128)(2,1)S(1)} %collective-permute-done.5.refs_2_, ...), custom_call_target="tpu_custom_call" | custom-call | flops 340000000 | bytes 8000000 | tf_op jit(solution)/shard_map/merge_o/pallas_call | solution.py:371
  65.2 1.3 %collective-permute-done.11.c1 = bf16[256,256]{1,0:T(8,128)(2,1)S(1)} collective-permute-done((bf16[256,256]{1,0:T(8,128)(2,1)S(1)}, bf16[256,256]{1,0:T(8,128)(2,1)S(1)}, u32[]{:S(2)}, u32[]{:S(2)}) %collective-permute-start.11) | collective-permute-done | bytes 131104 | tf_op jit(solution)/shard_map/ppermute | solution.py:368
  66.6 0.6 collective-permute-done.13.c3
  67.1 1.9 %project.1 = (bf16[640,128]{1,0:T(8,128)(2,1)S(1)}, bf16[640,128]{1,0:T(8,128)(2,1)S(1)}, bf16[640,128]{1,0:T(8,128)(2,1)S(1)}, bf16[640,128]{1,0:T(8,128)(2,1)S(1)}) custom-call(s32[5]{0:T(128)S(1)} %stack.23.ids, bf16[256,256]{1,0:T(8,128)(2,1)S(1)} %attend.1.c0, bf16[256,256]{1,0:T(8,128)(2,1)S(1)} %collective-permute-done.11.c1, ...), custom_call_target="tpu_custom_call" | custom-call | flops 680000000 | bytes 4000000 | tf_op jit(solution)/shard_map/project/pallas_call | solution.py:385
  69.0 3.7 %collective-permute-start.20 = (bf16[640,128]{1,0:T(8,128)(2,1)S(1)}, bf16[640,128]{1,0:T(8,128)(2,1)S(1)}, u32[]{:S(2)}, u32[]{:S(2)}) collective-permute-start(bf16[640,128]{1,0:T(8,128)(2,1)S(1)} %get-tuple-element.52), channel_id=1, source_target_pairs={{0,3},{1,2},{2,1},{3,0},{4,7},{5,6},{6,5},{7,4},{8,11},{9,10},{10,... | collective-permute-start | bytes 491528 | tf_op jit(solution)/shard_map/ppermute | solution.py:393
  72.7 0.8 collective-permute-start.22
  73.5 4.6 %collective-permute-done.20.p1 = bf16[640,128]{1,0:T(8,128)(2,1)S(1)} collective-permute-done((bf16[640,128]{1,0:T(8,128)(2,1)S(1)}, bf16[640,128]{1,0:T(8,128)(2,1)S(1)}, u32[]{:S(2)}, u32[]{:S(2)}) %collective-permute-start.20) | collective-permute-done | bytes 163872 | tf_op jit(solution)/shard_map/ppermute | solution.py:393
  78.1 7.8 %collective-permute-done.21.p2 = bf16[640,128]{1,0:T(8,128)(2,1)S(1)} collective-permute-done((bf16[640,128]{1,0:T(8,128)(2,1)S(1)}, bf16[640,128]{1,0:T(8,128)(2,1)S(1)}, u32[]{:S(2)}, u32[]{:S(2)}) %collective-permute-start.21) | collective-permute-done | bytes 163872 | tf_op jit(solution)/shard_map/ppermute | solution.py:393
  85.9 0.8 sum_parts.1
  (28 shorter events, 0.6 us)
Async XLA Ops:
  1.8 29.5 %all-to-all-start = ((bf16[32,40,128]{2,1,0:T(8,128)(2,1)}), bf16[32,40,128]{2,1,0:T(8,128)(2,1)S(1)}, u32[]{:S(2)}, u32[]{:S(2)}) async-start(bf16[32,40,128]{2,1,0:T(8,128)(2,1)} %pack.1), calls=%async_computation | async-start | bytes 655360 | tf_op jit(solution)/shard_map/all_to_all | solution.py:310
  13.4 35.1 %copy-start = (bf16[5120,256]{1,0:T(8,128)(2,1)S(1)}, bf16[5120,256]{1,0:T(8,128)(2,1)}, u32[]{:S(2)}) copy-start(bf16[5120,256]{1,0:T(8,128)(2,1)} %refs_8_.2) | copy-start | bytes 7864324
  13.4 35.1 %copy-start.1 = (s32[64]{0:T(128)S(1)}, s32[64]{0:T(128)}, u32[]{:S(2)}) copy-start(s32[64]{0:T(128)} %refs_16_.1) | copy-start | bytes 772
  19.5 12.8 %collective-permute-start = (bf16[64,256]{1,0:T(8,128)(2,1)S(1)}, bf16[64,256]{1,0:T(8,128)(2,1)S(1)}, u32[]{:S(2)}, u32[]{:S(2)}) collective-permute-start(bf16[64,256]{1,0:T(8,128)(2,1)S(1)} %get-tuple-element.31), channel_id=1, source_target_pairs={{0,0},{1,1},{2,4},{3,5},{4,8},{5,9},{6,12},{7,13},{8,2},{9,3},{10,... | collective-permute-start | bytes 98312 | tf_op jit(solution)/shard_map/ppermute | solution.py:329
  20.1 12.1 %collective-permute-start.1 = (bf16[64,256]{1,0:T(8,128)(2,1)S(1)}, bf16[64,256]{1,0:T(8,128)(2,1)S(1)}, u32[]{:S(2)}, u32[]{:S(2)}) collective-permute-start(bf16[64,256]{1,0:T(8,128)(2,1)S(1)} %get-tuple-element.31), channel_id=1, source_target_pairs={{0,1},{1,0},{2,5},{3,4},{4,9},{5,8},{6,13},{7,12},{8,3},{9,2},{10,... | collective-permute-start | bytes 98312 | tf_op jit(solution)/shard_map/ppermute | solution.py:329
  22.0 10.3 %collective-permute-start.2 = (bf16[64,256]{1,0:T(8,128)(2,1)S(1)}, bf16[64,256]{1,0:T(8,128)(2,1)S(1)}, u32[]{:S(2)}, u32[]{:S(2)}) collective-permute-start(bf16[64,256]{1,0:T(8,128)(2,1)S(1)} %get-tuple-element.31), channel_id=1, source_target_pairs={{0,2},{1,3},{2,6},{3,7},{4,10},{5,11},{6,14},{7,15},{8,0},{9,1},{1... | collective-permute-start | bytes 98312 | tf_op jit(solution)/shard_map/ppermute | solution.py:329
  27.1 6.3 %collective-permute-start.3 = (bf16[64,256]{1,0:T(8,128)(2,1)S(1)}, bf16[64,256]{1,0:T(8,128)(2,1)S(1)}, u32[]{:S(2)}, u32[]{:S(2)}) collective-permute-start(bf16[64,256]{1,0:T(8,128)(2,1)S(1)} %get-tuple-element.31), channel_id=1, source_target_pairs={{0,3},{1,2},{2,7},{3,6},{4,11},{5,10},{6,15},{7,14},{8,1},{9,0},{1... | collective-permute-start | bytes 98312 | tf_op jit(solution)/shard_map/ppermute | solution.py:329
  33.4 8.5 %collective-permute-start.14 = (bf16[128,1280]{1,0:T(8,128)(2,1)}, bf16[128,1280]{1,0:T(8,128)(2,1)S(1)}, u32[]{:S(2)}, u32[]{:S(2)}) collective-permute-start(bf16[128,1280]{1,0:T(8,128)(2,1)} %get-tuple-element.42), channel_id=1, source_target_pairs={{0,4},{4,8},{8,12},{12,0},{1,5},{5,9},{9,13},{13,1},{2,6},{6,10},{... | collective-permute-start | bytes 983048 | tf_op jit(solution)/shard_map/ppermute | solution.py:341
  36.7 8.2 %collective-permute-start.15 = (bf16[128,1280]{1,0:T(8,128)(2,1)}, bf16[128,1280]{1,0:T(8,128)(2,1)S(1)}, u32[]{:S(2)}, u32[]{:S(2)}) collective-permute-start(bf16[128,1280]{1,0:T(8,128)(2,1)} %get-tuple-element.43), channel_id=1, source_target_pairs={{0,12},{4,0},{8,4},{12,8},{1,13},{5,1},{9,5},{13,9},{2,14},{6,2},{... | collective-permute-start | bytes 983048 | tf_op jit(solution)/shard_map/ppermute | solution.py:342
  36.7 8.2 %collective-permute-start.9 = (bf16[720,128]{1,0:T(8,128)(2,1)S(1)}, bf16[720,128]{1,0:T(8,128)(2,1)S(1)}, u32[]{:S(2)}, u32[]{:S(2)}) collective-permute-start(bf16[720,128]{1,0:T(8,128)(2,1)S(1)} %sort_rows.1.refs_0_), channel_id=1, source_target_pairs={{0,192},{64,128},{128,64},{192,0},{1,193},{65,129},{129,65},{193,1... | collective-permute-start | bytes 552968 | tf_op jit(solution)/shard_map/ppermute | solution.py:343
  38.2 7.2 %collective-permute-start.5 = (bf16[720,128]{1,0:T(8,128)(2,1)S(1)}, bf16[720,128]{1,0:T(8,128)(2,1)S(1)}, u32[]{:S(2)}, u32[]{:S(2)}) collective-permute-start(bf16[720,128]{1,0:T(8,128)(2,1)S(1)} %sort_rows.1.refs_0_), channel_id=1, source_target_pairs={{0,64},{64,0},{128,192},{192,128},{1,65},{65,1},{129,193},{193,129... | collective-permute-start | bytes 552968 | tf_op jit(solution)/shard_map/ppermute | solution.py:343
  40.0 7.0 %collective-permute-start.7 = (bf16[720,128]{1,0:T(8,128)(2,1)S(1)}, bf16[720,128]{1,0:T(8,128)(2,1)S(1)}, u32[]{:S(2)}, u32[]{:S(2)}) collective-permute-start(bf16[720,128]{1,0:T(8,128)(2,1)S(1)} %sort_rows.1.refs_0_), channel_id=1, source_target_pairs={{0,128},{64,192},{128,0},{192,64},{1,129},{65,193},{129,1},{193,65... | collective-permute-start | bytes 552968 | tf_op jit(solution)/shard_map/ppermute | solution.py:343
  44.9 11.1 %collective-permute-start.16 = (bf16[128,1280]{1,0:T(8,128)(2,1)}, bf16[128,1280]{1,0:T(8,128)(2,1)S(1)}, u32[]{:S(2)}, u32[]{:S(2)}) collective-permute-start(bf16[128,1280]{1,0:T(8,128)(2,1)} %get-tuple-element.46), channel_id=1, source_target_pairs={{0,8},{4,12},{8,0},{12,4},{1,9},{5,13},{9,1},{13,5},{2,10},{6,14},... | collective-permute-start | bytes 983048 | tf_op jit(solution)/shard_map/ppermute | solution.py:345
  44.9 2.1 %collective-permute-start.4 = (bf16[720,128]{1,0:T(8,128)(2,1)S(1)}, bf16[720,128]{1,0:T(8,128)(2,1)S(1)}, u32[]{:S(2)}, u32[]{:S(2)}) collective-permute-start(bf16[720,128]{1,0:T(8,128)(2,1)S(1)} %sort_rows.1.refs_0_), channel_id=1, source_target_pairs={{0,16},{16,0},{1,17},{17,1},{2,18},{18,2},{3,19},{19,3},{4,20},{20... | collective-permute-start | bytes 552968 | tf_op jit(solution)/shard_map/ppermute | solution.py:348
  44.9 2.1 %collective-permute-start.10 = (bf16[720,128]{1,0:T(8,128)(2,1)S(1)}, bf16[720,128]{1,0:T(8,128)(2,1)S(1)}, u32[]{:S(2)}, u32[]{:S(2)}) collective-permute-start(bf16[720,128]{1,0:T(8,128)(2,1)S(1)} %collective-permute-done.9.refs_6_), channel_id=1, source_target_pairs={{0,16},{16,0},{1,17},{17,1},{2,18},{18,2},{3,19},{19,3},{4,20},{20... | collective-permute-start | bytes 552968 | tf_op jit(solution)/shard_map/ppermute | solution.py:348
  45.4 1.6 %collective-permute-start.6 = (bf16[720,128]{1,0:T(8,128)(2,1)S(1)}, bf16[720,128]{1,0:T(8,128)(2,1)S(1)}, u32[]{:S(2)}, u32[]{:S(2)}) collective-permute-start(bf16[720,128]{1,0:T(8,128)(2,1)S(1)} %collective-permute-done.5.refs_2_), channel_id=1, source_target_pairs={{0,16},{16,0},{1,17},{17,1},{2,18},{18,2},{3,19},{19,3},{4,20},{20... | collective-permute-start | bytes 552968 | tf_op jit(solution)/shard_map/ppermute | solution.py:348
  47.0 1.4 %collective-permute-start.8 = (bf16[720,128]{1,0:T(8,128)(2,1)S(1)}, bf16[720,128]{1,0:T(8,128)(2,1)S(1)}, u32[]{:S(2)}, u32[]{:S(2)}) collective-permute-start(bf16[720,128]{1,0:T(8,128)(2,1)S(1)} %collective-permute-done.7.refs_4_), channel_id=1, source_target_pairs={{0,16},{16,0},{1,17},{17,1},{2,18},{18,2},{3,19},{19,3},{4,20},{20... | collective-permute-start | bytes 552968 | tf_op jit(solution)/shard_map/ppermute | solution.py:348
  56.0 3.3 %collective-permute-start.17 = (bf16[128,1280]{1,0:T(8,128)(2,1)S(1)}, bf16[128,1280]{1,0:T(8,128)(2,1)S(1)}, u32[]{:S(2)}, u32[]{:S(2)}) collective-permute-start(bf16[128,1280]{1,0:T(8,128)(2,1)S(1)} %collective-permute-done.14.refs_9_), channel_id=1, source_target_pairs={{0,16},{16,0},{1,17},{17,1},{2,18},{18,2},{3,19},{19,3},{4,20},{20... | collective-permute-start | bytes 983048 | tf_op jit(solution)/shard_map/ppermute | solution.py:370
  56.3 5.5 %collective-permute-start.18 = (bf16[128,1280]{1,0:T(8,128)(2,1)S(1)}, bf16[128,1280]{1,0:T(8,128)(2,1)S(1)}, u32[]{:S(2)}, u32[]{:S(2)}) collective-permute-start(bf16[128,1280]{1,0:T(8,128)(2,1)S(1)} %collective-permute-done.16.refs_10_), channel_id=1, source_target_pairs={{0,16},{16,0},{1,17},{17,1},{2,18},{18,2},{3,19},{19,3},{4,20},{20... | collective-permute-start | bytes 983048 | tf_op jit(solution)/shard_map/ppermute | solution.py:370
  56.6 5.1 %collective-permute-start.19 = (bf16[128,1280]{1,0:T(8,128)(2,1)S(1)}, bf16[128,1280]{1,0:T(8,128)(2,1)S(1)}, u32[]{:S(2)}, u32[]{:S(2)}) collective-permute-start(bf16[128,1280]{1,0:T(8,128)(2,1)S(1)} %collective-permute-done.15.refs_11_), channel_id=1, source_target_pairs={{0,16},{16,0},{1,17},{17,1},{2,18},{18,2},{3,19},{19,3},{4,20},{20... | collective-permute-start | bytes 983048 | tf_op jit(solution)/shard_map/ppermute | solution.py:370
  56.8 9.8 %collective-permute-start.11 = (bf16[256,256]{1,0:T(8,128)(2,1)S(1)}, bf16[256,256]{1,0:T(8,128)(2,1)S(1)}, u32[]{:S(2)}, u32[]{:S(2)}) collective-permute-start(bf16[256,256]{1,0:T(8,128)(2,1)S(1)} %attend.1.c0), channel_id=1, source_target_pairs={{0,4},{4,8},{8,12},{12,0},{1,5},{5,9},{9,13},{13,1},{2,6},{6,10},{... | collective-permute-start | bytes 393224 | tf_op jit(solution)/shard_map/ppermute | solution.py:368
  58.8 7.8 %collective-permute-start.12 = (bf16[256,256]{1,0:T(8,128)(2,1)S(1)}, bf16[256,256]{1,0:T(8,128)(2,1)S(1)}, u32[]{:S(2)}, u32[]{:S(2)}) collective-permute-start(bf16[256,256]{1,0:T(8,128)(2,1)S(1)} %attend.1.c0), channel_id=1, source_target_pairs={{0,8},{4,12},{8,0},{12,4},{1,9},{5,13},{9,1},{13,5},{2,10},{6,14},... | collective-permute-start | bytes 393224 | tf_op jit(solution)/shard_map/ppermute | solution.py:368
  59.4 7.8 %collective-permute-start.13 = (bf16[256,256]{1,0:T(8,128)(2,1)S(1)}, bf16[256,256]{1,0:T(8,128)(2,1)S(1)}, u32[]{:S(2)}, u32[]{:S(2)}) collective-permute-start(bf16[256,256]{1,0:T(8,128)(2,1)S(1)} %attend.1.c0), channel_id=1, source_target_pairs={{0,12},{4,0},{8,4},{12,8},{1,13},{5,1},{9,5},{13,9},{2,14},{6,2},{... | collective-permute-start | bytes 393224 | tf_op jit(solution)/shard_map/ppermute | solution.py:368
  69.0 9.1 %collective-permute-start.20 = (bf16[640,128]{1,0:T(8,128)(2,1)S(1)}, bf16[640,128]{1,0:T(8,128)(2,1)S(1)}, u32[]{:S(2)}, u32[]{:S(2)}) collective-permute-start(bf16[640,128]{1,0:T(8,128)(2,1)S(1)} %get-tuple-element.52), channel_id=1, source_target_pairs={{0,3},{1,2},{2,1},{3,0},{4,7},{5,6},{6,5},{7,4},{8,11},{9,10},{10,... | collective-permute-start | bytes 491528 | tf_op jit(solution)/shard_map/ppermute | solution.py:393
  72.7 13.2 %collective-permute-start.21 = (bf16[640,128]{1,0:T(8,128)(2,1)S(1)}, bf16[640,128]{1,0:T(8,128)(2,1)S(1)}, u32[]{:S(2)}, u32[]{:S(2)}) collective-permute-start(bf16[640,128]{1,0:T(8,128)(2,1)S(1)} %get-tuple-element.53), channel_id=1, source_target_pairs={{0,2},{1,3},{2,0},{3,1},{4,6},{5,7},{6,4},{7,5},{8,10},{9,11},{10,... | collective-permute-start | bytes 491528 | tf_op jit(solution)/shard_map/ppermute | solution.py:393
  72.7 13.2 %collective-permute-start.22 = (bf16[640,128]{1,0:T(8,128)(2,1)S(1)}, bf16[640,128]{1,0:T(8,128)(2,1)S(1)}, u32[]{:S(2)}, u32[]{:S(2)}) collective-permute-start(bf16[640,128]{1,0:T(8,128)(2,1)S(1)} %get-tuple-element.54), channel_id=1, source_target_pairs={{0,1},{1,0},{2,3},{3,2},{4,5},{5,4},{6,7},{7,6},{8,9},{9,8},{10,11... | collective-permute-start | bytes 491528 | tf_op jit(solution)/shard_map/ppermute | solution.py:393

commit v4 on v3

--- a/solution.py
+++ b/solution.py
@@ -59,12 +59,12 @@
     lax.fori_loop(0, out.shape[0], write, 0)
 
 
-def norm_kernel(ids, states, wkv_t, wo, blocks, kv_t, w1, w2, w3, x_v, w_v, flat, out_v, cut, sems):
+def norm_kernel(ids, states, wkv_t, wo, normed_h, kv_t, w1, w2, w3, x_v, w_v, flat, cut, sems):
     c, y = ids[2], ids[3]
     half = pl.ds(pl.multiple_of(c * 128, 128), 128)
     loads = [pltpu.make_async_copy(states.at[n], x_v.at[n], sems.at[n]) for n in range(STEPS)]
     loads.append(pltpu.make_async_copy(wkv_t, w_v, sems.at[STEPS]))
-    cuts, puts = [], []
+    cuts, puts, stores = [], [], []
     for n, ref in enumerate((w1, w2, w3)):
         at = pl.multiple_of(((y + n + 1) & 3) * 1280, 1280)
         cuts.append(pltpu.make_async_copy(wo.at[half, pl.ds(at, 1280)], cut.at[n], sems.at[5 + n]))
@@ -80,23 +80,23 @@
             scale = lax.rsqrt(jnp.mean(x * x, axis=1, keepdims=True) + 1e-06)
             normed = (x * scale).astype(BF)
             to = pl.ds(pl.multiple_of(n * 64 + r, 32), 32)
-            flat[to, :] = normed
-            for xc in range(8):
-                g = (xc // 2) * 4 + xc % 2
-                out_v[xc, to, :] = jnp.concatenate(
-                    [normed[:, g * 320 : g * 320 + 320], normed[:, g * 320 + 640 : g * 320 + 960]], axis=1
-                )
+            for k in range(10):
+                flat[k, to, :] = normed[:, k * 512 : k * 512 + 512]
             return carry
 
-        lax.fori_loop(0, 2, rows, 0)
+        lax.fori_loop(0, 2, rows, 0, unroll=True)
+        span = pl.ds(n * 64, 64)
+        stores.append(pltpu.make_async_copy(flat.at[:, span], normed_h.at[:, span], sems.at[11 + n]))
+        stores[n].start()
     for cut_copy, put in zip(cuts, puts):
         cut_copy.wait()
         put.start()
-    store = pltpu.make_async_copy(out_v, blocks, sems.at[11])
-    store.start()
     loads[STEPS].wait()
-    kv_t[...] = mm_t(flat[...], w_v[...]).T.astype(BF)
-    for copy in puts + [store]:
+    total = mm_t(flat[0], w_v[:, 0:512])
+    for k in range(1, 10):
+        total = total + mm_t(flat[k], w_v[:, k * 512 : k * 512 + 512])
+    kv_t[...] = total.T.astype(BF)
+    for copy in puts + stores:
         copy.wait()
 
 
@@ -128,41 +128,54 @@
     return jnp.where((h == half) & (r == rank + first), 1.0, 0.0).astype(BF)
 
 
+def fold(a, op):
+    out = a[:, 0:128]
+    for at in range(128, a.shape[1], 128):
+        out = op(out, a[:, at : at + 128])
+    return out
+
+
 def attend_kernel(ids, *refs):
     blocks = refs[:8]
     wq, normed_h, kc_h, vc_h = refs[8:12]
     pieces, lens, ctx = refs[12:16], refs[16], refs[17]
-    kv, qs, cs, normed, kc, vc, sems = refs[18:]
+    kv, qs, qa, sn_all, pn_all, oc, normed, lower, merged, kc, vc, sems = refs[18:]
     x, c, y, z = ids[0], ids[2], ids[3], ids[4]
-    loads = [
-        pltpu.make_async_copy(kc_h.at[:, y], kc, sems.at[0]),
-        pltpu.make_async_copy(vc_h.at[:, y], vc, sems.at[1]),
+    load = pltpu.make_async_copy(normed_h, normed, sems.at[0])
+    caches = [
+        pltpu.make_async_copy(kc_h.at[:, y], kc, sems.at[1]),
+        pltpu.make_async_copy(vc_h.at[:, y], vc, sems.at[2]),
     ]
-    ats = [(x ^ (n // 2)) * 2 + c + n % 2 - 2 * c * (n % 2) for n in range(8)]
-    steps = [pltpu.make_async_copy(normed_h.at[at], normed.at[n], sems.at[2 + n]) for n, at in enumerate(ats)]
-    for copy in steps + loads:
+    for copy in [load] + caches:
         copy.start()
     stack = jnp.concatenate([b[640:656, :] for b in blocks], axis=0)
     upper = jnp.concatenate(
         [2.0 * mm(rank_order(ids, h, 0), stack) for h in range(2)], axis=1
     ).astype(BF)
-    total = jnp.zeros((ROWS, 256), F32)
     for n in range(8):
-        rank = mm(blocks[n][0:640, :], upper)
-        at = ats[n]
-        row = pl.multiple_of((at >> 1) * 1280 + (at & 1) * 320, 320)
-        base = jnp.concatenate([wq[pl.ds(row, 320), :], wq[pl.ds(row + 640, 320), :]], axis=0)
-        merged = (base.astype(F32) + rank).astype(BF)
-        steps[n].wait()
-        total = total + mm(normed[n], merged)
+        row = ((x ^ (n // 2)) * 4 + c + n % 2 - 2 * c * (n % 2)) * 320
+        for zh in range(2):
+            to = pl.ds(pl.multiple_of(row + 640 * zh, 320), 320)
+            lower[to, :] = blocks[n][zh * 320 : zh * 320 + 320, :]
+    for n in range(10):
+        rows = slice(n * 512, n * 512 + 512)
+        merged[n] = (wq[rows, :].astype(F32) + mm(lower[rows, :], upper)).astype(BF)
+    load.wait()
+    total = mm(normed[0], merged[0])
+    for n in range(1, 10):
+        total = total + mm(normed[n], merged[n])
     qs[...] = total.astype(BF).astype(F32)
+    for b in range(8):
+        pieces_b = [
+            qs[s * 64 + b * 8 : s * 64 + b * 8 + 8, h * 128 : h * 128 + 128] for s in range(4) for h in range(2)
+        ]
+        qa[b * 64 : b * 64 + 64, :] = jnp.concatenate(pieces_b, axis=0).astype(BF)
     for k, ref in enumerate(pieces):
         kv[(z ^ k) & 3] = ref[...]
     key_t = kv[0:2].reshape(128, 256)
     val = kv[2:4].reshape(128, 256).astype(F32).T.astype(BF)
-    for copy in loads:
-        copy.wait()
     factor = 1.0 / HD**0.5
+    sn_all[...] = mm(qa[...], key_t) * factor
     c8 = lax.broadcasted_iota(jnp.int32, (8, 512), 1)
     r8 = lax.broadcasted_iota(jnp.int32, (8, 512), 0)
     own_cached = (c8 >> 6) == r8
@@ -171,11 +184,12 @@
     rn = lax.broadcasted_iota(jnp.int32, (64, 256), 0)
     seen = (cn >> 6) <= (rn >> 4)
 
+    for copy in caches:
+        copy.wait()
+
     def batch(b, carry):
         r = pl.multiple_of(b * 8, 8)
-        q = jnp.concatenate(
-            [qs[pl.ds(s * 64 + r, 8), h * 128 : h * 128 + 128] for s in range(4) for h in range(2)], axis=0
-        ).astype(BF)
+        rows = pl.ds(pl.multiple_of(b * 64, 64), 64)
         keys = kc[pl.ds(r, 8)].reshape(512, 128)
         vals = vc[pl.ds(r, 8)].reshape(512, 128)
         length = jnp.zeros((8, 512), jnp.int32)
@@ -184,22 +198,24 @@
         ok = jnp.where(own_cached & (pos < length), 1.0, 0.0)
         okc = jnp.concatenate([ok] * 8, axis=0) > 0.5
         okn = seen & ((cn & 63) == (rn & 7) + r)
-        sc = jnp.where(okc, mm_t(q, keys) * factor, -1e30)
-        sn = jnp.where(okn, mm(q, key_t) * factor, -1e30)
-        top = jnp.maximum(jnp.max(sc, axis=1, keepdims=True), jnp.max(sn, axis=1, keepdims=True))
+        sc = jnp.where(okc, mm_t(qa[rows, :], keys) * factor, -1e30)
+        sn = jnp.where(okn, sn_all[rows, :], -1e30)
+        top = jnp.max(jnp.maximum(fold(sc, jnp.maximum), fold(sn, jnp.maximum)), axis=1, keepdims=True)
         ec, en = jnp.exp(sc - top), jnp.exp(sn - top)
-        total = jnp.sum(ec, axis=1, keepdims=True) + jnp.sum(en, axis=1, keepdims=True)
+        total = jnp.sum(fold(ec, jnp.add) + fold(en, jnp.add), axis=1, keepdims=True)
         inverse = 1.0 / total
-        pc, pn = (ec * inverse).astype(BF), (en * inverse).astype(BF)
-        out = mm(pc, vals) + mm(pn, val)
+        pn_all[rows, :] = (en * inverse).astype(BF)
+        oc[rows, :] = mm((ec * inverse).astype(BF), vals)
+        return carry
+
+    lax.fori_loop(0, 8, batch, 0, unroll=8)
+    out = oc[...] + mm(pn_all[...], val)
+    for b in range(8):
         for s in range(4):
             for h in range(2):
-                n = (s * 2 + h) * 8
-                cs[pl.ds(s * 64 + r, 8), h * 128 : h * 128 + 128] = out[n : n + 8]
-        return carry
-
-    lax.fori_loop(0, 8, batch, 0, unroll=4)
-    ctx[...] = cs[...].astype(BF)
+                n = b * 64 + (s * 2 + h) * 8
+                qs[s * 64 + b * 8 : s * 64 + b * 8 + 8, h * 128 : h * 128 + 128] = out[n : n + 8]
+    ctx[...] = qs[...].astype(BF)
 
 
 def merge_o_kernel(ids, *refs):
@@ -207,7 +223,7 @@
     wo = refs[8]
     same, other = refs[9:12], refs[12:15]
     out, hold, low, own, sem = refs[15:]
-    x, c, y = ids[0], ids[2], ids[3]
+    x, c, y, z = ids[0], ids[2], ids[3], ids[4]
     load = pltpu.make_async_copy(wo.at[:, pl.ds(pl.multiple_of(y * 1280, 1280), 1280)], own, sem)
     load.start()
     ks = x ^ y
@@ -233,19 +249,18 @@
             u = hold[o, zh * 320 : zh * 320 + 320, :]
             cols = slice(zz * 320, zz * 320 + 320)
             if k == 0:
-                out[k, zz] = (own[:, cols].astype(F32) + mm_t(low[...], u)).astype(BF)
+                out[k, zz ^ z] = (own[:, cols].astype(F32) + mm_t(low[...], u)).astype(BF)
             else:
                 for ref, core in ((same[k - 1], c), (other[k - 1], 1 - c)):
                     at = pl.ds(pl.multiple_of(core * 128, 128), 128)
-                    out[k, zz, at] = (ref[:, cols].astype(F32) + mm_t(low[at, :], u)).astype(BF)
-
-
-def project_kernel(ids, c0, c1, c2, c3, merged, *out):
+                    out[k, zz ^ z, at] = (ref[:, cols].astype(F32) + mm_t(low[at, :], u)).astype(BF)
+
+
+def project_kernel(c0, c1, c2, c3, merged, *out):
     for n in (3, 2, 1, 0):
-        zz = ids[4] ^ n
-        total = mm(c0[...], merged[0, zz])
+        total = mm(c0[...], merged[0, n])
         for k, ref in ((1, c1), (2, c2), (3, c3)):
-            total = total + mm(ref[...], merged[k, zz])
+            total = total + mm(ref[...], merged[k, n])
         total = total.astype(BF)
         out[n][0:256] = total[:, 0:128]
         out[n][256:512] = total[:, 128:256]
@@ -311,21 +326,21 @@
 
     normed, kv_t, *w_sent = pl.pallas_call(
         norm_kernel,
-        out_shape=(pltpu.HBM((8, ROWS, 640), BF), array(64, ROWS)) + (pltpu.HBM((128, 1280), BF),) * 3,
+        out_shape=(pltpu.HBM((10, ROWS, 512), BF), array(64, ROWS)) + (pltpu.HBM((128, 1280), BF),) * 3,
         in_specs=[SMEM, hbm, hbm, hbm],
         out_specs=(hbm, vmem, hbm, hbm, hbm),
         scratch_shapes=[
             pltpu.VMEM((STEPS, 64, WIDTH), BF),
             pltpu.VMEM((64, WIDTH), BF),
-            pltpu.VMEM((ROWS, WIDTH), BF),
-            pltpu.VMEM((8, ROWS, 640), BF),
+            pltpu.VMEM((10, ROWS, 512), BF),
             pltpu.VMEM((3, 128, 1280), BF),
-            pltpu.SemaphoreType.DMA((12,)),
+            pltpu.SemaphoreType.DMA((15,)),
         ],
         compiler_params=params(20),
         cost_estimate=pl.CostEstimate(flops=170_000_000, bytes_accessed=8_000_000, transcendentals=0),
         name="norm_kv",
     )(ids, far(states), far(wkv.T), far(wo))
+
     new_kv = [lax.ppermute(kv_t, TP, kv_pairs(k)) for k in range(4)]
 
     swap = [(0, 1), (1, 0)]
@@ -354,11 +369,16 @@
         scratch_shapes=[
             pltpu.VMEM((4, 64, 256), BF),
             pltpu.VMEM((ROWS, 256), F32),
-            pltpu.VMEM((ROWS, 256), F32),
-            pltpu.VMEM((8, ROWS, 640), BF),
+            pltpu.VMEM((512, 128), BF),
+            pltpu.VMEM((512, 256), F32),
+            pltpu.VMEM((512, 256), BF),
+            pltpu.VMEM((512, 128), F32),
+            pltpu.VMEM((10, ROWS, 512), BF),
+            pltpu.VMEM((WIDTH, 128), BF),
+            pltpu.VMEM((10, 512, 256), BF),
             pltpu.VMEM((64, 64, 128), BF),
             pltpu.VMEM((64, 64, 128), BF),
-            pltpu.SemaphoreType.DMA((10,)),
+            pltpu.SemaphoreType.DMA((3,)),
         ],
         compiler_params=params(24),
         cost_estimate=pl.CostEstimate(flops=1_000_000_000, bytes_accessed=10_000_000, transcendentals=400_000),
@@ -385,11 +405,10 @@
     sums = pl.pallas_call(
         project_kernel,
         out_shape=(array(640, 128),) * 4,
-        in_specs=[SMEM] + [vmem] * 5,
         compiler_params=params(16),
         cost_estimate=pl.CostEstimate(flops=680_000_000, bytes_accessed=4_000_000, transcendentals=0),
         name="project",
-    )(ids, ctx, others[1], others[2], others[3], merged)
+    )(ctx, others[1], others[2], others[3], merged)
     came = [lax.ppermute(sums[n], "z", partner(n)) for n in (3, 2, 1)]
     return pl.pallas_call(
         sum_kernel,

time: 87 us -> 84.5 us (0.971)
  Pallas kernels: 22.6 us -> 20.2 us
    pallas_call x2, Pallas kernels: 7.95 us -> 5.61 us  [the longest x1 4.29 us: local(): pl.pallas_call(norm_kernel, out_shape=(pltpu.HBM((10, ROWS, 512), BF), ar...]
  transfers between devices with their start and end apart: 24 -> 24, of which waited for: 9 -> 9; matrix products, arithmetic and copies ran while one was open for 0% -> 0% of each run, Pallas kernels for 21% -> 19%
where the time goes in v4:
time: 84.5 us; the launch traced here: 84.2 us
  starting transfers between devices  40.8 us (48%)
  waiting for transfers between devices  23.1 us (27%)
  Pallas kernels  20.2 us (24%)
    ppermute x3, waiting for transfers between devices, local(): came = [lax.ppermute(sums[n], 'z', partner(n)) for n in (3, 2, 1)]  12.4 us
    ppermute x4, starting transfers between devices, local(): new_kv = [lax.ppermute(kv_t, TP, kv_pairs(k)) for k in range(4)]  11.8 us
    all_to_all x1, starting transfers between devices, local(): got = lax.all_to_all(messages, ('zh', 'y', 'z'), 0, 0, tiled=True)  11.5 us
    pallas_call x1, Pallas kernels, local(): pl.pallas_call(attend_kernel, out_shape=array(ROWS, 256), in_specs=[SMEM]...  7.49 us
    ppermute x3, starting transfers between devices, local(): others = {s: lax.ppermute(ctx, 'y', ring(s)) for s in (1, 3, 2)}  4.94 us
    ppermute x3, starting transfers between devices, local(): came = [lax.ppermute(sums[n], 'z', partner(n)) for n in (3, 2, 1)]  4.47 us
    pallas_call x1, Pallas kernels, local(): pl.pallas_call(norm_kernel, out_shape=(pltpu.HBM((10, ROWS, 512), BF), ar...  4.29 us
    pallas_call x1, Pallas kernels, local(): pl.pallas_call(merge_o_kernel, out_shape=array(4, 4, 256, 320), in_specs=...  3.52 us
  transfers between devices with their start and end apart: 24, of which 9 were waited for; matrix products, arithmetic and copies ran while one was open for 0% of the time, Pallas kernels for 19%

profile of v4, /device:TPU:2, one launch (start us, length us, event | category | flops | bytes accessed | tf_op | source)
XLA Modules:
  0.0 84.2 jit_solution(15906867206848570772)
XLA Ops:
  0.0 1.7 %pack.1 = bf16[32,40,128]{2,1,0:T(8,128)(2,1)} custom-call(bf16[20,64]{1,0:T(8,128)(2,1)} %low.1, bf16[20,64]{1,0:T(8,128)(2,1)} %up.1, bf16[4,256]{1,0:T(4,128)(2,1)} %q_up.1, bf16[4,256]{1,0:T(4,128)(2,1)} %o_low.1), custom_call_target="tpu_custom_call" | custom-call | tf_op jit(solution)/shard_map/pack/pallas_call | solution.py:311
  1.8 11.5 %all-to-all-start = ((bf16[32,40,128]{2,1,0:T(8,128)(2,1)}), bf16[32,40,128]{2,1,0:T(8,128)(2,1)S(1)}, u32[]{:S(2)}, u32[]{:S(2)}) async-start(bf16[32,40,128]{2,1,0:T(8,128)(2,1)} %pack.1), calls=%async_computation | async-start | bytes 655360 | tf_op jit(solution)/shard_map/all_to_all | solution.py:325
  13.4 4.3 %norm_kv.1 = (bf16[10,256,512]{2,1,0:T(8,128)(2,1)}, bf16[64,256]{1,0:T(8,128)(2,1)S(1)}, bf16[128,1280]{1,0:T(8,128)(2,1)}, bf16[128,1280]{1,0:T(8,128)(2,1)}, bf16[128,1280]{1,0:T(8,128)(2,1)}) custom-call(s32[5]{0:T(128)S(1)} %stack.23.ids, bf16[4,64,5120]{2,1,0:T(8,128)(2,1)} %states.1, bf16[64,5120]{1,0:T(8,128)(2,1)} %bitcast.6, bf16[256,5120]{1,0:T(8,128)(2,1)} %refs_8_.3), custom_call_target="tpu_custom_call" | custom-call | flops 170000000 | bytes 8000000 | tf_op jit(solution)/shard_map/norm_kv/pallas_call | solution.py:327
  17.7 0.7 collective-permute-start
  18.3 1.9 %collective-permute-start.1 = (bf16[64,256]{1,0:T(8,128)(2,1)S(1)}, bf16[64,256]{1,0:T(8,128)(2,1)S(1)}, u32[]{:S(2)}, u32[]{:S(2)}) collective-permute-start(bf16[64,256]{1,0:T(8,128)(2,1)S(1)} %get-tuple-element.31), channel_id=1, source_target_pairs={{0,1},{1,0},{2,5},{3,4},{4,9},{5,8},{6,13},{7,12},{8,3},{9,2},{10,... | collective-permute-start | bytes 98312 | tf_op jit(solution)/shard_map/ppermute | solution.py:344
  20.2 5.1 %collective-permute-start.2 = (bf16[64,256]{1,0:T(8,128)(2,1)S(1)}, bf16[64,256]{1,0:T(8,128)(2,1)S(1)}, u32[]{:S(2)}, u32[]{:S(2)}) collective-permute-start(bf16[64,256]{1,0:T(8,128)(2,1)S(1)} %get-tuple-element.31), channel_id=1, source_target_pairs={{0,2},{1,3},{2,6},{3,7},{4,10},{5,11},{6,14},{7,15},{8,0},{9,1},{1... | collective-permute-start | bytes 98312 | tf_op jit(solution)/shard_map/ppermute | solution.py:344
  25.3 4.2 %collective-permute-start.3 = (bf16[64,256]{1,0:T(8,128)(2,1)S(1)}, bf16[64,256]{1,0:T(8,128)(2,1)S(1)}, u32[]{:S(2)}, u32[]{:S(2)}) collective-permute-start(bf16[64,256]{1,0:T(8,128)(2,1)S(1)} %get-tuple-element.31), channel_id=1, source_target_pairs={{0,3},{1,2},{2,7},{3,6},{4,11},{5,10},{6,15},{7,14},{8,1},{9,0},{1... | collective-permute-start | bytes 98312 | tf_op jit(solution)/shard_map/ppermute | solution.py:344
  29.4 1.0 %sort_rows.1.refs_0_ = bf16[720,128]{1,0:T(8,128)(2,1)S(1)} custom-call(s32[5]{0:T(128)S(1)} %stack.23.ids, bf16[32,40,128]{2,1,0:T(8,128)(2,1)S(1)} %all-to-all-done.got), custom_call_target="tpu_custom_call" | custom-call | tf_op jit(solution)/shard_map/sort_rows/pallas_call | solution.py:348
  30.5 1.1 %collective-permute-done.3.refs_15_ = bf16[64,256]{1,0:T(8,128)(2,1)S(1)} collective-permute-done((bf16[64,256]{1,0:T(8,128)(2,1)S(1)}, bf16[64,256]{1,0:T(8,128)(2,1)S(1)}, u32[]{:S(2)}, u32[]{:S(2)}) %collective-permute-start.3) | collective-permute-done | bytes 32800 | tf_op jit(solution)/shard_map/ppermute | solution.py:344
  31.6 3.3 %collective-permute-start.14 = (bf16[128,1280]{1,0:T(8,128)(2,1)}, bf16[128,1280]{1,0:T(8,128)(2,1)S(1)}, u32[]{:S(2)}, u32[]{:S(2)}) collective-permute-start(bf16[128,1280]{1,0:T(8,128)(2,1)} %get-tuple-element.42), channel_id=1, source_target_pairs={{0,4},{4,8},{8,12},{12,0},{1,5},{5,9},{9,13},{13,1},{2,6},{6,10},{... | collective-permute-start | bytes 983048 | tf_op jit(solution)/shard_map/ppermute | solution.py:356
  34.9 1.5 %collective-permute-start.9 = (bf16[720,128]{1,0:T(8,128)(2,1)S(1)}, bf16[720,128]{1,0:T(8,128)(2,1)S(1)}, u32[]{:S(2)}, u32[]{:S(2)}) collective-permute-start(bf16[720,128]{1,0:T(8,128)(2,1)S(1)} %sort_rows.1.refs_0_), channel_id=1, source_target_pairs={{0,192},{64,128},{128,64},{192,0},{1,193},{65,129},{129,65},{193,1... | collective-permute-start | bytes 552968 | tf_op jit(solution)/shard_map/ppermute | solution.py:358
  36.4 1.8 %collective-permute-start.5 = (bf16[720,128]{1,0:T(8,128)(2,1)S(1)}, bf16[720,128]{1,0:T(8,128)(2,1)S(1)}, u32[]{:S(2)}, u32[]{:S(2)}) collective-permute-start(bf16[720,128]{1,0:T(8,128)(2,1)S(1)} %sort_rows.1.refs_0_), channel_id=1, source_target_pairs={{0,64},{64,0},{128,192},{192,128},{1,65},{65,1},{129,193},{193,129... | collective-permute-start | bytes 552968 | tf_op jit(solution)/shard_map/ppermute | solution.py:358
  38.3 1.7 %collective-permute-done.14.refs_9_ = bf16[128,1280]{1,0:T(8,128)(2,1)S(1)} collective-permute-done((bf16[128,1280]{1,0:T(8,128)(2,1)}, bf16[128,1280]{1,0:T(8,128)(2,1)S(1)}, u32[]{:S(2)}, u32[]{:S(2)}) %collective-permute-start.14) | collective-permute-done | bytes 327712 | tf_op jit(solution)/shard_map/ppermute | solution.py:356
  40.1 3.0 %collective-permute-done.15.refs_11_ = bf16[128,1280]{1,0:T(8,128)(2,1)S(1)} collective-permute-done((bf16[128,1280]{1,0:T(8,128)(2,1)}, bf16[128,1280]{1,0:T(8,128)(2,1)S(1)}, u32[]{:S(2)}, u32[]{:S(2)}) %collective-permute-start.15) | collective-permute-done | bytes 327712 | tf_op jit(solution)/shard_map/ppermute | solution.py:357
  43.1 0.5 collective-permute-start.10
  43.7 1.5 %collective-permute-done.7.refs_4_ = bf16[720,128]{1,0:T(8,128)(2,1)S(1)} collective-permute-done((bf16[720,128]{1,0:T(8,128)(2,1)S(1)}, bf16[720,128]{1,0:T(8,128)(2,1)S(1)}, u32[]{:S(2)}, u32[]{:S(2)}) %collective-permute-start.7) | collective-permute-done | bytes 184352 | tf_op jit(solution)/shard_map/ppermute | solution.py:358
  45.2 1.4 %collective-permute-done.8.refs_5_ = bf16[720,128]{1,0:T(8,128)(2,1)S(1)} collective-permute-done((bf16[720,128]{1,0:T(8,128)(2,1)S(1)}, bf16[720,128]{1,0:T(8,128)(2,1)S(1)}, u32[]{:S(2)}, u32[]{:S(2)}) %collective-permute-start.8) | collective-permute-done | bytes 184352 | tf_op jit(solution)/shard_map/ppermute | solution.py:363
  46.6 7.5 %attend.1.c0 = bf16[256,256]{1,0:T(8,128)(2,1)S(1)} custom-call(s32[5]{0:T(128)S(1)} %stack.23.ids, bf16[720,128]{1,0:T(8,128)(2,1)S(1)} %sort_rows.1.refs_0_, bf16[720,128]{1,0:T(8,128)(2,1)S(1)} %collective-permute-done.4.refs_1_, bf16[720,128]{1,0:T(8,128)(2,1)S(1)} %collective-permute-done.5.refs_2_, ...), custom_call_target="tpu_custom_call" | custom-call | flops 1000000000 | bytes 10000000 | tf_op jit(solution)/shard_map/attend/pallas_call | solution.py:365
  54.1 0.2 collective-permute-start.17
  54.4 0.4 collective-permute-start.18
  54.9 2.0 %collective-permute-start.11 = (bf16[256,256]{1,0:T(8,128)(2,1)S(1)}, bf16[256,256]{1,0:T(8,128)(2,1)S(1)}, u32[]{:S(2)}, u32[]{:S(2)}) collective-permute-start(bf16[256,256]{1,0:T(8,128)(2,1)S(1)} %attend.1.c0), channel_id=1, source_target_pairs={{0,4},{4,8},{8,12},{12,0},{1,5},{5,9},{9,13},{13,1},{2,6},{6,10},{... | collective-permute-start | bytes 393224 | tf_op jit(solution)/shard_map/ppermute | solution.py:388
  56.9 0.6 collective-permute-start.12
  57.5 2.3 %collective-permute-start.13 = (bf16[256,256]{1,0:T(8,128)(2,1)S(1)}, bf16[256,256]{1,0:T(8,128)(2,1)S(1)}, u32[]{:S(2)}, u32[]{:S(2)}) collective-permute-start(bf16[256,256]{1,0:T(8,128)(2,1)S(1)} %attend.1.c0), channel_id=1, source_target_pairs={{0,12},{4,0},{8,4},{12,8},{1,13},{5,1},{9,5},{13,9},{2,14},{6,2},{... | collective-permute-start | bytes 393224 | tf_op jit(solution)/shard_map/ppermute | solution.py:388
  59.8 3.5 %merge_o.1.merged = bf16[4,4,256,320]{3,2,1,0:T(8,128)(2,1)S(1)} custom-call(s32[5]{0:T(128)S(1)} %stack.23.ids, bf16[720,128]{1,0:T(8,128)(2,1)S(1)} %sort_rows.1.refs_0_, bf16[720,128]{1,0:T(8,128)(2,1)S(1)} %collective-permute-done.4.refs_1_, bf16[720,128]{1,0:T(8,128)(2,1)S(1)} %collective-permute-done.5.refs_2_, ...), custom_call_target="tpu_custom_call" | custom-call | flops 340000000 | bytes 8000000 | tf_op jit(solution)/shard_map/merge_o/pallas_call | solution.py:391
  63.3 1.3 %collective-permute-done.11.c1 = bf16[256,256]{1,0:T(8,128)(2,1)S(1)} collective-permute-done((bf16[256,256]{1,0:T(8,128)(2,1)S(1)}, bf16[256,256]{1,0:T(8,128)(2,1)S(1)}, u32[]{:S(2)}, u32[]{:S(2)}) %collective-permute-start.11) | collective-permute-done | bytes 131104 | tf_op jit(solution)/shard_map/ppermute | solution.py:388
  64.7 0.6 collective-permute-done.13.c3
  65.2 1.3 %project.1 = (bf16[640,128]{1,0:T(8,128)(2,1)S(1)}, bf16[640,128]{1,0:T(8,128)(2,1)S(1)}, bf16[640,128]{1,0:T(8,128)(2,1)S(1)}, bf16[640,128]{1,0:T(8,128)(2,1)S(1)}) custom-call(bf16[256,256]{1,0:T(8,128)(2,1)S(1)} %attend.1.c0, bf16[256,256]{1,0:T(8,128)(2,1)S(1)} %collective-permute-done.11.c1, bf16[256,256]{1,0:T(8,128)(2,1)S(1)} %collective-permute-done.12.c2, ...), custom_call_target="tpu_custom_call" | custom-call | flops 680000000 | bytes 4000000 | tf_op jit(solution)/shard_map/project/pallas_call | solution.py:405
  66.6 3.7 %collective-permute-start.20 = (bf16[640,128]{1,0:T(8,128)(2,1)S(1)}, bf16[640,128]{1,0:T(8,128)(2,1)S(1)}, u32[]{:S(2)}, u32[]{:S(2)}) collective-permute-start(bf16[640,128]{1,0:T(8,128)(2,1)S(1)} %get-tuple-element.52), channel_id=1, source_target_pairs={{0,3},{1,2},{2,1},{3,0},{4,7},{5,6},{6,5},{7,4},{8,11},{9,10},{10,... | collective-permute-start | bytes 491528 | tf_op jit(solution)/shard_map/ppermute | solution.py:412
  70.2 0.8 collective-permute-start.22
  71.0 4.6 %collective-permute-done.20.p1 = bf16[640,128]{1,0:T(8,128)(2,1)S(1)} collective-permute-done((bf16[640,128]{1,0:T(8,128)(2,1)S(1)}, bf16[640,128]{1,0:T(8,128)(2,1)S(1)}, u32[]{:S(2)}, u32[]{:S(2)}) %collective-permute-start.20) | collective-permute-done | bytes 163872 | tf_op jit(solution)/shard_map/ppermute | solution.py:412
  75.6 7.8 %collective-permute-done.21.p2 = bf16[640,128]{1,0:T(8,128)(2,1)S(1)} collective-permute-done((bf16[640,128]{1,0:T(8,128)(2,1)S(1)}, bf16[640,128]{1,0:T(8,128)(2,1)S(1)}, u32[]{:S(2)}, u32[]{:S(2)}) %collective-permute-start.21) | collective-permute-done | bytes 163872 | tf_op jit(solution)/shard_map/ppermute | solution.py:412
  83.4 0.8 sum_parts.1
  (28 shorter events, 0.6 us)
Async XLA Ops:
  1.8 27.7 %all-to-all-start = ((bf16[32,40,128]{2,1,0:T(8,128)(2,1)}), bf16[32,40,128]{2,1,0:T(8,128)(2,1)S(1)}, u32[]{:S(2)}, u32[]{:S(2)}) async-start(bf16[32,40,128]{2,1,0:T(8,128)(2,1)} %pack.1), calls=%async_computation | async-start | bytes 655360 | tf_op jit(solution)/shard_map/all_to_all | solution.py:325
  13.4 33.3 %copy-start = (bf16[5120,256]{1,0:T(8,128)(2,1)S(1)}, bf16[5120,256]{1,0:T(8,128)(2,1)}, u32[]{:S(2)}) copy-start(bf16[5120,256]{1,0:T(8,128)(2,1)} %refs_8_.2) | copy-start | bytes 7864324
  13.4 33.3 %copy-start.1 = (s32[64]{0:T(128)S(1)}, s32[64]{0:T(128)}, u32[]{:S(2)}) copy-start(s32[64]{0:T(128)} %refs_16_.1) | copy-start | bytes 772
  17.7 12.8 %collective-permute-start = (bf16[64,256]{1,0:T(8,128)(2,1)S(1)}, bf16[64,256]{1,0:T(8,128)(2,1)S(1)}, u32[]{:S(2)}, u32[]{:S(2)}) collective-permute-start(bf16[64,256]{1,0:T(8,128)(2,1)S(1)} %get-tuple-element.31), channel_id=1, source_target_pairs={{0,0},{1,1},{2,4},{3,5},{4,8},{5,9},{6,12},{7,13},{8,2},{9,3},{10,... | collective-permute-start | bytes 98312 | tf_op jit(solution)/shard_map/ppermute | solution.py:344
  18.3 12.1 %collective-permute-start.1 = (bf16[64,256]{1,0:T(8,128)(2,1)S(1)}, bf16[64,256]{1,0:T(8,128)(2,1)S(1)}, u32[]{:S(2)}, u32[]{:S(2)}) collective-permute-start(bf16[64,256]{1,0:T(8,128)(2,1)S(1)} %get-tuple-element.31), channel_id=1, source_target_pairs={{0,1},{1,0},{2,5},{3,4},{4,9},{5,8},{6,13},{7,12},{8,3},{9,2},{10,... | collective-permute-start | bytes 98312 | tf_op jit(solution)/shard_map/ppermute | solution.py:344
  20.2 10.3 %collective-permute-start.2 = (bf16[64,256]{1,0:T(8,128)(2,1)S(1)}, bf16[64,256]{1,0:T(8,128)(2,1)S(1)}, u32[]{:S(2)}, u32[]{:S(2)}) collective-permute-start(bf16[64,256]{1,0:T(8,128)(2,1)S(1)} %get-tuple-element.31), channel_id=1, source_target_pairs={{0,2},{1,3},{2,6},{3,7},{4,10},{5,11},{6,14},{7,15},{8,0},{9,1},{1... | collective-permute-start | bytes 98312 | tf_op jit(solution)/shard_map/ppermute | solution.py:344
  25.3 6.3 %collective-permute-start.3 = (bf16[64,256]{1,0:T(8,128)(2,1)S(1)}, bf16[64,256]{1,0:T(8,128)(2,1)S(1)}, u32[]{:S(2)}, u32[]{:S(2)}) collective-permute-start(bf16[64,256]{1,0:T(8,128)(2,1)S(1)} %get-tuple-element.31), channel_id=1, source_target_pairs={{0,3},{1,2},{2,7},{3,6},{4,11},{5,10},{6,15},{7,14},{8,1},{9,0},{1... | collective-permute-start | bytes 98312 | tf_op jit(solution)/shard_map/ppermute | solution.py:344
  31.6 8.5 %collective-permute-start.14 = (bf16[128,1280]{1,0:T(8,128)(2,1)}, bf16[128,1280]{1,0:T(8,128)(2,1)S(1)}, u32[]{:S(2)}, u32[]{:S(2)}) collective-permute-start(bf16[128,1280]{1,0:T(8,128)(2,1)} %get-tuple-element.42), channel_id=1, source_target_pairs={{0,4},{4,8},{8,12},{12,0},{1,5},{5,9},{9,13},{13,1},{2,6},{6,10},{... | collective-permute-start | bytes 983048 | tf_op jit(solution)/shard_map/ppermute | solution.py:356
  34.9 8.2 %collective-permute-start.15 = (bf16[128,1280]{1,0:T(8,128)(2,1)}, bf16[128,1280]{1,0:T(8,128)(2,1)S(1)}, u32[]{:S(2)}, u32[]{:S(2)}) collective-permute-start(bf16[128,1280]{1,0:T(8,128)(2,1)} %get-tuple-element.43), channel_id=1, source_target_pairs={{0,12},{4,0},{8,4},{12,8},{1,13},{5,1},{9,5},{13,9},{2,14},{6,2},{... | collective-permute-start | bytes 983048 | tf_op jit(solution)/shard_map/ppermute | solution.py:357
  34.9 8.2 %collective-permute-start.9 = (bf16[720,128]{1,0:T(8,128)(2,1)S(1)}, bf16[720,128]{1,0:T(8,128)(2,1)S(1)}, u32[]{:S(2)}, u32[]{:S(2)}) collective-permute-start(bf16[720,128]{1,0:T(8,128)(2,1)S(1)} %sort_rows.1.refs_0_), channel_id=1, source_target_pairs={{0,192},{64,128},{128,64},{192,0},{1,193},{65,129},{129,65},{193,1... | collective-permute-start | bytes 552968 | tf_op jit(solution)/shard_map/ppermute | solution.py:358
  36.4 7.2 %collective-permute-start.5 = (bf16[720,128]{1,0:T(8,128)(2,1)S(1)}, bf16[720,128]{1,0:T(8,128)(2,1)S(1)}, u32[]{:S(2)}, u32[]{:S(2)}) collective-permute-start(bf16[720,128]{1,0:T(8,128)(2,1)S(1)} %sort_rows.1.refs_0_), channel_id=1, source_target_pairs={{0,64},{64,0},{128,192},{192,128},{1,65},{65,1},{129,193},{193,129... | collective-permute-start | bytes 552968 | tf_op jit(solution)/shard_map/ppermute | solution.py:358
  38.2 7.0 %collective-permute-start.7 = (bf16[720,128]{1,0:T(8,128)(2,1)S(1)}, bf16[720,128]{1,0:T(8,128)(2,1)S(1)}, u32[]{:S(2)}, u32[]{:S(2)}) collective-permute-start(bf16[720,128]{1,0:T(8,128)(2,1)S(1)} %sort_rows.1.refs_0_), channel_id=1, source_target_pairs={{0,128},{64,192},{128,0},{192,64},{1,129},{65,193},{129,1},{193,65... | collective-permute-start | bytes 552968 | tf_op jit(solution)/shard_map/ppermute | solution.py:358
  43.1 11.1 %collective-permute-start.16 = (bf16[128,1280]{1,0:T(8,128)(2,1)}, bf16[128,1280]{1,0:T(8,128)(2,1)S(1)}, u32[]{:S(2)}, u32[]{:S(2)}) collective-permute-start(bf16[128,1280]{1,0:T(8,128)(2,1)} %get-tuple-element.46), channel_id=1, source_target_pairs={{0,8},{4,12},{8,0},{12,4},{1,9},{5,13},{9,1},{13,5},{2,10},{6,14},... | collective-permute-start | bytes 983048 | tf_op jit(solution)/shard_map/ppermute | solution.py:360
  43.1 2.1 %collective-permute-start.4 = (bf16[720,128]{1,0:T(8,128)(2,1)S(1)}, bf16[720,128]{1,0:T(8,128)(2,1)S(1)}, u32[]{:S(2)}, u32[]{:S(2)}) collective-permute-start(bf16[720,128]{1,0:T(8,128)(2,1)S(1)} %sort_rows.1.refs_0_), channel_id=1, source_target_pairs={{0,16},{16,0},{1,17},{17,1},{2,18},{18,2},{3,19},{19,3},{4,20},{20... | collective-permute-start | bytes 552968 | tf_op jit(solution)/shard_map/ppermute | solution.py:363
  43.1 2.1 %collective-permute-start.10 = (bf16[720,128]{1,0:T(8,128)(2,1)S(1)}, bf16[720,128]{1,0:T(8,128)(2,1)S(1)}, u32[]{:S(2)}, u32[]{:S(2)}) collective-permute-start(bf16[720,128]{1,0:T(8,128)(2,1)S(1)} %collective-permute-done.9.refs_6_), channel_id=1, source_target_pairs={{0,16},{16,0},{1,17},{17,1},{2,18},{18,2},{3,19},{19,3},{4,20},{20... | collective-permute-start | bytes 552968 | tf_op jit(solution)/shard_map/ppermute | solution.py:363
  43.6 1.6 %collective-permute-start.6 = (bf16[720,128]{1,0:T(8,128)(2,1)S(1)}, bf16[720,128]{1,0:T(8,128)(2,1)S(1)}, u32[]{:S(2)}, u32[]{:S(2)}) collective-permute-start(bf16[720,128]{1,0:T(8,128)(2,1)S(1)} %collective-permute-done.5.refs_2_), channel_id=1, source_target_pairs={{0,16},{16,0},{1,17},{17,1},{2,18},{18,2},{3,19},{19,3},{4,20},{20... | collective-permute-start | bytes 552968 | tf_op jit(solution)/shard_map/ppermute | solution.py:363
  45.2 1.4 %collective-permute-start.8 = (bf16[720,128]{1,0:T(8,128)(2,1)S(1)}, bf16[720,128]{1,0:T(8,128)(2,1)S(1)}, u32[]{:S(2)}, u32[]{:S(2)}) collective-permute-start(bf16[720,128]{1,0:T(8,128)(2,1)S(1)} %collective-permute-done.7.refs_4_), channel_id=1, source_target_pairs={{0,16},{16,0},{1,17},{17,1},{2,18},{18,2},{3,19},{19,3},{4,20},{20... | collective-permute-start | bytes 552968 | tf_op jit(solution)/shard_map/ppermute | solution.py:363
  54.1 3.3 %collective-permute-start.17 = (bf16[128,1280]{1,0:T(8,128)(2,1)S(1)}, bf16[128,1280]{1,0:T(8,128)(2,1)S(1)}, u32[]{:S(2)}, u32[]{:S(2)}) collective-permute-start(bf16[128,1280]{1,0:T(8,128)(2,1)S(1)} %collective-permute-done.14.refs_9_), channel_id=1, source_target_pairs={{0,16},{16,0},{1,17},{17,1},{2,18},{18,2},{3,19},{19,3},{4,20},{20... | collective-permute-start | bytes 983048 | tf_op jit(solution)/shard_map/ppermute | solution.py:390
  54.4 5.5 %collective-permute-start.18 = (bf16[128,1280]{1,0:T(8,128)(2,1)S(1)}, bf16[128,1280]{1,0:T(8,128)(2,1)S(1)}, u32[]{:S(2)}, u32[]{:S(2)}) collective-permute-start(bf16[128,1280]{1,0:T(8,128)(2,1)S(1)} %collective-permute-done.16.refs_10_), channel_id=1, source_target_pairs={{0,16},{16,0},{1,17},{17,1},{2,18},{18,2},{3,19},{19,3},{4,20},{20... | collective-permute-start | bytes 983048 | tf_op jit(solution)/shard_map/ppermute | solution.py:390
  54.7 5.1 %collective-permute-start.19 = (bf16[128,1280]{1,0:T(8,128)(2,1)S(1)}, bf16[128,1280]{1,0:T(8,128)(2,1)S(1)}, u32[]{:S(2)}, u32[]{:S(2)}) collective-permute-start(bf16[128,1280]{1,0:T(8,128)(2,1)S(1)} %collective-permute-done.15.refs_11_), channel_id=1, source_target_pairs={{0,16},{16,0},{1,17},{17,1},{2,18},{18,2},{3,19},{19,3},{4,20},{20... | collective-permute-start | bytes 983048 | tf_op jit(solution)/shard_map/ppermute | solution.py:390
  54.9 9.8 %collective-permute-start.11 = (bf16[256,256]{1,0:T(8,128)(2,1)S(1)}, bf16[256,256]{1,0:T(8,128)(2,1)S(1)}, u32[]{:S(2)}, u32[]{:S(2)}) collective-permute-start(bf16[256,256]{1,0:T(8,128)(2,1)S(1)} %attend.1.c0), channel_id=1, source_target_pairs={{0,4},{4,8},{8,12},{12,0},{1,5},{5,9},{9,13},{13,1},{2,6},{6,10},{... | collective-permute-start | bytes 393224 | tf_op jit(solution)/shard_map/ppermute | solution.py:388
  56.9 7.8 %collective-permute-start.12 = (bf16[256,256]{1,0:T(8,128)(2,1)S(1)}, bf16[256,256]{1,0:T(8,128)(2,1)S(1)}, u32[]{:S(2)}, u32[]{:S(2)}) collective-permute-start(bf16[256,256]{1,0:T(8,128)(2,1)S(1)} %attend.1.c0), channel_id=1, source_target_pairs={{0,8},{4,12},{8,0},{12,4},{1,9},{5,13},{9,1},{13,5},{2,10},{6,14},... | collective-permute-start | bytes 393224 | tf_op jit(solution)/shard_map/ppermute | solution.py:388
  57.5 7.8 %collective-permute-start.13 = (bf16[256,256]{1,0:T(8,128)(2,1)S(1)}, bf16[256,256]{1,0:T(8,128)(2,1)S(1)}, u32[]{:S(2)}, u32[]{:S(2)}) collective-permute-start(bf16[256,256]{1,0:T(8,128)(2,1)S(1)} %attend.1.c0), channel_id=1, source_target_pairs={{0,12},{4,0},{8,4},{12,8},{1,13},{5,1},{9,5},{13,9},{2,14},{6,2},{... | collective-permute-start | bytes 393224 | tf_op jit(solution)/shard_map/ppermute | solution.py:388
  66.6 9.1 %collective-permute-start.20 = (bf16[640,128]{1,0:T(8,128)(2,1)S(1)}, bf16[640,128]{1,0:T(8,128)(2,1)S(1)}, u32[]{:S(2)}, u32[]{:S(2)}) collective-permute-start(bf16[640,128]{1,0:T(8,128)(2,1)S(1)} %get-tuple-element.52), channel_id=1, source_target_pairs={{0,3},{1,2},{2,1},{3,0},{4,7},{5,6},{6,5},{7,4},{8,11},{9,10},{10,... | collective-permute-start | bytes 491528 | tf_op jit(solution)/shard_map/ppermute | solution.py:412
  70.2 13.2 %collective-permute-start.21 = (bf16[640,128]{1,0:T(8,128)(2,1)S(1)}, bf16[640,128]{1,0:T(8,128)(2,1)S(1)}, u32[]{:S(2)}, u32[]{:S(2)}) collective-permute-start(bf16[640,128]{1,0:T(8,128)(2,1)S(1)} %get-tuple-element.53), channel_id=1, source_target_pairs={{0,2},{1,3},{2,0},{3,1},{4,6},{5,7},{6,4},{7,5},{8,10},{9,11},{10,... | collective-permute-start | bytes 491528 | tf_op jit(solution)/shard_map/ppermute | solution.py:412
  70.2 13.2 %collective-permute-start.22 = (bf16[640,128]{1,0:T(8,128)(2,1)S(1)}, bf16[640,128]{1,0:T(8,128)(2,1)S(1)}, u32[]{:S(2)}, u32[]{:S(2)}) collective-permute-start(bf16[640,128]{1,0:T(8,128)(2,1)S(1)} %get-tuple-element.54), channel_id=1, source_target_pairs={{0,1},{1,0},{2,3},{3,2},{4,5},{5,4},{6,7},{7,6},{8,9},{9,8},{10,11... | collective-permute-start | bytes 491528 | tf_op jit(solution)/shard_map/ppermute | solution.py:412

commit v5 on v4

--- a/solution.py
+++ b/solution.py
@@ -1,3 +1,5 @@
+import functools
+
 import jax
 import jax.numpy as jnp
 import numpy as np
@@ -16,7 +18,8 @@
 TP = ("y", "z")
 BF = jnp.bfloat16
 F32 = jnp.float32
-MSG = 40
+MSG = 48
+ORDER = (0, 3, 2, 1)
 XROWS = 720
 
 SMEM = pl.BlockSpec(memory_space=pltpu.SMEM)
@@ -34,22 +37,13 @@
     return lax.dot_general(a, b, (((1,), (1,)), ((), ())), preferred_element_type=F32)
 
 
-def pack_kernel(low, up, q_up, o_low, out, low_v, up_v, qu_v, ol_v, sems):
-    copies = [
-        pltpu.make_async_copy(a, b, sems.at[n])
-        for n, (a, b) in enumerate(((low, low_v), (up, up_v), (q_up, qu_v), (o_low, ol_v)))
-    ]
-    for copy in copies:
-        copy.start()
-    for copy in copies:
-        copy.wait()
-
+def pack_kernel(low, up, q_up, o_low, out):
     def halves(ref):
         a = ref[...].astype(F32)
         return [a[:, :128], a[:, 128:]]
 
-    first = jnp.concatenate([low_v[...].astype(F32), up_v[...].astype(F32)], axis=1)
-    rows = [first, jnp.zeros((4, 128), F32)] + halves(qu_v) + halves(ol_v)
+    first = jnp.concatenate([low[...].astype(F32), up[...].astype(F32)], axis=1)
+    rows = [first, jnp.zeros((12, 128), F32)] + halves(q_up) + halves(o_low)
     message = jnp.concatenate(rows, axis=0).astype(BF)
 
     def write(i, carry):
@@ -101,19 +95,19 @@
 
 
 def sort_kernel(ids, got, out):
-    i = lax.broadcasted_iota(jnp.int32, (80, MSG), 0)
-    j = lax.broadcasted_iota(jnp.int32, (80, MSG), 1)
-    picks = [jnp.where((j == i - 20 * p) & (j < 20), 1.0, 0.0).astype(BF) for p in range(4)]
+    i = lax.broadcasted_iota(jnp.int32, (80, 4 * MSG), 0)
+    j = lax.broadcasted_iota(jnp.int32, (80, 4 * MSG), 1)
+    hit = i < 0
+    for p in range(4):
+        hit = hit | ((j - MSG * p == i - 20 * p) & (i >= 20 * p) & (i < 20 * p + 20))
+    pick = jnp.where(hit, 1.0, 0.0).astype(BF)
     for q in range(8):
-        rows = mm(picks[0], got[4 * q])
-        for p in range(1, 4):
-            rows = rows + mm(picks[p], got[4 * q + p])
-        out[80 * q : 80 * q + 80, :] = rows.astype(BF)
+        out[80 * q : 80 * q + 80, :] = mm(pick, got[4 * q : 4 * q + 4].reshape(4 * MSG, 128)).astype(BF)
     y, z = ids[3], ids[4]
-    own = [got[zh * 16 + y * NZ + z].astype(F32)[24:32] for zh in range(2)]
+    own = [got[zh * 16 + y * NZ + z, 32:48, :].astype(F32)[:8] for zh in range(2)]
     out[640:656, :] = jnp.concatenate(own, axis=0).astype(BF)
     for yy in range(NY):
-        part = [got[zh * 16 + yy * NZ + z].astype(F32)[32:40] for zh in range(2)]
+        part = [got[zh * 16 + yy * NZ + z, 32:48, :].astype(F32)[8:] for zh in range(2)]
         out[656 + 16 * yy : 672 + 16 * yy, :] = jnp.concatenate(part, axis=0).astype(BF)
 
 
@@ -123,7 +117,7 @@
     x, c = ids[0], ids[2]
     k, o = (j >> 5) & 3, (j >> 4) & 1
     zh, h, i = (j >> 3) & 1, (j >> 2) & 1, j & 3
-    xs = x ^ k
+    xs = x ^ ((4 - k) & 3)
     rank = (xs * 4 + zh * 2 + (c + o - 2 * c * o)) * 4 + i
     return jnp.where((h == half) & (r == rank + first), 1.0, 0.0).astype(BF)
 
@@ -153,7 +147,7 @@
         [2.0 * mm(rank_order(ids, h, 0), stack) for h in range(2)], axis=1
     ).astype(BF)
     for n in range(8):
-        row = ((x ^ (n // 2)) * 4 + c + n % 2 - 2 * c * (n % 2)) * 320
+        row = ((x ^ ORDER[n // 2]) * 4 + c + n % 2 - 2 * c * (n % 2)) * 320
         for zh in range(2):
             to = pl.ds(pl.multiple_of(row + 640 * zh, 320), 320)
             lower[to, :] = blocks[n][zh * 320 : zh * 320 + 320, :]
@@ -232,7 +226,7 @@
 
             @pl.when(ks == k)
             def _():
-                hold[o] = blocks[2 * k + o][0:640, :]
+                hold[o] = blocks[2 * ORDER[k] + o][0:640, :]
 
     order = [rank_order(ids, h, 64) for h in range(2)]
     for k in (1, 2, 3, 0):
@@ -256,15 +250,15 @@
                     out[k, zz ^ z, at] = (ref[:, cols].astype(F32) + mm_t(low[at, :], u)).astype(BF)
 
 
-def project_kernel(c0, c1, c2, c3, merged, *out):
-    for n in (3, 2, 1, 0):
+def project_kernel(order, c0, c1, c3, c2, merged, *out):
+    for n, ref_out in zip(order, out):
         total = mm(c0[...], merged[0, n])
         for k, ref in ((1, c1), (2, c2), (3, c3)):
             total = total + mm(ref[...], merged[k, n])
         total = total.astype(BF)
-        out[n][0:256] = total[:, 0:128]
-        out[n][256:512] = total[:, 128:256]
-        out[n][512:640] = jnp.concatenate([total[0:128, 256:320], total[128:256, 256:320]], axis=1)
+        ref_out[0:256] = total[:, 0:128]
+        ref_out[256:512] = total[:, 128:256]
+        ref_out[512:640] = jnp.concatenate([total[0:128, 256:320], total[128:256, 256:320]], axis=1)
 
 
 def sum_kernel(p0, p1, p2, p3, out):
@@ -311,14 +305,6 @@
     messages = pl.pallas_call(
         pack_kernel,
         out_shape=array(32, MSG, 128),
-        in_specs=[hbm] * 4,
-        scratch_shapes=[
-            pltpu.VMEM((20, 64), BF),
-            pltpu.VMEM((20, 64), BF),
-            pltpu.VMEM((4, 256), BF),
-            pltpu.VMEM((4, 256), BF),
-            pltpu.SemaphoreType.DMA((4,)),
-        ],
         compiler_params=params(4),
         name="pack",
     )(*(far(a) for a in (qa_low, oa_up, qa_up, oa_low)))
@@ -355,7 +341,7 @@
     mine, w_sent, new_kv = lax.optimization_barrier((mine, w_sent, new_kv))
     w_first = lax.ppermute(w_sent[0], "y", ring(1))
     w_third = lax.ppermute(w_sent[2], "y", ring(3))
-    parts = [mine] + [lax.ppermute(mine, "x", partner(s)) for s in (1, 2, 3)]
+    parts = [mine] + [lax.ppermute(mine, "x", partner(s)) for s in ORDER[1:]]
     w_first, w_third, w_second = lax.optimization_barrier((w_first, w_third, w_sent[1]))
     w_same = [w_first, lax.ppermute(w_second, "y", ring(2)), w_third]
     blocks = []
@@ -402,14 +388,17 @@
         cost_estimate=pl.CostEstimate(flops=340_000_000, bytes_accessed=8_000_000, transcendentals=0),
         name="merge_o",
     )(ids, *blocks, far(wo), *w_same, *w_other)
-    sums = pl.pallas_call(
-        project_kernel,
-        out_shape=(array(640, 128),) * 4,
-        compiler_params=params(16),
-        cost_estimate=pl.CostEstimate(flops=680_000_000, bytes_accessed=4_000_000, transcendentals=0),
-        name="project",
-    )(ctx, others[1], others[2], others[3], merged)
-    came = [lax.ppermute(sums[n], "z", partner(n)) for n in (3, 2, 1)]
+    sums = {}
+    for order in ((2, 1), (3, 0)):
+        both = pl.pallas_call(
+            functools.partial(project_kernel, order),
+            out_shape=(array(640, 128),) * 2,
+            compiler_params=params(16),
+            cost_estimate=pl.CostEstimate(flops=340_000_000, bytes_accessed=4_000_000, transcendentals=0),
+            name="project",
+        )(ctx, others[1], others[3], others[2], merged)
+        sums.update(zip(order, both))
+    came = [lax.ppermute(sums[n], "z", partner(n)) for n in (2, 1, 3)]
     return pl.pallas_call(
         sum_kernel,
         out_shape=array(4, 64, 320),

time: 84.5 us -> 82.4 us (0.975)
  the two profiles are of different devices: /device:TPU:2 before, /device:TPU:32 now
where the time goes in v5:
time: 82.4 us; the launch traced here: 81.8 us
  starting transfers between devices  38.1 us (46%)
  waiting for transfers between devices  23.4 us (28%)
  Pallas kernels  20.1 us (24%)
    all_to_all x1, starting transfers between devices, local(): got = lax.all_to_all(messages, ('zh', 'y', 'z'), 0, 0, tiled=True)  11.4 us
    ppermute x3, waiting for transfers between devices, local(): came = [lax.ppermute(sums[n], 'z', partner(n)) for n in (2, 1, 3)]  11.2 us
    ppermute x4, starting transfers between devices, local(): new_kv = [lax.ppermute(kv_t, TP, kv_pairs(k)) for k in range(4)]  9.64 us
    pallas_call x1, Pallas kernels, local(): pl.pallas_call(attend_kernel, out_shape=array(ROWS, 256), in_specs=[SMEM]...  7.49 us
    pallas_call x1, Pallas kernels, local(): pl.pallas_call(norm_kernel, out_shape=(pltpu.HBM((10, ROWS, 512), BF), ar...  4.27 us
    ppermute x3, starting transfers between devices, local(): parts = [mine] + [lax.ppermute(mine, 'x', partner(s)) for s in ORDER[1:]]  4.22 us
    ppermute x3, starting transfers between devices, local(): came = [lax.ppermute(sums[n], 'z', partner(n)) for n in (2, 1, 3)]  3.66 us
    pallas_call x1, Pallas kernels, local(): pl.pallas_call(merge_o_kernel, out_shape=array(4, 4, 256, 320), in_specs=...  3.52 us
  transfers between devices with their start and end apart: 24, of which 11 were waited for; matrix products, arithmetic and copies ran while one was open for 0% of the time, Pallas kernels for 21%

profile of v5, /device:TPU:32, one launch (start us, length us, event | category | flops | bytes accessed | tf_op | source)
XLA Modules:
  0.0 81.8 jit_solution(400732452670754239)
XLA Ops:
  0.0 1.7 %pack.1 = bf16[32,48,128]{2,1,0:T(8,128)(2,1)} custom-call(bf16[20,64]{1,0:T(8,128)(2,1)} %low.1, bf16[20,64]{1,0:T(8,128)(2,1)} %up.1, bf16[4,256]{1,0:T(4,128)(2,1)} %q_up.1, bf16[4,256]{1,0:T(4,128)(2,1)} %o_low.1), custom_call_target="tpu_custom_call" | custom-call | tf_op jit(solution)/shard_map/pack/pallas_call | solution.py:305
  1.7 11.4 %all-to-all-start = ((bf16[32,48,128]{2,1,0:T(8,128)(2,1)}), bf16[32,48,128]{2,1,0:T(8,128)(2,1)S(1)}, u32[]{:S(2)}, u32[]{:S(2)}) async-start(bf16[32,48,128]{2,1,0:T(8,128)(2,1)} %pack.1), calls=%async_computation | async-start | bytes 786432 | tf_op jit(solution)/shard_map/all_to_all | solution.py:311
  13.2 4.3 %norm_kv.1 = (bf16[10,256,512]{2,1,0:T(8,128)(2,1)}, bf16[64,256]{1,0:T(8,128)(2,1)S(1)}, bf16[128,1280]{1,0:T(8,128)(2,1)}, bf16[128,1280]{1,0:T(8,128)(2,1)}, bf16[128,1280]{1,0:T(8,128)(2,1)}) custom-call(s32[5]{0:T(128)S(1)} %stack.23.ids, bf16[4,64,5120]{2,1,0:T(8,128)(2,1)} %states.1, bf16[64,5120]{1,0:T(8,128)(2,1)} %bitcast.6, bf16[256,5120]{1,0:T(8,128)(2,1)} %refs_8_.3), custom_call_target="tpu_custom_call" | custom-call | flops 170000000 | bytes 8000000 | tf_op jit(solution)/shard_map/norm_kv/pallas_call | solution.py:313
  17.5 0.7 collective-permute-start
  18.4 6.3 %collective-permute-start.2 = (bf16[64,256]{1,0:T(8,128)(2,1)S(1)}, bf16[64,256]{1,0:T(8,128)(2,1)S(1)}, u32[]{:S(2)}, u32[]{:S(2)}) collective-permute-start(bf16[64,256]{1,0:T(8,128)(2,1)S(1)} %get-tuple-element.31), channel_id=1, source_target_pairs={{0,2},{1,3},{2,6},{3,7},{4,10},{5,11},{6,14},{7,15},{8,0},{9,1},{1... | collective-permute-start | bytes 98312 | tf_op jit(solution)/shard_map/ppermute | solution.py:330
  24.7 2.4 %collective-permute-start.3 = (bf16[64,256]{1,0:T(8,128)(2,1)S(1)}, bf16[64,256]{1,0:T(8,128)(2,1)S(1)}, u32[]{:S(2)}, u32[]{:S(2)}) collective-permute-start(bf16[64,256]{1,0:T(8,128)(2,1)S(1)} %get-tuple-element.31), channel_id=1, source_target_pairs={{0,3},{1,2},{2,7},{3,6},{4,11},{5,10},{6,15},{7,14},{8,1},{9,0},{1... | collective-permute-start | bytes 98312 | tf_op jit(solution)/shard_map/ppermute | solution.py:330
  27.1 0.5 all-to-all-done.got
  27.6 0.8 sort_rows.1.refs_0_
  28.5 2.6 %collective-permute-done.3.refs_15_ = bf16[64,256]{1,0:T(8,128)(2,1)S(1)} collective-permute-done((bf16[64,256]{1,0:T(8,128)(2,1)S(1)}, bf16[64,256]{1,0:T(8,128)(2,1)S(1)}, u32[]{:S(2)}, u32[]{:S(2)}) %collective-permute-start.3) | collective-permute-done | bytes 32800 | tf_op jit(solution)/shard_map/ppermute | solution.py:330
  31.1 0.6 collective-permute-start.14
  31.6 2.7 %collective-permute-start.15 = (bf16[128,1280]{1,0:T(8,128)(2,1)}, bf16[128,1280]{1,0:T(8,128)(2,1)S(1)}, u32[]{:S(2)}, u32[]{:S(2)}) collective-permute-start(bf16[128,1280]{1,0:T(8,128)(2,1)} %get-tuple-element.43), channel_id=1, source_target_pairs={{0,12},{4,0},{8,4},{12,8},{1,13},{5,1},{9,5},{13,9},{2,14},{6,2},{... | collective-permute-start | bytes 983048 | tf_op jit(solution)/shard_map/ppermute | solution.py:343
  34.3 1.5 %collective-permute-start.9 = (bf16[720,128]{1,0:T(8,128)(2,1)S(1)}, bf16[720,128]{1,0:T(8,128)(2,1)S(1)}, u32[]{:S(2)}, u32[]{:S(2)}) collective-permute-start(bf16[720,128]{1,0:T(8,128)(2,1)S(1)} %sort_rows.1.refs_0_), channel_id=1, source_target_pairs={{0,64},{64,0},{128,192},{192,128},{1,65},{65,1},{129,193},{193,129... | collective-permute-start | bytes 552968 | tf_op jit(solution)/shard_map/ppermute | solution.py:344
  35.8 2.1 %collective-permute-start.5 = (bf16[720,128]{1,0:T(8,128)(2,1)S(1)}, bf16[720,128]{1,0:T(8,128)(2,1)S(1)}, u32[]{:S(2)}, u32[]{:S(2)}) collective-permute-start(bf16[720,128]{1,0:T(8,128)(2,1)S(1)} %sort_rows.1.refs_0_), channel_id=1, source_target_pairs={{0,192},{64,128},{128,64},{192,0},{1,193},{65,129},{129,65},{193,1... | collective-permute-start | bytes 552968 | tf_op jit(solution)/shard_map/ppermute | solution.py:344
  37.9 0.6 collective-permute-start.7
  38.5 1.0 %collective-permute-done.14.refs_9_ = bf16[128,1280]{1,0:T(8,128)(2,1)S(1)} collective-permute-done((bf16[128,1280]{1,0:T(8,128)(2,1)}, bf16[128,1280]{1,0:T(8,128)(2,1)S(1)}, u32[]{:S(2)}, u32[]{:S(2)}) %collective-permute-start.14) | collective-permute-done | bytes 327712 | tf_op jit(solution)/shard_map/ppermute | solution.py:342
  39.6 1.5 %collective-permute-start.16 = (bf16[128,1280]{1,0:T(8,128)(2,1)}, bf16[128,1280]{1,0:T(8,128)(2,1)S(1)}, u32[]{:S(2)}, u32[]{:S(2)}) collective-permute-start(bf16[128,1280]{1,0:T(8,128)(2,1)} %get-tuple-element.46), channel_id=1, source_target_pairs={{0,8},{4,12},{8,0},{12,4},{1,9},{5,13},{9,1},{13,5},{2,10},{6,14},... | collective-permute-start | bytes 983048 | tf_op jit(solution)/shard_map/ppermute | solution.py:346
  41.0 0.5 collective-permute-start.10
  41.5 1.4 %collective-permute-done.5.refs_2_ = bf16[720,128]{1,0:T(8,128)(2,1)S(1)} collective-permute-done((bf16[720,128]{1,0:T(8,128)(2,1)S(1)}, bf16[720,128]{1,0:T(8,128)(2,1)S(1)}, u32[]{:S(2)}, u32[]{:S(2)}) %collective-permute-start.5) | collective-permute-done | bytes 184352 | tf_op jit(solution)/shard_map/ppermute | solution.py:344
  43.0 2.0 %collective-permute-done.7.refs_4_ = bf16[720,128]{1,0:T(8,128)(2,1)S(1)} collective-permute-done((bf16[720,128]{1,0:T(8,128)(2,1)S(1)}, bf16[720,128]{1,0:T(8,128)(2,1)S(1)}, u32[]{:S(2)}, u32[]{:S(2)}) %collective-permute-start.7) | collective-permute-done | bytes 184352 | tf_op jit(solution)/shard_map/ppermute | solution.py:344
  45.0 1.4 %collective-permute-done.8.refs_5_ = bf16[720,128]{1,0:T(8,128)(2,1)S(1)} collective-permute-done((bf16[720,128]{1,0:T(8,128)(2,1)S(1)}, bf16[720,128]{1,0:T(8,128)(2,1)S(1)}, u32[]{:S(2)}, u32[]{:S(2)}) %collective-permute-start.8) | collective-permute-done | bytes 184352 | tf_op jit(solution)/shard_map/ppermute | solution.py:349
  46.4 7.5 %attend.1.c0 = bf16[256,256]{1,0:T(8,128)(2,1)S(1)} custom-call(s32[5]{0:T(128)S(1)} %stack.23.ids, bf16[720,128]{1,0:T(8,128)(2,1)S(1)} %sort_rows.1.refs_0_, bf16[720,128]{1,0:T(8,128)(2,1)S(1)} %collective-permute-done.4.refs_1_, bf16[720,128]{1,0:T(8,128)(2,1)S(1)} %collective-permute-done.5.refs_2_, ...), custom_call_target="tpu_custom_call" | custom-call | flops 1000000000 | bytes 10000000 | tf_op jit(solution)/shard_map/attend/pallas_call | solution.py:351
  54.6 3.2 %collective-permute-start.12 = (bf16[256,256]{1,0:T(8,128)(2,1)S(1)}, bf16[256,256]{1,0:T(8,128)(2,1)S(1)}, u32[]{:S(2)}, u32[]{:S(2)}) collective-permute-start(bf16[256,256]{1,0:T(8,128)(2,1)S(1)} %attend.1.c0), channel_id=1, source_target_pairs={{0,12},{4,0},{8,4},{12,8},{1,13},{5,1},{9,5},{13,9},{2,14},{6,2},{... | collective-permute-start | bytes 393224 | tf_op jit(solution)/shard_map/ppermute | solution.py:374
  57.9 3.5 %merge_o.1.merged = bf16[4,4,256,320]{3,2,1,0:T(8,128)(2,1)S(1)} custom-call(s32[5]{0:T(128)S(1)} %stack.23.ids, bf16[720,128]{1,0:T(8,128)(2,1)S(1)} %sort_rows.1.refs_0_, bf16[720,128]{1,0:T(8,128)(2,1)S(1)} %collective-permute-done.4.refs_1_, bf16[720,128]{1,0:T(8,128)(2,1)S(1)} %collective-permute-done.5.refs_2_, ...), custom_call_target="tpu_custom_call" | custom-call | flops 340000000 | bytes 8000000 | tf_op jit(solution)/shard_map/merge_o/pallas_call | solution.py:377
  61.6 2.1 %collective-permute-done.12.c3 = bf16[256,256]{1,0:T(8,128)(2,1)S(1)} collective-permute-done((bf16[256,256]{1,0:T(8,128)(2,1)S(1)}, bf16[256,256]{1,0:T(8,128)(2,1)S(1)}, u32[]{:S(2)}, u32[]{:S(2)}) %collective-permute-start.12) | collective-permute-done | bytes 131104 | tf_op jit(solution)/shard_map/ppermute | solution.py:374
  63.7 0.9 %collective-permute-done.13.c2 = bf16[256,256]{1,0:T(8,128)(2,1)S(1)} collective-permute-done((bf16[256,256]{1,0:T(8,128)(2,1)S(1)}, bf16[256,256]{1,0:T(8,128)(2,1)S(1)}, u32[]{:S(2)}, u32[]{:S(2)}) %collective-permute-start.13) | collective-permute-done | bytes 131104 | tf_op jit(solution)/shard_map/ppermute | solution.py:374
  64.6 0.8 project.3
  65.3 2.7 %collective-permute-start.20 = (bf16[640,128]{1,0:T(8,128)(2,1)S(1)}, bf16[640,128]{1,0:T(8,128)(2,1)S(1)}, u32[]{:S(2)}, u32[]{:S(2)}) collective-permute-start(bf16[640,128]{1,0:T(8,128)(2,1)S(1)} %get-tuple-element.52), channel_id=1, source_target_pairs={{0,2},{1,3},{2,0},{3,1},{4,6},{5,7},{6,4},{7,5},{8,10},{9,11},{10,... | collective-permute-start | bytes 491528 | tf_op jit(solution)/shard_map/ppermute | solution.py:401
  68.1 0.8 project.2
  68.9 0.9 %collective-permute-start.22 = (bf16[640,128]{1,0:T(8,128)(2,1)S(1)}, bf16[640,128]{1,0:T(8,128)(2,1)S(1)}, u32[]{:S(2)}, u32[]{:S(2)}) collective-permute-start(bf16[640,128]{1,0:T(8,128)(2,1)S(1)} %get-tuple-element.54), channel_id=1, source_target_pairs={{0,3},{1,2},{2,1},{3,0},{4,7},{5,6},{6,5},{7,4},{8,11},{9,10},{10,... | collective-permute-start | bytes 491528 | tf_op jit(solution)/shard_map/ppermute | solution.py:401
  69.8 7.2 %collective-permute-done.20.p1 = bf16[640,128]{1,0:T(8,128)(2,1)S(1)} collective-permute-done((bf16[640,128]{1,0:T(8,128)(2,1)S(1)}, bf16[640,128]{1,0:T(8,128)(2,1)S(1)}, u32[]{:S(2)}, u32[]{:S(2)}) %collective-permute-start.20) | collective-permute-done | bytes 163872 | tf_op jit(solution)/shard_map/ppermute | solution.py:401
  77.0 4.1 %collective-permute-done.22.p3 = bf16[640,128]{1,0:T(8,128)(2,1)S(1)} collective-permute-done((bf16[640,128]{1,0:T(8,128)(2,1)S(1)}, bf16[640,128]{1,0:T(8,128)(2,1)S(1)}, u32[]{:S(2)}, u32[]{:S(2)}) %collective-permute-start.22) | collective-permute-done | bytes 163872 | tf_op jit(solution)/shard_map/ppermute | solution.py:401
  81.0 0.8 sum_parts.1
  (29 shorter events, 1.4 us)
Async XLA Ops:
  1.7 25.9 %all-to-all-start = ((bf16[32,48,128]{2,1,0:T(8,128)(2,1)}), bf16[32,48,128]{2,1,0:T(8,128)(2,1)S(1)}, u32[]{:S(2)}, u32[]{:S(2)}) async-start(bf16[32,48,128]{2,1,0:T(8,128)(2,1)} %pack.1), calls=%async_computation | async-start | bytes 786432 | tf_op jit(solution)/shard_map/all_to_all | solution.py:311
  13.2 33.2 %copy-start = (bf16[5120,256]{1,0:T(8,128)(2,1)S(1)}, bf16[5120,256]{1,0:T(8,128)(2,1)}, u32[]{:S(2)}) copy-start(bf16[5120,256]{1,0:T(8,128)(2,1)} %refs_8_.2) | copy-start | bytes 7864324
  13.2 33.2 %copy-start.1 = (s32[64]{0:T(128)S(1)}, s32[64]{0:T(128)}, u32[]{:S(2)}) copy-start(s32[64]{0:T(128)} %refs_16_.1) | copy-start | bytes 772
  17.5 11.0 %collective-permute-start = (bf16[64,256]{1,0:T(8,128)(2,1)S(1)}, bf16[64,256]{1,0:T(8,128)(2,1)S(1)}, u32[]{:S(2)}, u32[]{:S(2)}) collective-permute-start(bf16[64,256]{1,0:T(8,128)(2,1)S(1)} %get-tuple-element.31), channel_id=1, source_target_pairs={{0,0},{1,1},{2,4},{3,5},{4,8},{5,9},{6,12},{7,13},{8,2},{9,3},{10,... | collective-permute-start | bytes 98312 | tf_op jit(solution)/shard_map/ppermute | solution.py:330
  18.1 10.3 %collective-permute-start.1 = (bf16[64,256]{1,0:T(8,128)(2,1)S(1)}, bf16[64,256]{1,0:T(8,128)(2,1)S(1)}, u32[]{:S(2)}, u32[]{:S(2)}) collective-permute-start(bf16[64,256]{1,0:T(8,128)(2,1)S(1)} %get-tuple-element.31), channel_id=1, source_target_pairs={{0,1},{1,0},{2,5},{3,4},{4,9},{5,8},{6,13},{7,12},{8,3},{9,2},{10,... | collective-permute-start | bytes 98312 | tf_op jit(solution)/shard_map/ppermute | solution.py:330
  18.4 10.0 %collective-permute-start.2 = (bf16[64,256]{1,0:T(8,128)(2,1)S(1)}, bf16[64,256]{1,0:T(8,128)(2,1)S(1)}, u32[]{:S(2)}, u32[]{:S(2)}) collective-permute-start(bf16[64,256]{1,0:T(8,128)(2,1)S(1)} %get-tuple-element.31), channel_id=1, source_target_pairs={{0,2},{1,3},{2,6},{3,7},{4,10},{5,11},{6,14},{7,15},{8,0},{9,1},{1... | collective-permute-start | bytes 98312 | tf_op jit(solution)/shard_map/ppermute | solution.py:330
  24.7 6.3 %collective-permute-start.3 = (bf16[64,256]{1,0:T(8,128)(2,1)S(1)}, bf16[64,256]{1,0:T(8,128)(2,1)S(1)}, u32[]{:S(2)}, u32[]{:S(2)}) collective-permute-start(bf16[64,256]{1,0:T(8,128)(2,1)S(1)} %get-tuple-element.31), channel_id=1, source_target_pairs={{0,3},{1,2},{2,7},{3,6},{4,11},{5,10},{6,15},{7,14},{8,1},{9,0},{1... | collective-permute-start | bytes 98312 | tf_op jit(solution)/shard_map/ppermute | solution.py:330
  31.1 8.5 %collective-permute-start.14 = (bf16[128,1280]{1,0:T(8,128)(2,1)}, bf16[128,1280]{1,0:T(8,128)(2,1)S(1)}, u32[]{:S(2)}, u32[]{:S(2)}) collective-permute-start(bf16[128,1280]{1,0:T(8,128)(2,1)} %get-tuple-element.42), channel_id=1, source_target_pairs={{0,4},{4,8},{8,12},{12,0},{1,5},{5,9},{9,13},{13,1},{2,6},{6,10},{... | collective-permute-start | bytes 983048 | tf_op jit(solution)/shard_map/ppermute | solution.py:342
  31.6 7.9 %collective-permute-start.15 = (bf16[128,1280]{1,0:T(8,128)(2,1)}, bf16[128,1280]{1,0:T(8,128)(2,1)S(1)}, u32[]{:S(2)}, u32[]{:S(2)}) collective-permute-start(bf16[128,1280]{1,0:T(8,128)(2,1)} %get-tuple-element.43), channel_id=1, source_target_pairs={{0,12},{4,0},{8,4},{12,8},{1,13},{5,1},{9,5},{13,9},{2,14},{6,2},{... | collective-permute-start | bytes 983048 | tf_op jit(solution)/shard_map/ppermute | solution.py:343
  34.3 6.7 %collective-permute-start.9 = (bf16[720,128]{1,0:T(8,128)(2,1)S(1)}, bf16[720,128]{1,0:T(8,128)(2,1)S(1)}, u32[]{:S(2)}, u32[]{:S(2)}) collective-permute-start(bf16[720,128]{1,0:T(8,128)(2,1)S(1)} %sort_rows.1.refs_0_), channel_id=1, source_target_pairs={{0,64},{64,0},{128,192},{192,128},{1,65},{65,1},{129,193},{193,129... | collective-permute-start | bytes 552968 | tf_op jit(solution)/shard_map/ppermute | solution.py:344
  35.8 7.2 %collective-permute-start.5 = (bf16[720,128]{1,0:T(8,128)(2,1)S(1)}, bf16[720,128]{1,0:T(8,128)(2,1)S(1)}, u32[]{:S(2)}, u32[]{:S(2)}) collective-permute-start(bf16[720,128]{1,0:T(8,128)(2,1)S(1)} %sort_rows.1.refs_0_), channel_id=1, source_target_pairs={{0,192},{64,128},{128,64},{192,0},{1,193},{65,129},{129,65},{193,1... | collective-permute-start | bytes 552968 | tf_op jit(solution)/shard_map/ppermute | solution.py:344
  37.9 7.0 %collective-permute-start.7 = (bf16[720,128]{1,0:T(8,128)(2,1)S(1)}, bf16[720,128]{1,0:T(8,128)(2,1)S(1)}, u32[]{:S(2)}, u32[]{:S(2)}) collective-permute-start(bf16[720,128]{1,0:T(8,128)(2,1)S(1)} %sort_rows.1.refs_0_), channel_id=1, source_target_pairs={{0,128},{64,192},{128,0},{192,64},{1,129},{65,193},{129,1},{193,65... | collective-permute-start | bytes 552968 | tf_op jit(solution)/shard_map/ppermute | solution.py:344
  39.6 14.3 %collective-permute-start.16 = (bf16[128,1280]{1,0:T(8,128)(2,1)}, bf16[128,1280]{1,0:T(8,128)(2,1)S(1)}, u32[]{:S(2)}, u32[]{:S(2)}) collective-permute-start(bf16[128,1280]{1,0:T(8,128)(2,1)} %get-tuple-element.46), channel_id=1, source_target_pairs={{0,8},{4,12},{8,0},{12,4},{1,9},{5,13},{9,1},{13,5},{2,10},{6,14},... | collective-permute-start | bytes 983048 | tf_op jit(solution)/shard_map/ppermute | solution.py:346
  41.0 3.9 %collective-permute-start.4 = (bf16[720,128]{1,0:T(8,128)(2,1)S(1)}, bf16[720,128]{1,0:T(8,128)(2,1)S(1)}, u32[]{:S(2)}, u32[]{:S(2)}) collective-permute-start(bf16[720,128]{1,0:T(8,128)(2,1)S(1)} %sort_rows.1.refs_0_), channel_id=1, source_target_pairs={{0,16},{16,0},{1,17},{17,1},{2,18},{18,2},{3,19},{19,3},{4,20},{20... | collective-permute-start | bytes 552968 | tf_op jit(solution)/shard_map/ppermute | solution.py:349
  41.0 3.9 %collective-permute-start.10 = (bf16[720,128]{1,0:T(8,128)(2,1)S(1)}, bf16[720,128]{1,0:T(8,128)(2,1)S(1)}, u32[]{:S(2)}, u32[]{:S(2)}) collective-permute-start(bf16[720,128]{1,0:T(8,128)(2,1)S(1)} %collective-permute-done.9.refs_6_), channel_id=1, source_target_pairs={{0,16},{16,0},{1,17},{17,1},{2,18},{18,2},{3,19},{19,3},{4,20},{20... | collective-permute-start | bytes 552968 | tf_op jit(solution)/shard_map/ppermute | solution.py:349
  43.0 2.0 %collective-permute-start.6 = (bf16[720,128]{1,0:T(8,128)(2,1)S(1)}, bf16[720,128]{1,0:T(8,128)(2,1)S(1)}, u32[]{:S(2)}, u32[]{:S(2)}) collective-permute-start(bf16[720,128]{1,0:T(8,128)(2,1)S(1)} %collective-permute-done.5.refs_2_), channel_id=1, source_target_pairs={{0,16},{16,0},{1,17},{17,1},{2,18},{18,2},{3,19},{19,3},{4,20},{20... | collective-permute-start | bytes 552968 | tf_op jit(solution)/shard_map/ppermute | solution.py:349
  44.9 1.4 %collective-permute-start.8 = (bf16[720,128]{1,0:T(8,128)(2,1)S(1)}, bf16[720,128]{1,0:T(8,128)(2,1)S(1)}, u32[]{:S(2)}, u32[]{:S(2)}) collective-permute-start(bf16[720,128]{1,0:T(8,128)(2,1)S(1)} %collective-permute-done.7.refs_4_), channel_id=1, source_target_pairs={{0,16},{16,0},{1,17},{17,1},{2,18},{18,2},{3,19},{19,3},{4,20},{20... | collective-permute-start | bytes 552968 | tf_op jit(solution)/shard_map/ppermute | solution.py:349
  53.9 4.0 %collective-permute-start.17 = (bf16[128,1280]{1,0:T(8,128)(2,1)S(1)}, bf16[128,1280]{1,0:T(8,128)(2,1)S(1)}, u32[]{:S(2)}, u32[]{:S(2)}) collective-permute-start(bf16[128,1280]{1,0:T(8,128)(2,1)S(1)} %collective-permute-done.14.refs_9_), channel_id=1, source_target_pairs={{0,16},{16,0},{1,17},{17,1},{2,18},{18,2},{3,19},{19,3},{4,20},{20... | collective-permute-start | bytes 983048 | tf_op jit(solution)/shard_map/ppermute | solution.py:376
  54.1 3.8 %collective-permute-start.18 = (bf16[128,1280]{1,0:T(8,128)(2,1)S(1)}, bf16[128,1280]{1,0:T(8,128)(2,1)S(1)}, u32[]{:S(2)}, u32[]{:S(2)}) collective-permute-start(bf16[128,1280]{1,0:T(8,128)(2,1)S(1)} %collective-permute-done.16.refs_10_), channel_id=1, source_target_pairs={{0,16},{16,0},{1,17},{17,1},{2,18},{18,2},{3,19},{19,3},{4,20},{20... | collective-permute-start | bytes 983048 | tf_op jit(solution)/shard_map/ppermute | solution.py:376
  54.5 3.4 %collective-permute-start.19 = (bf16[128,1280]{1,0:T(8,128)(2,1)S(1)}, bf16[128,1280]{1,0:T(8,128)(2,1)S(1)}, u32[]{:S(2)}, u32[]{:S(2)}) collective-permute-start(bf16[128,1280]{1,0:T(8,128)(2,1)S(1)} %collective-permute-done.15.refs_11_), channel_id=1, source_target_pairs={{0,16},{16,0},{1,17},{17,1},{2,18},{18,2},{3,19},{19,3},{4,20},{20... | collective-permute-start | bytes 983048 | tf_op jit(solution)/shard_map/ppermute | solution.py:376
  54.6 7.0 %collective-permute-start.11 = (bf16[256,256]{1,0:T(8,128)(2,1)S(1)}, bf16[256,256]{1,0:T(8,128)(2,1)S(1)}, u32[]{:S(2)}, u32[]{:S(2)}) collective-permute-start(bf16[256,256]{1,0:T(8,128)(2,1)S(1)} %attend.1.c0), channel_id=1, source_target_pairs={{0,4},{4,8},{8,12},{12,0},{1,5},{5,9},{9,13},{13,1},{2,6},{6,10},{... | collective-permute-start | bytes 393224 | tf_op jit(solution)/shard_map/ppermute | solution.py:374
  54.6 9.1 %collective-permute-start.12 = (bf16[256,256]{1,0:T(8,128)(2,1)S(1)}, bf16[256,256]{1,0:T(8,128)(2,1)S(1)}, u32[]{:S(2)}, u32[]{:S(2)}) collective-permute-start(bf16[256,256]{1,0:T(8,128)(2,1)S(1)} %attend.1.c0), channel_id=1, source_target_pairs={{0,12},{4,0},{8,4},{12,8},{1,13},{5,1},{9,5},{13,9},{2,14},{6,2},{... | collective-permute-start | bytes 393224 | tf_op jit(solution)/shard_map/ppermute | solution.py:374
  57.9 6.7 %collective-permute-start.13 = (bf16[256,256]{1,0:T(8,128)(2,1)S(1)}, bf16[256,256]{1,0:T(8,128)(2,1)S(1)}, u32[]{:S(2)}, u32[]{:S(2)}) collective-permute-start(bf16[256,256]{1,0:T(8,128)(2,1)S(1)} %attend.1.c0), channel_id=1, source_target_pairs={{0,8},{4,12},{8,0},{12,4},{1,9},{5,13},{9,1},{13,5},{2,10},{6,14},... | collective-permute-start | bytes 393224 | tf_op jit(solution)/shard_map/ppermute | solution.py:374
  65.3 11.6 %collective-permute-start.20 = (bf16[640,128]{1,0:T(8,128)(2,1)S(1)}, bf16[640,128]{1,0:T(8,128)(2,1)S(1)}, u32[]{:S(2)}, u32[]{:S(2)}) collective-permute-start(bf16[640,128]{1,0:T(8,128)(2,1)S(1)} %get-tuple-element.52), channel_id=1, source_target_pairs={{0,2},{1,3},{2,0},{3,1},{4,6},{5,7},{6,4},{7,5},{8,10},{9,11},{10,... | collective-permute-start | bytes 491528 | tf_op jit(solution)/shard_map/ppermute | solution.py:401
  68.1 8.9 %collective-permute-start.21 = (bf16[640,128]{1,0:T(8,128)(2,1)S(1)}, bf16[640,128]{1,0:T(8,128)(2,1)S(1)}, u32[]{:S(2)}, u32[]{:S(2)}) collective-permute-start(bf16[640,128]{1,0:T(8,128)(2,1)S(1)} %get-tuple-element.53), channel_id=1, source_target_pairs={{0,1},{1,0},{2,3},{3,2},{4,5},{5,4},{6,7},{7,6},{8,9},{9,8},{10,11... | collective-permute-start | bytes 491528 | tf_op jit(solution)/shard_map/ppermute | solution.py:401
  68.9 12.2 %collective-permute-start.22 = (bf16[640,128]{1,0:T(8,128)(2,1)S(1)}, bf16[640,128]{1,0:T(8,128)(2,1)S(1)}, u32[]{:S(2)}, u32[]{:S(2)}) collective-permute-start(bf16[640,128]{1,0:T(8,128)(2,1)S(1)} %get-tuple-element.54), channel_id=1, source_target_pairs={{0,3},{1,2},{2,1},{3,0},{4,7},{5,6},{6,5},{7,4},{8,11},{9,10},{10,... | collective-permute-start | bytes 491528 | tf_op jit(solution)/shard_map/ppermute | solution.py:401

commit v6 on v5

--- a/solution.py
+++ b/solution.py
@@ -250,11 +250,14 @@
                     out[k, zz ^ z, at] = (ref[:, cols].astype(F32) + mm_t(low[at, :], u)).astype(BF)
 
 
-def project_kernel(order, c0, c1, c3, c2, merged, *out):
+def begin_kernel(c0, c1, merged, out):
+    for n in range(4):
+        out[n] = mm(c0[...], merged[0, n]) + mm(c1[...], merged[1, n])
+
+
+def project_kernel(order, c3, c2, merged, begun, *out):
     for n, ref_out in zip(order, out):
-        total = mm(c0[...], merged[0, n])
-        for k, ref in ((1, c1), (2, c2), (3, c3)):
-            total = total + mm(ref[...], merged[k, n])
+        total = begun[n] + mm(c3[...], merged[3, n]) + mm(c2[...], merged[2, n])
         total = total.astype(BF)
         ref_out[0:256] = total[:, 0:128]
         ref_out[256:512] = total[:, 128:256]
@@ -388,6 +391,13 @@
         cost_estimate=pl.CostEstimate(flops=340_000_000, bytes_accessed=8_000_000, transcendentals=0),
         name="merge_o",
     )(ids, *blocks, far(wo), *w_same, *w_other)
+    begun = pl.pallas_call(
+        begin_kernel,
+        out_shape=jax.ShapeDtypeStruct((4, ROWS, 320), F32),
+        compiler_params=params(16),
+        cost_estimate=pl.CostEstimate(flops=340_000_000, bytes_accessed=4_000_000, transcendentals=0),
+        name="begin",
+    )(ctx, others[1], merged)
     sums = {}
     for order in ((2, 1), (3, 0)):
         both = pl.pallas_call(
@@ -396,7 +406,7 @@
             compiler_params=params(16),
             cost_estimate=pl.CostEstimate(flops=340_000_000, bytes_accessed=4_000_000, transcendentals=0),
             name="project",
-        )(ctx, others[1], others[3], others[2], merged)
+        )(others[3], others[2], merged, begun)
         sums.update(zip(order, both))
     came = [lax.ppermute(sums[n], "z", partner(n)) for n in (2, 1, 3)]
     return pl.pallas_call(

time: 82.4 us -> 82.2 us (level)
  no operation moved by 1% of the time
where the time goes in v6:
time: 82.2 us; the launch traced here: 81.5 us
  starting transfers between devices  38.1 us (46%)
  waiting for transfers between devices  22.9 us (28%)
  Pallas kernels  20.3 us (25%)
    ppermute x3, waiting for transfers between devices, local(): came = [lax.ppermute(sums[n], 'z', partner(n)) for n in (2, 1, 3)]  11.5 us
    all_to_all x1, starting transfers between devices, local(): got = lax.all_to_all(messages, ('zh', 'y', 'z'), 0, 0, tiled=True)  11.4 us
    ppermute x4, starting transfers between devices, local(): new_kv = [lax.ppermute(kv_t, TP, kv_pairs(k)) for k in range(4)]  9.64 us
    pallas_call x1, Pallas kernels, local(): pl.pallas_call(attend_kernel, out_shape=array(ROWS, 256), in_specs=[SMEM]...  7.49 us
    pallas_call x1, Pallas kernels, local(): pl.pallas_call(norm_kernel, out_shape=(pltpu.HBM((10, ROWS, 512), BF), ar...  4.27 us
    ppermute x3, starting transfers between devices, local(): parts = [mine] + [lax.ppermute(mine, 'x', partner(s)) for s in ORDER[1:]]  4.22 us
    ppermute x3, starting transfers between devices, local(): came = [lax.ppermute(sums[n], 'z', partner(n)) for n in (2, 1, 3)]  3.66 us
    pallas_call x1, Pallas kernels, local(): pl.pallas_call(merge_o_kernel, out_shape=array(4, 4, 256, 320), in_specs=...  3.52 us
  transfers between devices with their start and end apart: 24, of which 11 were waited for; matrix products, arithmetic and copies ran while one was open for 0% of the time, Pallas kernels for 21%

profile of v6, /device:TPU:32, one launch (start us, length us, event | category | flops | bytes accessed | tf_op | source)
XLA Modules:
  0.0 81.5 jit_solution(6094033271347022098)
XLA Ops:
  0.0 1.7 %pack.1 = bf16[32,48,128]{2,1,0:T(8,128)(2,1)} custom-call(bf16[20,64]{1,0:T(8,128)(2,1)} %low.1, bf16[20,64]{1,0:T(8,128)(2,1)} %up.1, bf16[4,256]{1,0:T(4,128)(2,1)} %q_up.1, bf16[4,256]{1,0:T(4,128)(2,1)} %o_low.1), custom_call_target="tpu_custom_call" | custom-call | tf_op jit(solution)/shard_map/pack/pallas_call | solution.py:308
  1.7 11.4 %all-to-all-start = ((bf16[32,48,128]{2,1,0:T(8,128)(2,1)}), bf16[32,48,128]{2,1,0:T(8,128)(2,1)S(1)}, u32[]{:S(2)}, u32[]{:S(2)}) async-start(bf16[32,48,128]{2,1,0:T(8,128)(2,1)} %pack.1), calls=%async_computation | async-start | bytes 786432 | tf_op jit(solution)/shard_map/all_to_all | solution.py:314
  13.2 4.3 %norm_kv.1 = (bf16[10,256,512]{2,1,0:T(8,128)(2,1)}, bf16[64,256]{1,0:T(8,128)(2,1)S(1)}, bf16[128,1280]{1,0:T(8,128)(2,1)}, bf16[128,1280]{1,0:T(8,128)(2,1)}, bf16[128,1280]{1,0:T(8,128)(2,1)}) custom-call(s32[5]{0:T(128)S(1)} %stack.23.ids, bf16[4,64,5120]{2,1,0:T(8,128)(2,1)} %states.1, bf16[64,5120]{1,0:T(8,128)(2,1)} %bitcast.6, bf16[256,5120]{1,0:T(8,128)(2,1)} %refs_8_.3), custom_call_target="tpu_custom_call" | custom-call | flops 170000000 | bytes 8000000 | tf_op jit(solution)/shard_map/norm_kv/pallas_call | solution.py:316
  17.5 0.7 collective-permute-start
  18.4 6.3 %collective-permute-start.2 = (bf16[64,256]{1,0:T(8,128)(2,1)S(1)}, bf16[64,256]{1,0:T(8,128)(2,1)S(1)}, u32[]{:S(2)}, u32[]{:S(2)}) collective-permute-start(bf16[64,256]{1,0:T(8,128)(2,1)S(1)} %get-tuple-element.31), channel_id=1, source_target_pairs={{0,2},{1,3},{2,6},{3,7},{4,10},{5,11},{6,14},{7,15},{8,0},{9,1},{1... | collective-permute-start | bytes 98312 | tf_op jit(solution)/shard_map/ppermute | solution.py:333
  24.7 2.4 %collective-permute-start.3 = (bf16[64,256]{1,0:T(8,128)(2,1)S(1)}, bf16[64,256]{1,0:T(8,128)(2,1)S(1)}, u32[]{:S(2)}, u32[]{:S(2)}) collective-permute-start(bf16[64,256]{1,0:T(8,128)(2,1)S(1)} %get-tuple-element.31), channel_id=1, source_target_pairs={{0,3},{1,2},{2,7},{3,6},{4,11},{5,10},{6,15},{7,14},{8,1},{9,0},{1... | collective-permute-start | bytes 98312 | tf_op jit(solution)/shard_map/ppermute | solution.py:333
  27.1 0.5 all-to-all-done.got
  27.6 0.8 sort_rows.1.refs_0_
  28.5 2.6 %collective-permute-done.3.refs_15_ = bf16[64,256]{1,0:T(8,128)(2,1)S(1)} collective-permute-done((bf16[64,256]{1,0:T(8,128)(2,1)S(1)}, bf16[64,256]{1,0:T(8,128)(2,1)S(1)}, u32[]{:S(2)}, u32[]{:S(2)}) %collective-permute-start.3) | collective-permute-done | bytes 32800 | tf_op jit(solution)/shard_map/ppermute | solution.py:333
  31.1 0.6 collective-permute-start.13
  31.6 2.7 %collective-permute-start.14 = (bf16[128,1280]{1,0:T(8,128)(2,1)}, bf16[128,1280]{1,0:T(8,128)(2,1)S(1)}, u32[]{:S(2)}, u32[]{:S(2)}) collective-permute-start(bf16[128,1280]{1,0:T(8,128)(2,1)} %get-tuple-element.43), channel_id=1, source_target_pairs={{0,12},{4,0},{8,4},{12,8},{1,13},{5,1},{9,5},{13,9},{2,14},{6,2},{... | collective-permute-start | bytes 983048 | tf_op jit(solution)/shard_map/ppermute | solution.py:346
  34.3 1.5 %collective-permute-start.9 = (bf16[720,128]{1,0:T(8,128)(2,1)S(1)}, bf16[720,128]{1,0:T(8,128)(2,1)S(1)}, u32[]{:S(2)}, u32[]{:S(2)}) collective-permute-start(bf16[720,128]{1,0:T(8,128)(2,1)S(1)} %sort_rows.1.refs_0_), channel_id=1, source_target_pairs={{0,64},{64,0},{128,192},{192,128},{1,65},{65,1},{129,193},{193,129... | collective-permute-start | bytes 552968 | tf_op jit(solution)/shard_map/ppermute | solution.py:347
  35.8 2.1 %collective-permute-start.5 = (bf16[720,128]{1,0:T(8,128)(2,1)S(1)}, bf16[720,128]{1,0:T(8,128)(2,1)S(1)}, u32[]{:S(2)}, u32[]{:S(2)}) collective-permute-start(bf16[720,128]{1,0:T(8,128)(2,1)S(1)} %sort_rows.1.refs_0_), channel_id=1, source_target_pairs={{0,192},{64,128},{128,64},{192,0},{1,193},{65,129},{129,65},{193,1... | collective-permute-start | bytes 552968 | tf_op jit(solution)/shard_map/ppermute | solution.py:347
  37.9 0.6 collective-permute-start.7
  38.5 1.0 %collective-permute-done.13.refs_9_ = bf16[128,1280]{1,0:T(8,128)(2,1)S(1)} collective-permute-done((bf16[128,1280]{1,0:T(8,128)(2,1)}, bf16[128,1280]{1,0:T(8,128)(2,1)S(1)}, u32[]{:S(2)}, u32[]{:S(2)}) %collective-permute-start.13) | collective-permute-done | bytes 327712 | tf_op jit(solution)/shard_map/ppermute | solution.py:345
  39.6 1.5 %collective-permute-start.15 = (bf16[128,1280]{1,0:T(8,128)(2,1)}, bf16[128,1280]{1,0:T(8,128)(2,1)S(1)}, u32[]{:S(2)}, u32[]{:S(2)}) collective-permute-start(bf16[128,1280]{1,0:T(8,128)(2,1)} %get-tuple-element.46), channel_id=1, source_target_pairs={{0,8},{4,12},{8,0},{12,4},{1,9},{5,13},{9,1},{13,5},{2,10},{6,14},... | collective-permute-start | bytes 983048 | tf_op jit(solution)/shard_map/ppermute | solution.py:349
  41.0 0.5 collective-permute-start.10
  41.5 1.4 %collective-permute-done.5.refs_2_ = bf16[720,128]{1,0:T(8,128)(2,1)S(1)} collective-permute-done((bf16[720,128]{1,0:T(8,128)(2,1)S(1)}, bf16[720,128]{1,0:T(8,128)(2,1)S(1)}, u32[]{:S(2)}, u32[]{:S(2)}) %collective-permute-start.5) | collective-permute-done | bytes 184352 | tf_op jit(solution)/shard_map/ppermute | solution.py:347
  43.0 2.0 %collective-permute-done.7.refs_4_ = bf16[720,128]{1,0:T(8,128)(2,1)S(1)} collective-permute-done((bf16[720,128]{1,0:T(8,128)(2,1)S(1)}, bf16[720,128]{1,0:T(8,128)(2,1)S(1)}, u32[]{:S(2)}, u32[]{:S(2)}) %collective-permute-start.7) | collective-permute-done | bytes 184352 | tf_op jit(solution)/shard_map/ppermute | solution.py:347
  45.0 1.4 %collective-permute-done.8.refs_5_ = bf16[720,128]{1,0:T(8,128)(2,1)S(1)} collective-permute-done((bf16[720,128]{1,0:T(8,128)(2,1)S(1)}, bf16[720,128]{1,0:T(8,128)(2,1)S(1)}, u32[]{:S(2)}, u32[]{:S(2)}) %collective-permute-start.8) | collective-permute-done | bytes 184352 | tf_op jit(solution)/shard_map/ppermute | solution.py:352
  46.4 7.5 %attend.1.c0 = bf16[256,256]{1,0:T(8,128)(2,1)S(1)} custom-call(s32[5]{0:T(128)S(1)} %stack.23.ids, bf16[720,128]{1,0:T(8,128)(2,1)S(1)} %sort_rows.1.refs_0_, bf16[720,128]{1,0:T(8,128)(2,1)S(1)} %collective-permute-done.4.refs_1_, bf16[720,128]{1,0:T(8,128)(2,1)S(1)} %collective-permute-done.5.refs_2_, ...), custom_call_target="tpu_custom_call" | custom-call | flops 1000000000 | bytes 10000000 | tf_op jit(solution)/shard_map/attend/pallas_call | solution.py:354
  54.6 3.2 %collective-permute-start.11 = (bf16[256,256]{1,0:T(8,128)(2,1)S(1)}, bf16[256,256]{1,0:T(8,128)(2,1)S(1)}, u32[]{:S(2)}, u32[]{:S(2)}) collective-permute-start(bf16[256,256]{1,0:T(8,128)(2,1)S(1)} %attend.1.c0), channel_id=1, source_target_pairs={{0,12},{4,0},{8,4},{12,8},{1,13},{5,1},{9,5},{13,9},{2,14},{6,2},{... | collective-permute-start | bytes 393224 | tf_op jit(solution)/shard_map/ppermute | solution.py:377
  57.9 3.5 %merge_o.1.merged = bf16[4,4,256,320]{3,2,1,0:T(8,128)(2,1)S(1)} custom-call(s32[5]{0:T(128)S(1)} %stack.23.ids, bf16[720,128]{1,0:T(8,128)(2,1)S(1)} %sort_rows.1.refs_0_, bf16[720,128]{1,0:T(8,128)(2,1)S(1)} %collective-permute-done.4.refs_1_, bf16[720,128]{1,0:T(8,128)(2,1)S(1)} %collective-permute-done.5.refs_2_, ...), custom_call_target="tpu_custom_call" | custom-call | flops 340000000 | bytes 8000000 | tf_op jit(solution)/shard_map/merge_o/pallas_call | solution.py:380
  61.6 0.7 begin.1.begun
  62.3 1.4 %collective-permute-done.11.c3 = bf16[256,256]{1,0:T(8,128)(2,1)S(1)} collective-permute-done((bf16[256,256]{1,0:T(8,128)(2,1)S(1)}, bf16[256,256]{1,0:T(8,128)(2,1)S(1)}, u32[]{:S(2)}, u32[]{:S(2)}) %collective-permute-start.11) | collective-permute-done | bytes 131104 | tf_op jit(solution)/shard_map/ppermute | solution.py:377
  63.7 0.9 %collective-permute-done.12.c2 = bf16[256,256]{1,0:T(8,128)(2,1)S(1)} collective-permute-done((bf16[256,256]{1,0:T(8,128)(2,1)S(1)}, bf16[256,256]{1,0:T(8,128)(2,1)S(1)}, u32[]{:S(2)}, u32[]{:S(2)}) %collective-permute-start.12) | collective-permute-done | bytes 131104 | tf_op jit(solution)/shard_map/ppermute | solution.py:377
  65.1 2.7 %collective-permute-start.20 = (bf16[640,128]{1,0:T(8,128)(2,1)S(1)}, bf16[640,128]{1,0:T(8,128)(2,1)S(1)}, u32[]{:S(2)}, u32[]{:S(2)}) collective-permute-start(bf16[640,128]{1,0:T(8,128)(2,1)S(1)} %get-tuple-element.52), channel_id=1, source_target_pairs={{0,2},{1,3},{2,0},{3,1},{4,6},{5,7},{6,4},{7,5},{8,10},{9,11},{10,... | collective-permute-start | bytes 491528 | tf_op jit(solution)/shard_map/ppermute | solution.py:411
  67.8 0.5 project.2
  68.3 0.9 %collective-permute-start.22 = (bf16[640,128]{1,0:T(8,128)(2,1)S(1)}, bf16[640,128]{1,0:T(8,128)(2,1)S(1)}, u32[]{:S(2)}, u32[]{:S(2)}) collective-permute-start(bf16[640,128]{1,0:T(8,128)(2,1)S(1)} %get-tuple-element.54), channel_id=1, source_target_pairs={{0,3},{1,2},{2,1},{3,0},{4,7},{5,6},{6,5},{7,4},{8,11},{9,10},{10,... | collective-permute-start | bytes 491528 | tf_op jit(solution)/shard_map/ppermute | solution.py:411
  69.2 7.5 %collective-permute-done.20.p1 = bf16[640,128]{1,0:T(8,128)(2,1)S(1)} collective-permute-done((bf16[640,128]{1,0:T(8,128)(2,1)S(1)}, bf16[640,128]{1,0:T(8,128)(2,1)S(1)}, u32[]{:S(2)}, u32[]{:S(2)}) %collective-permute-start.20) | collective-permute-done | bytes 163872 | tf_op jit(solution)/shard_map/ppermute | solution.py:411
  76.7 4.1 %collective-permute-done.22.p3 = bf16[640,128]{1,0:T(8,128)(2,1)S(1)} collective-permute-done((bf16[640,128]{1,0:T(8,128)(2,1)S(1)}, bf16[640,128]{1,0:T(8,128)(2,1)S(1)}, u32[]{:S(2)}, u32[]{:S(2)}) %collective-permute-start.22) | collective-permute-done | bytes 163872 | tf_op jit(solution)/shard_map/ppermute | solution.py:411
  80.7 0.8 sum_parts.1
  (30 shorter events, 1.9 us)
Async XLA Ops:
  1.7 25.9 %all-to-all-start = ((bf16[32,48,128]{2,1,0:T(8,128)(2,1)}), bf16[32,48,128]{2,1,0:T(8,128)(2,1)S(1)}, u32[]{:S(2)}, u32[]{:S(2)}) async-start(bf16[32,48,128]{2,1,0:T(8,128)(2,1)} %pack.1), calls=%async_computation | async-start | bytes 786432 | tf_op jit(solution)/shard_map/all_to_all | solution.py:314
  13.2 33.2 %copy-start = (bf16[5120,256]{1,0:T(8,128)(2,1)S(1)}, bf16[5120,256]{1,0:T(8,128)(2,1)}, u32[]{:S(2)}) copy-start(bf16[5120,256]{1,0:T(8,128)(2,1)} %refs_8_.2) | copy-start | bytes 7864324
  13.2 33.2 %copy-start.1 = (s32[64]{0:T(128)S(1)}, s32[64]{0:T(128)}, u32[]{:S(2)}) copy-start(s32[64]{0:T(128)} %refs_16_.1) | copy-start | bytes 772
  17.5 11.0 %collective-permute-start = (bf16[64,256]{1,0:T(8,128)(2,1)S(1)}, bf16[64,256]{1,0:T(8,128)(2,1)S(1)}, u32[]{:S(2)}, u32[]{:S(2)}) collective-permute-start(bf16[64,256]{1,0:T(8,128)(2,1)S(1)} %get-tuple-element.31), channel_id=1, source_target_pairs={{0,0},{1,1},{2,4},{3,5},{4,8},{5,9},{6,12},{7,13},{8,2},{9,3},{10,... | collective-permute-start | bytes 98312 | tf_op jit(solution)/shard_map/ppermute | solution.py:333
  18.1 10.3 %collective-permute-start.1 = (bf16[64,256]{1,0:T(8,128)(2,1)S(1)}, bf16[64,256]{1,0:T(8,128)(2,1)S(1)}, u32[]{:S(2)}, u32[]{:S(2)}) collective-permute-start(bf16[64,256]{1,0:T(8,128)(2,1)S(1)} %get-tuple-element.31), channel_id=1, source_target_pairs={{0,1},{1,0},{2,5},{3,4},{4,9},{5,8},{6,13},{7,12},{8,3},{9,2},{10,... | collective-permute-start | bytes 98312 | tf_op jit(solution)/shard_map/ppermute | solution.py:333
  18.4 10.0 %collective-permute-start.2 = (bf16[64,256]{1,0:T(8,128)(2,1)S(1)}, bf16[64,256]{1,0:T(8,128)(2,1)S(1)}, u32[]{:S(2)}, u32[]{:S(2)}) collective-permute-start(bf16[64,256]{1,0:T(8,128)(2,1)S(1)} %get-tuple-element.31), channel_id=1, source_target_pairs={{0,2},{1,3},{2,6},{3,7},{4,10},{5,11},{6,14},{7,15},{8,0},{9,1},{1... | collective-permute-start | bytes 98312 | tf_op jit(solution)/shard_map/ppermute | solution.py:333
  24.7 6.3 %collective-permute-start.3 = (bf16[64,256]{1,0:T(8,128)(2,1)S(1)}, bf16[64,256]{1,0:T(8,128)(2,1)S(1)}, u32[]{:S(2)}, u32[]{:S(2)}) collective-permute-start(bf16[64,256]{1,0:T(8,128)(2,1)S(1)} %get-tuple-element.31), channel_id=1, source_target_pairs={{0,3},{1,2},{2,7},{3,6},{4,11},{5,10},{6,15},{7,14},{8,1},{9,0},{1... | collective-permute-start | bytes 98312 | tf_op jit(solution)/shard_map/ppermute | solution.py:333
  31.1 8.5 %collective-permute-start.13 = (bf16[128,1280]{1,0:T(8,128)(2,1)}, bf16[128,1280]{1,0:T(8,128)(2,1)S(1)}, u32[]{:S(2)}, u32[]{:S(2)}) collective-permute-start(bf16[128,1280]{1,0:T(8,128)(2,1)} %get-tuple-element.42), channel_id=1, source_target_pairs={{0,4},{4,8},{8,12},{12,0},{1,5},{5,9},{9,13},{13,1},{2,6},{6,10},{... | collective-permute-start | bytes 983048 | tf_op jit(solution)/shard_map/ppermute | solution.py:345
  31.6 7.9 %collective-permute-start.14 = (bf16[128,1280]{1,0:T(8,128)(2,1)}, bf16[128,1280]{1,0:T(8,128)(2,1)S(1)}, u32[]{:S(2)}, u32[]{:S(2)}) collective-permute-start(bf16[128,1280]{1,0:T(8,128)(2,1)} %get-tuple-element.43), channel_id=1, source_target_pairs={{0,12},{4,0},{8,4},{12,8},{1,13},{5,1},{9,5},{13,9},{2,14},{6,2},{... | collective-permute-start | bytes 983048 | tf_op jit(solution)/shard_map/ppermute | solution.py:346
  34.3 6.7 %collective-permute-start.9 = (bf16[720,128]{1,0:T(8,128)(2,1)S(1)}, bf16[720,128]{1,0:T(8,128)(2,1)S(1)}, u32[]{:S(2)}, u32[]{:S(2)}) collective-permute-start(bf16[720,128]{1,0:T(8,128)(2,1)S(1)} %sort_rows.1.refs_0_), channel_id=1, source_target_pairs={{0,64},{64,0},{128,192},{192,128},{1,65},{65,1},{129,193},{193,129... | collective-permute-start | bytes 552968 | tf_op jit(solution)/shard_map/ppermute | solution.py:347
  35.8 7.2 %collective-permute-start.5 = (bf16[720,128]{1,0:T(8,128)(2,1)S(1)}, bf16[720,128]{1,0:T(8,128)(2,1)S(1)}, u32[]{:S(2)}, u32[]{:S(2)}) collective-permute-start(bf16[720,128]{1,0:T(8,128)(2,1)S(1)} %sort_rows.1.refs_0_), channel_id=1, source_target_pairs={{0,192},{64,128},{128,64},{192,0},{1,193},{65,129},{129,65},{193,1... | collective-permute-start | bytes 552968 | tf_op jit(solution)/shard_map/ppermute | solution.py:347
  37.9 7.0 %collective-permute-start.7 = (bf16[720,128]{1,0:T(8,128)(2,1)S(1)}, bf16[720,128]{1,0:T(8,128)(2,1)S(1)}, u32[]{:S(2)}, u32[]{:S(2)}) collective-permute-start(bf16[720,128]{1,0:T(8,128)(2,1)S(1)} %sort_rows.1.refs_0_), channel_id=1, source_target_pairs={{0,128},{64,192},{128,0},{192,64},{1,129},{65,193},{129,1},{193,65... | collective-permute-start | bytes 552968 | tf_op jit(solution)/shard_map/ppermute | solution.py:347
  39.6 14.3 %collective-permute-start.15 = (bf16[128,1280]{1,0:T(8,128)(2,1)}, bf16[128,1280]{1,0:T(8,128)(2,1)S(1)}, u32[]{:S(2)}, u32[]{:S(2)}) collective-permute-start(bf16[128,1280]{1,0:T(8,128)(2,1)} %get-tuple-element.46), channel_id=1, source_target_pairs={{0,8},{4,12},{8,0},{12,4},{1,9},{5,13},{9,1},{13,5},{2,10},{6,14},... | collective-permute-start | bytes 983048 | tf_op jit(solution)/shard_map/ppermute | solution.py:349
  41.0 3.9 %collective-permute-start.4 = (bf16[720,128]{1,0:T(8,128)(2,1)S(1)}, bf16[720,128]{1,0:T(8,128)(2,1)S(1)}, u32[]{:S(2)}, u32[]{:S(2)}) collective-permute-start(bf16[720,128]{1,0:T(8,128)(2,1)S(1)} %sort_rows.1.refs_0_), channel_id=1, source_target_pairs={{0,16},{16,0},{1,17},{17,1},{2,18},{18,2},{3,19},{19,3},{4,20},{20... | collective-permute-start | bytes 552968 | tf_op jit(solution)/shard_map/ppermute | solution.py:352
  41.0 3.9 %collective-permute-start.10 = (bf16[720,128]{1,0:T(8,128)(2,1)S(1)}, bf16[720,128]{1,0:T(8,128)(2,1)S(1)}, u32[]{:S(2)}, u32[]{:S(2)}) collective-permute-start(bf16[720,128]{1,0:T(8,128)(2,1)S(1)} %collective-permute-done.9.refs_6_), channel_id=1, source_target_pairs={{0,16},{16,0},{1,17},{17,1},{2,18},{18,2},{3,19},{19,3},{4,20},{20... | collective-permute-start | bytes 552968 | tf_op jit(solution)/shard_map/ppermute | solution.py:352
  43.0 2.0 %collective-permute-start.6 = (bf16[720,128]{1,0:T(8,128)(2,1)S(1)}, bf16[720,128]{1,0:T(8,128)(2,1)S(1)}, u32[]{:S(2)}, u32[]{:S(2)}) collective-permute-start(bf16[720,128]{1,0:T(8,128)(2,1)S(1)} %collective-permute-done.5.refs_2_), channel_id=1, source_target_pairs={{0,16},{16,0},{1,17},{17,1},{2,18},{18,2},{3,19},{19,3},{4,20},{20... | collective-permute-start | bytes 552968 | tf_op jit(solution)/shard_map/ppermute | solution.py:352
  44.9 1.4 %collective-permute-start.8 = (bf16[720,128]{1,0:T(8,128)(2,1)S(1)}, bf16[720,128]{1,0:T(8,128)(2,1)S(1)}, u32[]{:S(2)}, u32[]{:S(2)}) collective-permute-start(bf16[720,128]{1,0:T(8,128)(2,1)S(1)} %collective-permute-done.7.refs_4_), channel_id=1, source_target_pairs={{0,16},{16,0},{1,17},{17,1},{2,18},{18,2},{3,19},{19,3},{4,20},{20... | collective-permute-start | bytes 552968 | tf_op jit(solution)/shard_map/ppermute | solution.py:352
  53.9 4.0 %collective-permute-start.16 = (bf16[128,1280]{1,0:T(8,128)(2,1)S(1)}, bf16[128,1280]{1,0:T(8,128)(2,1)S(1)}, u32[]{:S(2)}, u32[]{:S(2)}) collective-permute-start(bf16[128,1280]{1,0:T(8,128)(2,1)S(1)} %collective-permute-done.13.refs_9_), channel_id=1, source_target_pairs={{0,16},{16,0},{1,17},{17,1},{2,18},{18,2},{3,19},{19,3},{4,20},{20... | collective-permute-start | bytes 983048 | tf_op jit(solution)/shard_map/ppermute | solution.py:379
  54.1 3.8 %collective-permute-start.17 = (bf16[128,1280]{1,0:T(8,128)(2,1)S(1)}, bf16[128,1280]{1,0:T(8,128)(2,1)S(1)}, u32[]{:S(2)}, u32[]{:S(2)}) collective-permute-start(bf16[128,1280]{1,0:T(8,128)(2,1)S(1)} %collective-permute-done.15.refs_10_), channel_id=1, source_target_pairs={{0,16},{16,0},{1,17},{17,1},{2,18},{18,2},{3,19},{19,3},{4,20},{20... | collective-permute-start | bytes 983048 | tf_op jit(solution)/shard_map/ppermute | solution.py:379
  54.5 3.4 %collective-permute-start.18 = (bf16[128,1280]{1,0:T(8,128)(2,1)S(1)}, bf16[128,1280]{1,0:T(8,128)(2,1)S(1)}, u32[]{:S(2)}, u32[]{:S(2)}) collective-permute-start(bf16[128,1280]{1,0:T(8,128)(2,1)S(1)} %collective-permute-done.14.refs_11_), channel_id=1, source_target_pairs={{0,16},{16,0},{1,17},{17,1},{2,18},{18,2},{3,19},{19,3},{4,20},{20... | collective-permute-start | bytes 983048 | tf_op jit(solution)/shard_map/ppermute | solution.py:379
  54.6 7.0 %collective-permute-start.19 = (bf16[256,256]{1,0:T(8,128)(2,1)S(1)}, bf16[256,256]{1,0:T(8,128)(2,1)S(1)}, u32[]{:S(2)}, u32[]{:S(2)}) collective-permute-start(bf16[256,256]{1,0:T(8,128)(2,1)S(1)} %attend.1.c0), channel_id=1, source_target_pairs={{0,4},{4,8},{8,12},{12,0},{1,5},{5,9},{9,13},{13,1},{2,6},{6,10},{... | collective-permute-start | bytes 393224 | tf_op jit(solution)/shard_map/ppermute | solution.py:377
  54.6 9.1 %collective-permute-start.11 = (bf16[256,256]{1,0:T(8,128)(2,1)S(1)}, bf16[256,256]{1,0:T(8,128)(2,1)S(1)}, u32[]{:S(2)}, u32[]{:S(2)}) collective-permute-start(bf16[256,256]{1,0:T(8,128)(2,1)S(1)} %attend.1.c0), channel_id=1, source_target_pairs={{0,12},{4,0},{8,4},{12,8},{1,13},{5,1},{9,5},{13,9},{2,14},{6,2},{... | collective-permute-start | bytes 393224 | tf_op jit(solution)/shard_map/ppermute | solution.py:377
  57.9 6.7 %collective-permute-start.12 = (bf16[256,256]{1,0:T(8,128)(2,1)S(1)}, bf16[256,256]{1,0:T(8,128)(2,1)S(1)}, u32[]{:S(2)}, u32[]{:S(2)}) collective-permute-start(bf16[256,256]{1,0:T(8,128)(2,1)S(1)} %attend.1.c0), channel_id=1, source_target_pairs={{0,8},{4,12},{8,0},{12,4},{1,9},{5,13},{9,1},{13,5},{2,10},{6,14},... | collective-permute-start | bytes 393224 | tf_op jit(solution)/shard_map/ppermute | solution.py:377
  65.1 11.6 %collective-permute-start.20 = (bf16[640,128]{1,0:T(8,128)(2,1)S(1)}, bf16[640,128]{1,0:T(8,128)(2,1)S(1)}, u32[]{:S(2)}, u32[]{:S(2)}) collective-permute-start(bf16[640,128]{1,0:T(8,128)(2,1)S(1)} %get-tuple-element.52), channel_id=1, source_target_pairs={{0,2},{1,3},{2,0},{3,1},{4,6},{5,7},{6,4},{7,5},{8,10},{9,11},{10,... | collective-permute-start | bytes 491528 | tf_op jit(solution)/shard_map/ppermute | solution.py:411
  67.8 8.9 %collective-permute-start.21 = (bf16[640,128]{1,0:T(8,128)(2,1)S(1)}, bf16[640,128]{1,0:T(8,128)(2,1)S(1)}, u32[]{:S(2)}, u32[]{:S(2)}) collective-permute-start(bf16[640,128]{1,0:T(8,128)(2,1)S(1)} %get-tuple-element.53), channel_id=1, source_target_pairs={{0,1},{1,0},{2,3},{3,2},{4,5},{5,4},{6,7},{7,6},{8,9},{9,8},{10,11... | collective-permute-start | bytes 491528 | tf_op jit(solution)/shard_map/ppermute | solution.py:411
  68.3 12.4 %collective-permute-start.22 = (bf16[640,128]{1,0:T(8,128)(2,1)S(1)}, bf16[640,128]{1,0:T(8,128)(2,1)S(1)}, u32[]{:S(2)}, u32[]{:S(2)}) collective-permute-start(bf16[640,128]{1,0:T(8,128)(2,1)S(1)} %get-tuple-element.54), channel_id=1, source_target_pairs={{0,3},{1,2},{2,1},{3,0},{4,7},{5,6},{6,5},{7,4},{8,11},{9,10},{10,... | collective-permute-start | bytes 491528 | tf_op jit(solution)/shard_map/ppermute | solution.py:411

commit v7 on v6

--- a/solution.py
+++ b/solution.py
@@ -399,10 +399,10 @@
         name="begin",
     )(ctx, others[1], merged)
     sums = {}
-    for order in ((2, 1), (3, 0)):
+    for order in ((2,), (1,), (3, 0)):
         both = pl.pallas_call(
             functools.partial(project_kernel, order),
-            out_shape=(array(640, 128),) * 2,
+            out_shape=(array(640, 128),) * len(order),
             compiler_params=params(16),
             cost_estimate=pl.CostEstimate(flops=340_000_000, bytes_accessed=4_000_000, transcendentals=0),
             name="project",

time: 82.2 us -> 83.5 us (1.016)
  waiting for transfers between devices: 22.9 us -> 24.1 us
    ppermute x3, waiting for transfers between devices: 11.5 us -> 12.7 us  [local(): came = [lax.ppermute(sums[n], 'z', partner(n)) for n in (2, 1, 3)]]
  transfers between devices with their start and end apart: 24 -> 24, of which waited for: 11 -> 12; matrix products, arithmetic and copies ran while one was open for 0% -> 0% of each run, Pallas kernels for 21% -> 21%
where the time goes in v7:
time: 83.5 us; the launch traced here: 83.1 us
  starting transfers between devices  38.2 us (46%)
  waiting for transfers between devices  24.1 us (29%)
  Pallas kernels  20.5 us (25%)
    ppermute x3, waiting for transfers between devices, local(): came = [lax.ppermute(sums[n], 'z', partner(n)) for n in (2, 1, 3)]  12.7 us
    all_to_all x1, starting transfers between devices, local(): got = lax.all_to_all(messages, ('zh', 'y', 'z'), 0, 0, tiled=True)  11.4 us
    ppermute x4, starting transfers between devices, local(): new_kv = [lax.ppermute(kv_t, TP, kv_pairs(k)) for k in range(4)]  9.64 us
    pallas_call x1, Pallas kernels, local(): pl.pallas_call(attend_kernel, out_shape=array(ROWS, 256), in_specs=[SMEM]...  7.49 us
    pallas_call x1, Pallas kernels, local(): pl.pallas_call(norm_kernel, out_shape=(pltpu.HBM((10, ROWS, 512), BF), ar...  4.29 us
    ppermute x3, starting transfers between devices, local(): parts = [mine] + [lax.ppermute(mine, 'x', partner(s)) for s in ORDER[1:]]  4.22 us
    ppermute x3, starting transfers between devices, local(): came = [lax.ppermute(sums[n], 'z', partner(n)) for n in (2, 1, 3)]  3.75 us
    pallas_call x1, Pallas kernels, local(): pl.pallas_call(merge_o_kernel, out_shape=array(4, 4, 256, 320), in_specs=...  3.53 us
  transfers between devices with their start and end apart: 24, of which 12 were waited for; matrix products, arithmetic and copies ran while one was open for 0% of the time, Pallas kernels for 21%

profile of v7, /device:TPU:32, one launch (start us, length us, event | category | flops | bytes accessed | tf_op | source)
XLA Modules:
  0.0 83.1 jit_solution(10240463796068856841)
XLA Ops:
  0.0 1.7 %pack.1 = bf16[32,48,128]{2,1,0:T(8,128)(2,1)} custom-call(bf16[20,64]{1,0:T(8,128)(2,1)} %low.1, bf16[20,64]{1,0:T(8,128)(2,1)} %up.1, bf16[4,256]{1,0:T(4,128)(2,1)} %q_up.1, bf16[4,256]{1,0:T(4,128)(2,1)} %o_low.1), custom_call_target="tpu_custom_call" | custom-call | tf_op jit(solution)/shard_map/pack/pallas_call | solution.py:308
  1.7 11.4 %all-to-all-start = ((bf16[32,48,128]{2,1,0:T(8,128)(2,1)}), bf16[32,48,128]{2,1,0:T(8,128)(2,1)S(1)}, u32[]{:S(2)}, u32[]{:S(2)}) async-start(bf16[32,48,128]{2,1,0:T(8,128)(2,1)} %pack.1), calls=%async_computation | async-start | bytes 786432 | tf_op jit(solution)/shard_map/all_to_all | solution.py:314
  13.2 4.3 %norm_kv.1 = (bf16[10,256,512]{2,1,0:T(8,128)(2,1)}, bf16[64,256]{1,0:T(8,128)(2,1)S(1)}, bf16[128,1280]{1,0:T(8,128)(2,1)}, bf16[128,1280]{1,0:T(8,128)(2,1)}, bf16[128,1280]{1,0:T(8,128)(2,1)}) custom-call(s32[5]{0:T(128)S(1)} %stack.23.ids, bf16[4,64,5120]{2,1,0:T(8,128)(2,1)} %states.1, bf16[64,5120]{1,0:T(8,128)(2,1)} %bitcast.6, bf16[256,5120]{1,0:T(8,128)(2,1)} %refs_8_.3), custom_call_target="tpu_custom_call" | custom-call | flops 170000000 | bytes 8000000 | tf_op jit(solution)/shard_map/norm_kv/pallas_call | solution.py:316
  17.5 0.7 collective-permute-start
  18.5 6.3 %collective-permute-start.2 = (bf16[64,256]{1,0:T(8,128)(2,1)S(1)}, bf16[64,256]{1,0:T(8,128)(2,1)S(1)}, u32[]{:S(2)}, u32[]{:S(2)}) collective-permute-start(bf16[64,256]{1,0:T(8,128)(2,1)S(1)} %get-tuple-element.29), channel_id=1, source_target_pairs={{0,2},{1,3},{2,6},{3,7},{4,10},{5,11},{6,14},{7,15},{8,0},{9,1},{1... | collective-permute-start | bytes 98312 | tf_op jit(solution)/shard_map/ppermute | solution.py:333
  24.8 2.4 %collective-permute-start.3 = (bf16[64,256]{1,0:T(8,128)(2,1)S(1)}, bf16[64,256]{1,0:T(8,128)(2,1)S(1)}, u32[]{:S(2)}, u32[]{:S(2)}) collective-permute-start(bf16[64,256]{1,0:T(8,128)(2,1)S(1)} %get-tuple-element.29), channel_id=1, source_target_pairs={{0,3},{1,2},{2,7},{3,6},{4,11},{5,10},{6,15},{7,14},{8,1},{9,0},{1... | collective-permute-start | bytes 98312 | tf_op jit(solution)/shard_map/ppermute | solution.py:333
  27.1 0.5 all-to-all-done.got
  27.7 0.8 sort_rows.1.refs_0_
  28.5 2.6 %collective-permute-done.3.refs_15_ = bf16[64,256]{1,0:T(8,128)(2,1)S(1)} collective-permute-done((bf16[64,256]{1,0:T(8,128)(2,1)S(1)}, bf16[64,256]{1,0:T(8,128)(2,1)S(1)}, u32[]{:S(2)}, u32[]{:S(2)}) %collective-permute-start.3) | collective-permute-done | bytes 32800 | tf_op jit(solution)/shard_map/ppermute | solution.py:333
  31.1 0.6 collective-permute-start.13
  31.7 2.7 %collective-permute-start.14 = (bf16[128,1280]{1,0:T(8,128)(2,1)}, bf16[128,1280]{1,0:T(8,128)(2,1)S(1)}, u32[]{:S(2)}, u32[]{:S(2)}) collective-permute-start(bf16[128,1280]{1,0:T(8,128)(2,1)} %get-tuple-element.41), channel_id=1, source_target_pairs={{0,12},{4,0},{8,4},{12,8},{1,13},{5,1},{9,5},{13,9},{2,14},{6,2},{... | collective-permute-start | bytes 983048 | tf_op jit(solution)/shard_map/ppermute | solution.py:346
  34.3 1.5 %collective-permute-start.9 = (bf16[720,128]{1,0:T(8,128)(2,1)S(1)}, bf16[720,128]{1,0:T(8,128)(2,1)S(1)}, u32[]{:S(2)}, u32[]{:S(2)}) collective-permute-start(bf16[720,128]{1,0:T(8,128)(2,1)S(1)} %sort_rows.1.refs_0_), channel_id=1, source_target_pairs={{0,64},{64,0},{128,192},{192,128},{1,65},{65,1},{129,193},{193,129... | collective-permute-start | bytes 552968 | tf_op jit(solution)/shard_map/ppermute | solution.py:347
  35.8 2.1 %collective-permute-start.5 = (bf16[720,128]{1,0:T(8,128)(2,1)S(1)}, bf16[720,128]{1,0:T(8,128)(2,1)S(1)}, u32[]{:S(2)}, u32[]{:S(2)}) collective-permute-start(bf16[720,128]{1,0:T(8,128)(2,1)S(1)} %sort_rows.1.refs_0_), channel_id=1, source_target_pairs={{0,192},{64,128},{128,64},{192,0},{1,193},{65,129},{129,65},{193,1... | collective-permute-start | bytes 552968 | tf_op jit(solution)/shard_map/ppermute | solution.py:347
  37.9 0.6 collective-permute-start.7
  38.5 1.0 %collective-permute-done.13.refs_9_ = bf16[128,1280]{1,0:T(8,128)(2,1)S(1)} collective-permute-done((bf16[128,1280]{1,0:T(8,128)(2,1)}, bf16[128,1280]{1,0:T(8,128)(2,1)S(1)}, u32[]{:S(2)}, u32[]{:S(2)}) %collective-permute-start.13) | collective-permute-done | bytes 327712 | tf_op jit(solution)/shard_map/ppermute | solution.py:345
  39.6 1.5 %collective-permute-start.15 = (bf16[128,1280]{1,0:T(8,128)(2,1)}, bf16[128,1280]{1,0:T(8,128)(2,1)S(1)}, u32[]{:S(2)}, u32[]{:S(2)}) collective-permute-start(bf16[128,1280]{1,0:T(8,128)(2,1)} %get-tuple-element.44), channel_id=1, source_target_pairs={{0,8},{4,12},{8,0},{12,4},{1,9},{5,13},{9,1},{13,5},{2,10},{6,14},... | collective-permute-start | bytes 983048 | tf_op jit(solution)/shard_map/ppermute | solution.py:349
  41.6 1.4 %collective-permute-done.5.refs_2_ = bf16[720,128]{1,0:T(8,128)(2,1)S(1)} collective-permute-done((bf16[720,128]{1,0:T(8,128)(2,1)S(1)}, bf16[720,128]{1,0:T(8,128)(2,1)S(1)}, u32[]{:S(2)}, u32[]{:S(2)}) %collective-permute-start.5) | collective-permute-done | bytes 184352 | tf_op jit(solution)/shard_map/ppermute | solution.py:347
  43.0 2.0 %collective-permute-done.7.refs_4_ = bf16[720,128]{1,0:T(8,128)(2,1)S(1)} collective-permute-done((bf16[720,128]{1,0:T(8,128)(2,1)S(1)}, bf16[720,128]{1,0:T(8,128)(2,1)S(1)}, u32[]{:S(2)}, u32[]{:S(2)}) %collective-permute-start.7) | collective-permute-done | bytes 184352 | tf_op jit(solution)/shard_map/ppermute | solution.py:347
  45.0 1.4 %collective-permute-done.8.refs_5_ = bf16[720,128]{1,0:T(8,128)(2,1)S(1)} collective-permute-done((bf16[720,128]{1,0:T(8,128)(2,1)S(1)}, bf16[720,128]{1,0:T(8,128)(2,1)S(1)}, u32[]{:S(2)}, u32[]{:S(2)}) %collective-permute-start.8) | collective-permute-done | bytes 184352 | tf_op jit(solution)/shard_map/ppermute | solution.py:352
  46.4 7.5 %attend.1.c0 = bf16[256,256]{1,0:T(8,128)(2,1)S(1)} custom-call(s32[5]{0:T(128)S(1)} %stack.23.ids, bf16[720,128]{1,0:T(8,128)(2,1)S(1)} %sort_rows.1.refs_0_, bf16[720,128]{1,0:T(8,128)(2,1)S(1)} %collective-permute-done.4.refs_1_, bf16[720,128]{1,0:T(8,128)(2,1)S(1)} %collective-permute-done.5.refs_2_, ...), custom_call_target="tpu_custom_call" | custom-call | flops 1000000000 | bytes 10000000 | tf_op jit(solution)/shard_map/attend/pallas_call | solution.py:354
  54.6 3.2 %collective-permute-start.11 = (bf16[256,256]{1,0:T(8,128)(2,1)S(1)}, bf16[256,256]{1,0:T(8,128)(2,1)S(1)}, u32[]{:S(2)}, u32[]{:S(2)}) collective-permute-start(bf16[256,256]{1,0:T(8,128)(2,1)S(1)} %attend.1.c0), channel_id=1, source_target_pairs={{0,12},{4,0},{8,4},{12,8},{1,13},{5,1},{9,5},{13,9},{2,14},{6,2},{... | collective-permute-start | bytes 393224 | tf_op jit(solution)/shard_map/ppermute | solution.py:377
  57.9 3.5 %merge_o.1.merged = bf16[4,4,256,320]{3,2,1,0:T(8,128)(2,1)S(1)} custom-call(s32[5]{0:T(128)S(1)} %stack.23.ids, bf16[720,128]{1,0:T(8,128)(2,1)S(1)} %sort_rows.1.refs_0_, bf16[720,128]{1,0:T(8,128)(2,1)S(1)} %collective-permute-done.4.refs_1_, bf16[720,128]{1,0:T(8,128)(2,1)S(1)} %collective-permute-done.5.refs_2_, ...), custom_call_target="tpu_custom_call" | custom-call | flops 340000000 | bytes 8000000 | tf_op jit(solution)/shard_map/merge_o/pallas_call | solution.py:380
  61.6 0.7 begin.1.begun
  62.3 1.4 %collective-permute-done.11.c3 = bf16[256,256]{1,0:T(8,128)(2,1)S(1)} collective-permute-done((bf16[256,256]{1,0:T(8,128)(2,1)S(1)}, bf16[256,256]{1,0:T(8,128)(2,1)S(1)}, u32[]{:S(2)}, u32[]{:S(2)}) %collective-permute-start.11) | collective-permute-done | bytes 131104 | tf_op jit(solution)/shard_map/ppermute | solution.py:377
  63.7 0.9 %collective-permute-done.12.c2 = bf16[256,256]{1,0:T(8,128)(2,1)S(1)} collective-permute-done((bf16[256,256]{1,0:T(8,128)(2,1)S(1)}, bf16[256,256]{1,0:T(8,128)(2,1)S(1)}, u32[]{:S(2)}, u32[]{:S(2)}) %collective-permute-start.12) | collective-permute-done | bytes 131104 | tf_op jit(solution)/shard_map/ppermute | solution.py:377
  64.9 0.7 collective-permute-start.21
  66.0 2.2 %collective-permute-start.20 = (bf16[640,128]{1,0:T(8,128)(2,1)S(1)}, bf16[640,128]{1,0:T(8,128)(2,1)S(1)}, u32[]{:S(2)}, u32[]{:S(2)}) collective-permute-start(bf16[640,128]{1,0:T(8,128)(2,1)S(1)} %project.4), channel_id=1, source_target_pairs={{0,2},{1,3},{2,0},{3,1},{4,6},{5,7},{6,4},{7,5},{8,10},{9,11},{10,... | collective-permute-start | bytes 491528 | tf_op jit(solution)/shard_map/ppermute | solution.py:411
  68.6 0.9 %collective-permute-start.22 = (bf16[640,128]{1,0:T(8,128)(2,1)S(1)}, bf16[640,128]{1,0:T(8,128)(2,1)S(1)}, u32[]{:S(2)}, u32[]{:S(2)}) collective-permute-start(bf16[640,128]{1,0:T(8,128)(2,1)S(1)} %get-tuple-element.50), channel_id=1, source_target_pairs={{0,3},{1,2},{2,1},{3,0},{4,7},{5,6},{6,5},{7,4},{8,11},{9,10},{10,... | collective-permute-start | bytes 491528 | tf_op jit(solution)/shard_map/ppermute | solution.py:411
  69.5 1.8 %collective-permute-done.21.p2 = bf16[640,128]{1,0:T(8,128)(2,1)S(1)} collective-permute-done((bf16[640,128]{1,0:T(8,128)(2,1)S(1)}, bf16[640,128]{1,0:T(8,128)(2,1)S(1)}, u32[]{:S(2)}, u32[]{:S(2)}) %collective-permute-start.21) | collective-permute-done | bytes 163872 | tf_op jit(solution)/shard_map/ppermute | solution.py:411
  71.4 8.0 %collective-permute-done.20.p1 = bf16[640,128]{1,0:T(8,128)(2,1)S(1)} collective-permute-done((bf16[640,128]{1,0:T(8,128)(2,1)S(1)}, bf16[640,128]{1,0:T(8,128)(2,1)S(1)}, u32[]{:S(2)}, u32[]{:S(2)}) %collective-permute-start.20) | collective-permute-done | bytes 163872 | tf_op jit(solution)/shard_map/ppermute | solution.py:411
  79.4 2.9 %collective-permute-done.22.p3 = bf16[640,128]{1,0:T(8,128)(2,1)S(1)} collective-permute-done((bf16[640,128]{1,0:T(8,128)(2,1)S(1)}, bf16[640,128]{1,0:T(8,128)(2,1)S(1)}, u32[]{:S(2)}, u32[]{:S(2)}) %collective-permute-start.22) | collective-permute-done | bytes 163872 | tf_op jit(solution)/shard_map/ppermute | solution.py:411
  82.3 0.8 sum_parts.1
  (31 shorter events, 3.1 us)
Async XLA Ops:
  1.7 25.9 %all-to-all-start = ((bf16[32,48,128]{2,1,0:T(8,128)(2,1)}), bf16[32,48,128]{2,1,0:T(8,128)(2,1)S(1)}, u32[]{:S(2)}, u32[]{:S(2)}) async-start(bf16[32,48,128]{2,1,0:T(8,128)(2,1)} %pack.1), calls=%async_computation | async-start | bytes 786432 | tf_op jit(solution)/shard_map/all_to_all | solution.py:314
  13.2 33.2 %copy-start = (bf16[5120,256]{1,0:T(8,128)(2,1)S(1)}, bf16[5120,256]{1,0:T(8,128)(2,1)}, u32[]{:S(2)}) copy-start(bf16[5120,256]{1,0:T(8,128)(2,1)} %refs_8_.2) | copy-start | bytes 7864324
  13.2 33.2 %copy-start.1 = (s32[64]{0:T(128)S(1)}, s32[64]{0:T(128)}, u32[]{:S(2)}) copy-start(s32[64]{0:T(128)} %refs_16_.1) | copy-start | bytes 772
  17.5 11.0 %collective-permute-start = (bf16[64,256]{1,0:T(8,128)(2,1)S(1)}, bf16[64,256]{1,0:T(8,128)(2,1)S(1)}, u32[]{:S(2)}, u32[]{:S(2)}) collective-permute-start(bf16[64,256]{1,0:T(8,128)(2,1)S(1)} %get-tuple-element.29), channel_id=1, source_target_pairs={{0,0},{1,1},{2,4},{3,5},{4,8},{5,9},{6,12},{7,13},{8,2},{9,3},{10,... | collective-permute-start | bytes 98312 | tf_op jit(solution)/shard_map/ppermute | solution.py:333
  18.2 10.3 %collective-permute-start.1 = (bf16[64,256]{1,0:T(8,128)(2,1)S(1)}, bf16[64,256]{1,0:T(8,128)(2,1)S(1)}, u32[]{:S(2)}, u32[]{:S(2)}) collective-permute-start(bf16[64,256]{1,0:T(8,128)(2,1)S(1)} %get-tuple-element.29), channel_id=1, source_target_pairs={{0,1},{1,0},{2,5},{3,4},{4,9},{5,8},{6,13},{7,12},{8,3},{9,2},{10,... | collective-permute-start | bytes 98312 | tf_op jit(solution)/shard_map/ppermute | solution.py:333
  18.5 10.0 %collective-permute-start.2 = (bf16[64,256]{1,0:T(8,128)(2,1)S(1)}, bf16[64,256]{1,0:T(8,128)(2,1)S(1)}, u32[]{:S(2)}, u32[]{:S(2)}) collective-permute-start(bf16[64,256]{1,0:T(8,128)(2,1)S(1)} %get-tuple-element.29), channel_id=1, source_target_pairs={{0,2},{1,3},{2,6},{3,7},{4,10},{5,11},{6,14},{7,15},{8,0},{9,1},{1... | collective-permute-start | bytes 98312 | tf_op jit(solution)/shard_map/ppermute | solution.py:333
  24.8 6.3 %collective-permute-start.3 = (bf16[64,256]{1,0:T(8,128)(2,1)S(1)}, bf16[64,256]{1,0:T(8,128)(2,1)S(1)}, u32[]{:S(2)}, u32[]{:S(2)}) collective-permute-start(bf16[64,256]{1,0:T(8,128)(2,1)S(1)} %get-tuple-element.29), channel_id=1, source_target_pairs={{0,3},{1,2},{2,7},{3,6},{4,11},{5,10},{6,15},{7,14},{8,1},{9,0},{1... | collective-permute-start | bytes 98312 | tf_op jit(solution)/shard_map/ppermute | solution.py:333
  31.1 8.5 %collective-permute-start.13 = (bf16[128,1280]{1,0:T(8,128)(2,1)}, bf16[128,1280]{1,0:T(8,128)(2,1)S(1)}, u32[]{:S(2)}, u32[]{:S(2)}) collective-permute-start(bf16[128,1280]{1,0:T(8,128)(2,1)} %get-tuple-element.40), channel_id=1, source_target_pairs={{0,4},{4,8},{8,12},{12,0},{1,5},{5,9},{9,13},{13,1},{2,6},{6,10},{... | collective-permute-start | bytes 983048 | tf_op jit(solution)/shard_map/ppermute | solution.py:345
  31.7 7.9 %collective-permute-start.14 = (bf16[128,1280]{1,0:T(8,128)(2,1)}, bf16[128,1280]{1,0:T(8,128)(2,1)S(1)}, u32[]{:S(2)}, u32[]{:S(2)}) collective-permute-start(bf16[128,1280]{1,0:T(8,128)(2,1)} %get-tuple-element.41), channel_id=1, source_target_pairs={{0,12},{4,0},{8,4},{12,8},{1,13},{5,1},{9,5},{13,9},{2,14},{6,2},{... | collective-permute-start | bytes 983048 | tf_op jit(solution)/shard_map/ppermute | solution.py:346
  34.3 6.7 %collective-permute-start.9 = (bf16[720,128]{1,0:T(8,128)(2,1)S(1)}, bf16[720,128]{1,0:T(8,128)(2,1)S(1)}, u32[]{:S(2)}, u32[]{:S(2)}) collective-permute-start(bf16[720,128]{1,0:T(8,128)(2,1)S(1)} %sort_rows.1.refs_0_), channel_id=1, source_target_pairs={{0,64},{64,0},{128,192},{192,128},{1,65},{65,1},{129,193},{193,129... | collective-permute-start | bytes 552968 | tf_op jit(solution)/shard_map/ppermute | solution.py:347
  35.8 7.2 %collective-permute-start.5 = (bf16[720,128]{1,0:T(8,128)(2,1)S(1)}, bf16[720,128]{1,0:T(8,128)(2,1)S(1)}, u32[]{:S(2)}, u32[]{:S(2)}) collective-permute-start(bf16[720,128]{1,0:T(8,128)(2,1)S(1)} %sort_rows.1.refs_0_), channel_id=1, source_target_pairs={{0,192},{64,128},{128,64},{192,0},{1,193},{65,129},{129,65},{193,1... | collective-permute-start | bytes 552968 | tf_op jit(solution)/shard_map/ppermute | solution.py:347
  37.9 7.0 %collective-permute-start.7 = (bf16[720,128]{1,0:T(8,128)(2,1)S(1)}, bf16[720,128]{1,0:T(8,128)(2,1)S(1)}, u32[]{:S(2)}, u32[]{:S(2)}) collective-permute-start(bf16[720,128]{1,0:T(8,128)(2,1)S(1)} %sort_rows.1.refs_0_), channel_id=1, source_target_pairs={{0,128},{64,192},{128,0},{192,64},{1,129},{65,193},{129,1},{193,65... | collective-permute-start | bytes 552968 | tf_op jit(solution)/shard_map/ppermute | solution.py:347
  39.6 14.3 %collective-permute-start.15 = (bf16[128,1280]{1,0:T(8,128)(2,1)}, bf16[128,1280]{1,0:T(8,128)(2,1)S(1)}, u32[]{:S(2)}, u32[]{:S(2)}) collective-permute-start(bf16[128,1280]{1,0:T(8,128)(2,1)} %get-tuple-element.44), channel_id=1, source_target_pairs={{0,8},{4,12},{8,0},{12,4},{1,9},{5,13},{9,1},{13,5},{2,10},{6,14},... | collective-permute-start | bytes 983048 | tf_op jit(solution)/shard_map/ppermute | solution.py:349
  41.0 3.9 %collective-permute-start.4 = (bf16[720,128]{1,0:T(8,128)(2,1)S(1)}, bf16[720,128]{1,0:T(8,128)(2,1)S(1)}, u32[]{:S(2)}, u32[]{:S(2)}) collective-permute-start(bf16[720,128]{1,0:T(8,128)(2,1)S(1)} %sort_rows.1.refs_0_), channel_id=1, source_target_pairs={{0,16},{16,0},{1,17},{17,1},{2,18},{18,2},{3,19},{19,3},{4,20},{20... | collective-permute-start | bytes 552968 | tf_op jit(solution)/shard_map/ppermute | solution.py:352
  41.1 3.9 %collective-permute-start.10 = (bf16[720,128]{1,0:T(8,128)(2,1)S(1)}, bf16[720,128]{1,0:T(8,128)(2,1)S(1)}, u32[]{:S(2)}, u32[]{:S(2)}) collective-permute-start(bf16[720,128]{1,0:T(8,128)(2,1)S(1)} %collective-permute-done.9.refs_6_), channel_id=1, source_target_pairs={{0,16},{16,0},{1,17},{17,1},{2,18},{18,2},{3,19},{19,3},{4,20},{20... | collective-permute-start | bytes 552968 | tf_op jit(solution)/shard_map/ppermute | solution.py:352
  43.0 2.0 %collective-permute-start.6 = (bf16[720,128]{1,0:T(8,128)(2,1)S(1)}, bf16[720,128]{1,0:T(8,128)(2,1)S(1)}, u32[]{:S(2)}, u32[]{:S(2)}) collective-permute-start(bf16[720,128]{1,0:T(8,128)(2,1)S(1)} %collective-permute-done.5.refs_2_), channel_id=1, source_target_pairs={{0,16},{16,0},{1,17},{17,1},{2,18},{18,2},{3,19},{19,3},{4,20},{20... | collective-permute-start | bytes 552968 | tf_op jit(solution)/shard_map/ppermute | solution.py:352
  45.0 1.4 %collective-permute-start.8 = (bf16[720,128]{1,0:T(8,128)(2,1)S(1)}, bf16[720,128]{1,0:T(8,128)(2,1)S(1)}, u32[]{:S(2)}, u32[]{:S(2)}) collective-permute-start(bf16[720,128]{1,0:T(8,128)(2,1)S(1)} %collective-permute-done.7.refs_4_), channel_id=1, source_target_pairs={{0,16},{16,0},{1,17},{17,1},{2,18},{18,2},{3,19},{19,3},{4,20},{20... | collective-permute-start | bytes 552968 | tf_op jit(solution)/shard_map/ppermute | solution.py:352
  53.9 4.0 %collective-permute-start.16 = (bf16[128,1280]{1,0:T(8,128)(2,1)S(1)}, bf16[128,1280]{1,0:T(8,128)(2,1)S(1)}, u32[]{:S(2)}, u32[]{:S(2)}) collective-permute-start(bf16[128,1280]{1,0:T(8,128)(2,1)S(1)} %collective-permute-done.13.refs_9_), channel_id=1, source_target_pairs={{0,16},{16,0},{1,17},{17,1},{2,18},{18,2},{3,19},{19,3},{4,20},{20... | collective-permute-start | bytes 983048 | tf_op jit(solution)/shard_map/ppermute | solution.py:379
  54.1 3.8 %collective-permute-start.17 = (bf16[128,1280]{1,0:T(8,128)(2,1)S(1)}, bf16[128,1280]{1,0:T(8,128)(2,1)S(1)}, u32[]{:S(2)}, u32[]{:S(2)}) collective-permute-start(bf16[128,1280]{1,0:T(8,128)(2,1)S(1)} %collective-permute-done.15.refs_10_), channel_id=1, source_target_pairs={{0,16},{16,0},{1,17},{17,1},{2,18},{18,2},{3,19},{19,3},{4,20},{20... | collective-permute-start | bytes 983048 | tf_op jit(solution)/shard_map/ppermute | solution.py:379
  54.5 3.4 %collective-permute-start.18 = (bf16[128,1280]{1,0:T(8,128)(2,1)S(1)}, bf16[128,1280]{1,0:T(8,128)(2,1)S(1)}, u32[]{:S(2)}, u32[]{:S(2)}) collective-permute-start(bf16[128,1280]{1,0:T(8,128)(2,1)S(1)} %collective-permute-done.14.refs_11_), channel_id=1, source_target_pairs={{0,16},{16,0},{1,17},{17,1},{2,18},{18,2},{3,19},{19,3},{4,20},{20... | collective-permute-start | bytes 983048 | tf_op jit(solution)/shard_map/ppermute | solution.py:379
  54.6 7.0 %collective-permute-start.19 = (bf16[256,256]{1,0:T(8,128)(2,1)S(1)}, bf16[256,256]{1,0:T(8,128)(2,1)S(1)}, u32[]{:S(2)}, u32[]{:S(2)}) collective-permute-start(bf16[256,256]{1,0:T(8,128)(2,1)S(1)} %attend.1.c0), channel_id=1, source_target_pairs={{0,4},{4,8},{8,12},{12,0},{1,5},{5,9},{9,13},{13,1},{2,6},{6,10},{... | collective-permute-start | bytes 393224 | tf_op jit(solution)/shard_map/ppermute | solution.py:377
  54.6 9.1 %collective-permute-start.11 = (bf16[256,256]{1,0:T(8,128)(2,1)S(1)}, bf16[256,256]{1,0:T(8,128)(2,1)S(1)}, u32[]{:S(2)}, u32[]{:S(2)}) collective-permute-start(bf16[256,256]{1,0:T(8,128)(2,1)S(1)} %attend.1.c0), channel_id=1, source_target_pairs={{0,12},{4,0},{8,4},{12,8},{1,13},{5,1},{9,5},{13,9},{2,14},{6,2},{... | collective-permute-start | bytes 393224 | tf_op jit(solution)/shard_map/ppermute | solution.py:377
  57.9 6.7 %collective-permute-start.12 = (bf16[256,256]{1,0:T(8,128)(2,1)S(1)}, bf16[256,256]{1,0:T(8,128)(2,1)S(1)}, u32[]{:S(2)}, u32[]{:S(2)}) collective-permute-start(bf16[256,256]{1,0:T(8,128)(2,1)S(1)} %attend.1.c0), channel_id=1, source_target_pairs={{0,8},{4,12},{8,0},{12,4},{1,9},{5,13},{9,1},{13,5},{2,10},{6,14},... | collective-permute-start | bytes 393224 | tf_op jit(solution)/shard_map/ppermute | solution.py:377
  64.9 6.4 %collective-permute-start.21 = (bf16[640,128]{1,0:T(8,128)(2,1)S(1)}, bf16[640,128]{1,0:T(8,128)(2,1)S(1)}, u32[]{:S(2)}, u32[]{:S(2)}) collective-permute-start(bf16[640,128]{1,0:T(8,128)(2,1)S(1)} %project.5), channel_id=1, source_target_pairs={{0,1},{1,0},{2,3},{3,2},{4,5},{5,4},{6,7},{7,6},{8,9},{9,8},{10,11... | collective-permute-start | bytes 491528 | tf_op jit(solution)/shard_map/ppermute | solution.py:411
  66.0 13.4 %collective-permute-start.20 = (bf16[640,128]{1,0:T(8,128)(2,1)S(1)}, bf16[640,128]{1,0:T(8,128)(2,1)S(1)}, u32[]{:S(2)}, u32[]{:S(2)}) collective-permute-start(bf16[640,128]{1,0:T(8,128)(2,1)S(1)} %project.4), channel_id=1, source_target_pairs={{0,2},{1,3},{2,0},{3,1},{4,6},{5,7},{6,4},{7,5},{8,10},{9,11},{10,... | collective-permute-start | bytes 491528 | tf_op jit(solution)/shard_map/ppermute | solution.py:411
  68.6 13.6 %collective-permute-start.22 = (bf16[640,128]{1,0:T(8,128)(2,1)S(1)}, bf16[640,128]{1,0:T(8,128)(2,1)S(1)}, u32[]{:S(2)}, u32[]{:S(2)}) collective-permute-start(bf16[640,128]{1,0:T(8,128)(2,1)S(1)} %get-tuple-element.50), channel_id=1, source_target_pairs={{0,3},{1,2},{2,1},{3,0},{4,7},{5,6},{6,5},{7,4},{8,11},{9,10},{10,... | collective-permute-start | bytes 491528 | tf_op jit(solution)/shard_map/ppermute | solution.py:411
